TPU v7x, 32 devices: a whole 2x2x4 slice. The times are simulated.
32 devices in a mesh: section: 4 (over y, x), dp: 2 (over core), tp: 4 (over z).
Axes of the slice: x: 2, y: 2, z: 4, core: 2. Of those that a mesh axis runs over, the one named last changes fastest.
Arguments:
- enc_kv: bfloat16 [2, 2, 4, 256, 3072], P('dp', None, 'tp', 'section'), as said below
- queries: bfloat16 [2, 4, 512, 3072], P('dp', 'section', None, 'tp'), as said below
- grad_out: bfloat16 [2, 4, 512, 3072], P('dp', 'section', None, 'tp'), may hold values from -6 to 6
- plan: int32 [2, 4], P('dp'), may hold values from 0 to 3
- enc_lengths: int32 [2, 4], P('dp'), may hold values from 32 to 256
- tgt_lengths: int32 [2, 4], P('dp'), may hold values from 64 to 512
Outputs:
- attended: bfloat16 [2, 4, 512, 3072], P('dp', 'section', None, 'tp')
- grad_queries: bfloat16 [2, 4, 512, 3072], P('dp', 'section', None, 'tp')
- grad_enc_kv: bfloat16 [2, 2, 4, 256, 3072], P('dp', None, 'tp', 'section')
Inputs may be any that keep to these rules, and one draw needn't show every extreme that they name: `enc_kv`: entries lie within -5.5 to 5.5. `queries`: entries lie within -5.5 to 5.5.
All inputs are finite; a program needn't handle non-finite values.
Results may differ from a plain program's by a relative error of at most 0.0084.
Values may be sent and summed in bfloat16 or wider, within the bound.
No kernel may reach another device: no remote copies, remote signals or barrier semaphores. Data moves between devices by JAX's collectives and lax.ppermute only.
A program may use at most 64 MiB of HBM per device.

v0:
```python
import jax
import jax.numpy as jnp
from jax import lax
from jax.sharding import PartitionSpec as P

HEAD_DIM = 128


def head_pass(query_rows, key_rows, value_rows, grad_rows, key_len, query_len):
    scaling = query_rows.shape[-1] ** (-0.5)
    scores = jnp.dot(query_rows, key_rows.T, preferred_element_type=jnp.float32) * scaling
    key_valid = jnp.arange(key_rows.shape[0], dtype=jnp.int32) < key_len
    scores = jnp.where(key_valid[None, :], scores, -jnp.inf)
    row_top = jnp.max(scores, axis=-1, keepdims=True)
    expon = jnp.exp(scores - row_top)
    probs_full = expon / jnp.sum(expon, axis=-1, keepdims=True)
    probs_half = probs_full.astype(jnp.bfloat16)
    query_valid = (jnp.arange(query_rows.shape[0], dtype=jnp.int32) < query_len)[:, None]
    context = jnp.dot(probs_half, value_rows, preferred_element_type=jnp.float32)
    attended = jnp.where(query_valid, context, 0.0).astype(jnp.bfloat16)
    masked_grad = jnp.where(query_valid, grad_rows, jnp.zeros_like(grad_rows))
    grad_value = jnp.dot(probs_half.T, masked_grad, preferred_element_type=jnp.float32).astype(
        jnp.bfloat16
    )
    grad_probs = jnp.dot(masked_grad, value_rows.T, preferred_element_type=jnp.float32)
    row_dot = jnp.sum(probs_full * grad_probs, axis=-1, keepdims=True)
    grad_scores = (probs_full * (grad_probs - row_dot)).astype(jnp.bfloat16)
    grad_query = (
        jnp.dot(grad_scores, key_rows, preferred_element_type=jnp.float32) * scaling
    ).astype(jnp.bfloat16)
    grad_key = (
        jnp.dot(grad_scores.T, query_rows, preferred_element_type=jnp.float32) * scaling
    ).astype(jnp.bfloat16)
    return (attended, grad_query, grad_key, grad_value)


def run_heads(query_three, key_three, value_three, grad_three, key_len, query_len):

    def one_head(pieces):
        return head_pass(pieces[0], pieces[1], pieces[2], pieces[3], key_len, query_len)

    results = lax.map(
        one_head,
        (
            query_three.transpose(1, 0, 2),
            key_three.transpose(1, 0, 2),
            value_three.transpose(1, 0, 2),
            grad_three.transpose(1, 0, 2),
        ),
    )
    return tuple((item.transpose(1, 0, 2) for item in results))


def body(enc_kv, queries, grad_out, plan, enc_lengths, tgt_lengths):
    memory = enc_kv[0]
    section_count = lax.axis_size("section")
    tp_count = lax.axis_size("tp")
    local_micro = memory.shape[1]
    block_len = memory.shape[2]
    columns = memory.shape[3]
    head_cols = columns // tp_count
    heads_local = head_cols // HEAD_DIM
    micro_count = local_micro * tp_count
    tgt_rows = queries.shape[2]
    enc_rows = section_count * block_len
    timetable = plan[0]
    micro_id = timetable[lax.axis_index("section")]
    key_len = enc_lengths[0][micro_id]
    query_len = tgt_lengths[0][micro_id]
    regrouped = lax.all_to_all(
        memory.reshape(2, local_micro, block_len, tp_count, head_cols),
        "tp",
        split_axis=3,
        concat_axis=1,
        tiled=True,
    )
    regrouped = regrouped.reshape(2, micro_count, block_len, head_cols)
    onehot = (timetable[:, None] == jnp.arange(micro_count, dtype=jnp.int32)[None, :]).astype(
        jnp.bfloat16
    )
    picked = jnp.einsum(
        "sm,kmxd->ksxd", onehot, regrouped, preferred_element_type=jnp.float32
    ).astype(jnp.bfloat16)
    query_three = queries[0, 0].reshape(tgt_rows, heads_local, HEAD_DIM)
    grad_three = grad_out[0, 0].reshape(tgt_rows, heads_local, HEAD_DIM)
    arrived = lax.all_to_all(picked, "section", split_axis=1, concat_axis=1, tiled=True)
    key_value = arrived.reshape(2, enc_rows, heads_local, HEAD_DIM)
    attended_three, grad_query_three, grad_key, grad_value = run_heads(
        query_three, key_value[0], key_value[1], grad_three, key_len, query_len
    )
    attended = attended_three.reshape(tgt_rows, head_cols)
    grad_query = grad_query_three.reshape(tgt_rows, head_cols)
    grad_local = jnp.stack([grad_key, grad_value]).reshape(2, section_count, block_len, head_cols)
    returned = lax.all_to_all(grad_local, "section", split_axis=1, concat_axis=1, tiled=True)
    summed = jnp.einsum("sm,ksxd->kmxd", onehot, returned, preferred_element_type=jnp.float32)
    summed_half = summed.astype(jnp.bfloat16)
    spread = lax.all_to_all(
        summed_half.reshape(2, tp_count, local_micro, block_len, head_cols),
        "tp",
        split_axis=1,
        concat_axis=4,
        tiled=True,
    )
    grad_memory = spread.reshape(2, local_micro, block_len, columns)
    return (attended[None, None], grad_query[None, None], grad_memory[None])


def solution(mesh):
    in_specs = (
        P("dp", None, "tp", "section", None),
        P("dp", "section", None, "tp"),
        P("dp", "section", None, "tp"),
        P("dp", None),
        P("dp", None),
        P("dp", None),
    )
    out_specs = (
        P("dp", "section", None, "tp"),
        P("dp", "section", None, "tp"),
        P("dp", None, "tp", "section", None),
    )
    return jax.shard_map(body, mesh=mesh, in_specs=in_specs, out_specs=out_specs, check_vma=False)
```

profile of v0, /device:TPU:0, one launch (start us, length us, event | category | flops | bytes accessed | tf_op | source)
XLA Modules:
  0.0 131.6 jit_solution(1942434235964260268)
XLA Ops:
  0.6 2.0 %reshape_squeeze.10 = bf16[2,1,64,4,768]{4,3,2,0,1:T(4,128)(2,1)S(1)} reshape(bf16[1,2,1,64,3072]{4,3,2,1,0:T(8,128)(2,1)} %param.8) | data formatting | bytes 1572864 | tf_op jit(solution)/shard_map/reshape;squeeze | solution.py:71
  2.7 26.2 %all_to_all.40 = bf16[2,1,64,4,768]{4,2,0,1,3:T(8,128)(2,1)S(1)} all-to-all(bf16[2,1,64,4,768]{4,2,0,1,3:T(8,128)(2,1)S(1)} %copy.50), channel_id=1, replica_groups=mesh['section'=4,'dp'=2,'tp'=4] {'tp'}, dimensions={3} | all-to-all | bytes 1572864 | tf_op jit(solution)/shard_map/all_to_all | solution.py:70
  29.0 0.8 fusion.42
  29.8 1.0 copy.53
  30.8 3.8 %all-to-all-start.1 = ((bf16[2,4,64,768]{3,2,0,1:T(8,128)(2,1)}), bf16[2,4,64,768]{3,2,0,1:T(8,128)(2,1)S(1)}, u32[]{:S(2)}, u32[]{:S(2)}) async-start(bf16[2,4,64,768]{3,2,0,1:T(8,128)(2,1)} %copy.53), calls=%async_computation.1 | async-start | bytes 1572864 | tf_op jit(solution)/shard_map/all_to_all | solution.py:86
  36.8 0.8 copy-done.1
  39.3 5.1 %all-to-all-done.1 = bf16[2,4,64,768]{3,2,0,1:T(8,128)(2,1)S(1)} async-done(((bf16[2,4,64,768]{3,2,0,1:T(8,128)(2,1)}), bf16[2,4,64,768]{3,2,0,1:T(8,128)(2,1)S(1)}, u32[]{:S(2)}, u32[]{:S(2)}) %all-to-all-start.1) | async-done | bytes 786464 | tf_op jit(solution)/shard_map/all_to_all | solution.py:86
  44.9 0.8 copy.57
  46.2 44.0 %while.16 = (s32[]{:T(128)}, bf16[6,512,128]{1,2,0:T(8,128)(2,1)}, bf16[6,512,128]{1,2,0:T(8,128)(2,1)}, bf16[6,256,128]{2,1,0:T(8,128)(2,1)}, bf16[6,256,128]{2...) while((s32[]{:T(128)}, bf16[6,512,128]{1,2,0:T(8,128)(2,1)}, ...), condition=%wide.region_4.5_spmd, body=%wide.region_0.4_spmd.sunk | while | flops 204438784 | bytes 7764893 | solution.py:42
  48.0 1.1 fusion.79
  49.2 1.0 fusion.81
  50.2 1.2 multiply_reduce_fusion.2
  51.9 0.9 fusion.80
  52.8 0.7 constant_dynamic-update-slice_fusion.3
  55.3 1.1 fusion.79
  56.6 1.0 fusion.81
  57.5 1.2 multiply_reduce_fusion.2
  59.3 0.9 fusion.80
  60.1 0.7 constant_dynamic-update-slice_fusion.3
  62.6 1.1 fusion.79
  63.9 1.0 fusion.81
  64.9 1.2 multiply_reduce_fusion.2
  66.6 0.9 fusion.80
  67.5 0.7 constant_dynamic-update-slice_fusion.3
  70.0 1.1 fusion.79
  71.2 1.0 fusion.81
  72.2 1.2 multiply_reduce_fusion.2
  73.9 0.9 fusion.80
  74.8 0.7 constant_dynamic-update-slice_fusion.3
  77.3 1.1 fusion.79
  78.6 1.0 fusion.81
  79.5 1.2 multiply_reduce_fusion.2
  81.3 0.9 fusion.80
  82.1 0.7 constant_dynamic-update-slice_fusion.3
  84.6 1.1 fusion.79
  85.9 1.0 fusion.81
  86.9 1.2 multiply_reduce_fusion.2
  88.6 0.9 fusion.80
  89.5 0.7 constant_dynamic-update-slice_fusion.3
  90.2 1.3 %copy.62 = bf16[256,6,128]{2,1,0:T(8,128)(2,1)S(1)} copy(bf16[256,6,128]{2,0,1:T(8,128)(2,1)} %bitcast.137) | data formatting | bytes 786432 | tf_op jit(solution)/shard_map/transpose | solution.py:51
  92.9 13.2 %all_to_all.41 = bf16[2,4,64,768]{3,2,0,1:T(8,128)(2,1)S(1)} all-to-all(bf16[2,4,64,768]{3,2,0,1:T(8,128)(2,1)S(1)} %copy.63), channel_id=1, replica_groups=mesh['section'=4,'dp'=2,'tp'=4] {'section'}, dimensions={1} | all-to-all | bytes 1572864 | tf_op jit(solution)/shard_map/all_to_all | solution.py:94
  106.1 0.7 fusion.43
  106.8 1.0 copy.65
  107.8 3.6 %all-to-all-start.3 = ((bf16[2,4,1,64,768]{4,3,0,2,1:T(8,128)(2,1)}), bf16[2,4,1,64,768]{4,3,0,2,1:T(8,128)(2,1)S(1)}, u32[]{:S(2)}, u32[]{:S(2)}) async-start(bf16[2,4,1,64,768]{4,3,0,2,1:T(8,128)(2,1)} %copy.65), calls=%async_computation.3 | async-start | bytes 1572864 | tf_op jit(solution)/shard_map/all_to_all | solution.py:97
  111.4 1.2 copy.67
  112.6 1.2 copy.68
  113.7 15.8 %all-to-all-done.3 = bf16[2,4,1,64,768]{4,3,0,2,1:T(8,128)(2,1)S(1)} async-done(((bf16[2,4,1,64,768]{4,3,0,2,1:T(8,128)(2,1)}), bf16[2,4,1,64,768]{4,3,0,2,1:T(8,128)(2,1)S(1)}, u32[]{:S(2)}, u32[]{:S(2)}) %all-to-all-start.3) | async-done | bytes 786464 | tf_op jit(solution)/shard_map/all_to_all | solution.py:97
  130.1 1.5 %broadcast_in_dim_reshape.11 = bf16[1,2,1,64,3072]{4,3,1,2,0:T(8,128)(2,1)} reshape(bf16[2,1,1,64,4,768]{5,4,3,0,2,1:T(4,128)(2,1)S(1)} %copy.66) | data formatting | bytes 1572864 | tf_op jit(solution)/shard_map/broadcast_in_dim;reshape | solution.py:105
  (94 shorter events, 19.3 us)
Async XLA Ops:
  2.7 26.2 %copy-start.5 = (s32[1,4]{1,0:T(1,128)S(1)}, s32[1,4]{1,0:T(1,128)}, u32[]{:S(2)}) copy-start(s32[1,4]{1,0:T(1,128)} %param.11) | copy-start | bytes 52
  30.8 5.8 %copy-start = (bf16[1,1,512,768]{3,2,1,0:T(8,128)(2,1)S(1)}, bf16[1,1,512,768]{3,2,1,0:T(8,128)(2,1)}, u32[]{:S(2)}) copy-start(bf16[1,1,512,768]{3,2,1,0:T(8,128)(2,1)} %param.9) | copy-start | bytes 2359300
  30.8 13.6 %all-to-all-start.1 = ((bf16[2,4,64,768]{3,2,0,1:T(8,128)(2,1)}), bf16[2,4,64,768]{3,2,0,1:T(8,128)(2,1)S(1)}, u32[]{:S(2)}, u32[]{:S(2)}) async-start(bf16[2,4,64,768]{3,2,0,1:T(8,128)(2,1)} %copy.53), calls=%async_computation.1 | async-start | bytes 1572864 | tf_op jit(solution)/shard_map/all_to_all | solution.py:86
  36.5 1.1 copy-start.1
  37.7 0.9 copy-start.6
  37.7 0.9 copy-start.7
  90.2 1.8 %copy-start.4 = (bf16[6,256,128]{2,1,0:T(8,128)(2,1)S(1)}, bf16[6,256,128]{2,1,0:T(8,128)(2,1)}, u32[]{:S(2)}) copy-start(bf16[6,256,128]{2,1,0:T(8,128)(2,1)} %get-tuple-element.65) | copy-start | bytes 1179652
  107.7 3.6 %copy-start.3 = (bf16[6,512,128]{1,2,0:T(8,128)(2,1)S(1)}, bf16[6,512,128]{1,2,0:T(8,128)(2,1)}, u32[]{:S(2)}) copy-start(bf16[6,512,128]{1,2,0:T(8,128)(2,1)} %get-tuple-element.63) | copy-start | bytes 2359300
  107.8 21.7 %all-to-all-start.3 = ((bf16[2,4,1,64,768]{4,3,0,2,1:T(8,128)(2,1)}), bf16[2,4,1,64,768]{4,3,0,2,1:T(8,128)(2,1)S(1)}, u32[]{:S(2)}, u32[]{:S(2)}) async-start(bf16[2,4,1,64,768]{4,3,0,2,1:T(8,128)(2,1)} %copy.65), calls=%async_computation.3 | async-start | bytes 1572864 | tf_op jit(solution)/shard_map/all_to_all | solution.py:97
  111.4 1.2 copy-start.2
where the time goes:
time: 133 us; the launch traced here: 132 us
  blocking collectives  39.4 us (30%)
  matrix products  29.5 us (22%)
  local copies, waits for them, and re-layouts  22 us (17%)
  waiting for transfers between devices  20.9 us (16%)
  other arithmetic  9.18 us (7%)
  starting transfers between devices  7.47 us (6%)
  between operations  2.72 us (2%)
    all_to_all x1, blocking collectives, body(): lax.all_to_all(memory.reshape(2, local_micro, block_len, tp_count, head_c...  26.2 us
    all_to_all x1, waiting for transfers between devices, body(): lax.all_to_all(summed_half.reshape(2, tp_count, local_micro, block_len, h...  15.8 us
    all_to_all x1, blocking collectives, body(): lax.all_to_all(grad_local, 'section', split_axis=1, concat_axis=1, tiled=...  13.2 us
    dot_general x6, matrix products, head_pass(): jnp.dot(masked_grad, value_rows.T, preferred_element_type=jnp.float32)  7.12 us
    dot_general x6, matrix products, head_pass(): jnp.dot(probs_half, value_rows, preferred_element_type=jnp.float32)  6.81 us
    dot_general x6, matrix products, head_pass(): jnp.dot(probs_half.T, masked_grad, preferred_element_type=jnp.float32)  5.85 us
    dynamic_update_slice x18, local copies, waits for them, and re-layouts, run_heads(): lax.map(one_head, (query_three.transpose(1, 0, 2), key_three.transpose(1,...  5.66 us
    dot_general x6, matrix products, head_pass(): jnp.dot(grad_scores.T, query_rows, preferred_element_type=jnp.float32)  5.19 us
  transfers between devices with their start and end apart: 2, of which 2 were waited for; matrix products, arithmetic and copies ran while one was open for 3% of the time, Pallas kernels for 0%

commit v1 on v0

v1 whole, which is shorter than its diff:
```python
import functools
import math

import jax
import jax.numpy as jnp
from jax import lax
from jax.experimental import pallas as pl
from jax.experimental.pallas import tpu as pltpu
from jax.sharding import PartitionSpec as P

HEAD_DIM = 128
CHUNKS = 3

SMEM = pl.BlockSpec(memory_space=pltpu.SMEM)
VMEM = pl.BlockSpec(memory_space=pltpu.VMEM)
ANY = pl.BlockSpec(memory_space=pl.ANY)


def ahead(index, step, count):
    return lax.rem(index + step, count)


def behind(index, step, count):
    return lax.rem(index + count - step, count)


def shift(piece, axis, count, step):
    return lax.ppermute(piece, axis, [(i, (i + step) % count) for i in range(count)])


def near(array):
    return pltpu.with_memory_space_constraint(array, pltpu.VMEM)


def split_kernel(tp_count, chunks, width, head_cols, memory_ref, *outs):
    me = lax.axis_index("tp")
    for chunk in range(chunks):
        for step in range(tp_count):
            start = ahead(me, step, tp_count) * head_cols + chunk * width
            outs[chunk * tp_count + step][...] = memory_ref[:, :, pl.ds(pl.multiple_of(start, 128), width)]


def pick_kernel(tp_count, section_count, plan_ref, *refs):
    pieces, outs = refs[:tp_count], refs[tp_count:]
    me, tp_me = lax.axis_index("section"), lax.axis_index("tp")
    for step in range(section_count):
        micro = plan_ref[0, ahead(me, step, section_count)]
        back = behind(tp_me, micro, tp_count)
        for which in range(tp_count):

            @pl.when(back == which)
            def _():
                outs[step][...] = pieces[which][...]


def heads_kernel(section_count, chunk, width, plan_ref, key_len_ref, query_len_ref, query_ref, grad_ref, *refs):
    blocks = refs[:section_count]
    refs = refs[section_count:]
    if len(refs) > section_count + 2:
        refs = refs[2:]
    attended_ref, grad_query_ref = refs[:2]
    outs = refs[2:]
    me = lax.axis_index("section")
    micro = plan_ref[0, me]
    key_len, query_len = key_len_ref[0, micro], query_len_ref[0, micro]
    block_len = blocks[0].shape[1]
    tgt = query_ref.shape[0]
    scaling = HEAD_DIM ** (-0.5)
    row = lax.broadcasted_iota(jnp.int32, (block_len, tgt), 0)
    query_valid = lax.broadcasted_iota(jnp.int32, (tgt, HEAD_DIM), 0) < query_len
    nt = (((1,), (1,)), ((), ()))
    tn = (((0,), (0,)), ((), ()))
    for head in range(width // HEAD_DIM):
        cols = slice(head * HEAD_DIM, (head + 1) * HEAD_DIM)
        wide = slice(chunk * width + head * HEAD_DIM, chunk * width + (head + 1) * HEAD_DIM)
        query = query_ref[:, wide]
        grad = jnp.where(query_valid, grad_ref[:, wide], jnp.zeros((), jnp.bfloat16))
        keys = jnp.concatenate([block[0, :, cols] for block in blocks], axis=0)
        values = jnp.concatenate([block[1, :, cols] for block in blocks], axis=0)
        scores = lax.dot_general(keys, query, nt, preferred_element_type=jnp.float32) * scaling
        masked = []
        for step in range(section_count):
            left = key_len - behind(me, step, section_count) * block_len
            part = scores[step * block_len : (step + 1) * block_len]
            masked.append(jnp.where(row < left, part, -jnp.inf))
        scores = jnp.concatenate(masked, axis=0)
        top = jnp.max(scores, axis=0, keepdims=True)
        expon = jnp.exp(scores - top)
        probs = expon * (1.0 / jnp.sum(expon, axis=0, keepdims=True))
        half = probs.astype(jnp.bfloat16)
        context = lax.dot_general(half, values, tn, preferred_element_type=jnp.float32)
        attended_ref[:, wide] = jnp.where(query_valid, context, 0.0).astype(jnp.bfloat16)
        grad_value = jnp.dot(half, grad, preferred_element_type=jnp.float32).astype(jnp.bfloat16)
        grad_probs = lax.dot_general(values, grad, nt, preferred_element_type=jnp.float32)
        row_dot = jnp.sum(probs * grad_probs, axis=0, keepdims=True)
        grad_scores = (probs * (grad_probs - row_dot)).astype(jnp.bfloat16)
        grad_query = lax.dot_general(grad_scores, keys, tn, preferred_element_type=jnp.float32)
        grad_query_ref[:, wide] = (grad_query * scaling).astype(jnp.bfloat16)
        grad_key = jnp.dot(grad_scores, query, preferred_element_type=jnp.float32) * scaling
        grad_key = grad_key.astype(jnp.bfloat16)
        for step in range(section_count):
            rows = slice(step * block_len, (step + 1) * block_len)
            outs[step][0, :, cols] = grad_key[rows]
            outs[step][1, :, cols] = grad_value[rows]


def sum_kernel(tp_count, section_count, plan_ref, *refs):
    pieces, outs = refs[:section_count], refs[section_count:]
    me, tp_me = lax.axis_index("section"), lax.axis_index("tp")
    for step in range(tp_count):
        micro = ahead(tp_me, step, tp_count)
        total = jnp.zeros(outs[step].shape, jnp.float32)
        for back in range(section_count):
            weight = jnp.where(plan_ref[0, ahead(me, back, section_count)] == micro, 1.0, 0.0)
            total = total + weight * pieces[back][...].astype(jnp.float32)
        outs[step][...] = total.astype(jnp.bfloat16)


def join_kernel(tp_count, chunks, width, head_cols, *refs):
    pieces, out_ref = refs[:-1], refs[-1]
    me = lax.axis_index("tp")
    for chunk in range(chunks):
        for step in range(tp_count):
            start = behind(me, step, tp_count) * head_cols + chunk * width
            out_ref[:, :, pl.ds(pl.multiple_of(start, 128), width)] = pieces[chunk * tp_count + step][...]


def body(enc_kv, queries, grad_out, plan, enc_lengths, tgt_lengths):
    section_count = lax.axis_size("section")
    tp_count = lax.axis_size("tp")
    memory = enc_kv[0, :, 0]
    query, grad = queries[0, 0], grad_out[0, 0]
    block_len, columns = memory.shape[1:]
    tgt, head_cols = query.shape
    heads = head_cols // HEAD_DIM
    chunks = math.gcd(CHUNKS, heads)
    width = head_cols // chunks
    piece = pltpu.VMEM((2, block_len, width), jnp.bfloat16)
    rows = pltpu.VMEM((tgt, head_cols), jnp.bfloat16)
    params = pltpu.CompilerParams(vmem_limit_bytes=16 * 1024 * 1024)

    split = pl.pallas_call(
        functools.partial(split_kernel, tp_count, chunks, width, head_cols),
        out_shape=[piece] * (tp_count * chunks),
        in_specs=[VMEM],
        out_specs=[VMEM] * (tp_count * chunks),
        compiler_params=params,
        name="split",
    )(memory)

    query, grad = near(query), near(grad)
    arrived = []
    for chunk in range(chunks):
        parts = split[chunk * tp_count : (chunk + 1) * tp_count]
        parts = [parts[0]] + [shift(parts[step], "tp", tp_count, step) for step in range(1, tp_count)]
        picked = pl.pallas_call(
            functools.partial(pick_kernel, tp_count, section_count),
            out_shape=[piece] * section_count,
            in_specs=[SMEM] + [VMEM] * tp_count,
            out_specs=[VMEM] * section_count,
            compiler_params=params,
            name=f"pick{chunk}",
        )(plan, *map(near, parts))
        arrived.append(
            [picked[0]] + [shift(picked[step], "section", section_count, step) for step in range(1, section_count)]
        )

    results = []
    grads = []
    for chunk in range(chunks):
        done = pl.pallas_call(
            functools.partial(heads_kernel, section_count, chunk, width),
            out_shape=[rows, rows] + [piece] * section_count,
            in_specs=[SMEM] * 3 + [VMEM] * (2 + section_count + len(results)),
            out_specs=[VMEM] * (2 + section_count),
            input_output_aliases={5 + section_count + i: i for i in range(len(results))},
            compiler_params=params,
            name=f"heads{chunk}",
        )(plan, enc_lengths, tgt_lengths, query, grad, *map(near, arrived[chunk]), *map(near, results))
        results = list(done[:2])
        grads.append(done[2:])

    joined = []
    for chunk in range(chunks):
        pieces = grads[chunk]
        pieces = [pieces[0]] + [
            shift(pieces[step], "section", section_count, section_count - step) for step in range(1, section_count)
        ]
        summed = pl.pallas_call(
            functools.partial(sum_kernel, tp_count, section_count),
            out_shape=[piece] * tp_count,
            in_specs=[SMEM] + [VMEM] * section_count,
            out_specs=[VMEM] * tp_count,
            compiler_params=params,
            name=f"sum{chunk}",
        )(plan, *map(near, pieces))
        joined += [summed[0]] + [shift(summed[step], "tp", tp_count, step) for step in range(1, tp_count)]
    grad_memory = pl.pallas_call(
        functools.partial(join_kernel, tp_count, chunks, width, head_cols),
        out_shape=jax.ShapeDtypeStruct((2, block_len, columns), jnp.bfloat16),
        in_specs=[VMEM] * len(joined),
        out_specs=VMEM,
        compiler_params=params,
        name="join",
    )(*map(near, joined))
    return (results[0][None, None], results[1][None, None], grad_memory[None, :, None])


def solution(mesh):
    in_specs = (
        P("dp", None, "tp", "section", None),
        P("dp", "section", None, "tp"),
        P("dp", "section", None, "tp"),
        P("dp", None),
        P("dp", None),
        P("dp", None),
    )
    out_specs = (
        P("dp", "section", None, "tp"),
        P("dp", "section", None, "tp"),
        P("dp", None, "tp", "section", None),
    )
    return jax.shard_map(body, mesh=mesh, in_specs=in_specs, out_specs=out_specs, check_vma=False)
```

time: 133 us -> 72.6 us (0.55)
  starting transfers between devices: 7.47 us -> 52.7 us
  blocking collectives: 39.4 us -> 0 us
  matrix products: 29.5 us -> 0 us
  waiting for transfers between devices: 20.9 us -> 1.2 us
  local copies, waits for them, and re-layouts: 22 us -> 4.86 us
  Pallas kernels: 0 us -> 12.9 us
  other arithmetic: 9.18 us -> 0 us
  between operations: 2.72 us -> 0.86 us
    ppermute x0 -> x36, starting transfers between devices: none -> 52.7 us  [shift(): lax.ppermute(piece, axis, [(i, (i + step) % count) for i in range(count)])]
    all_to_all x2 -> x0, blocking collectives: 39.4 us -> none  [the longest x1 26.2 us: body(): lax.all_to_all(memory.reshape(2, local_micro, block_len, tp_count, head_c...]
    dot_general x38 -> x0, matrix products: 29.5 us -> none  [the longest x6 7.12 us: head_pass(): jnp.dot(masked_grad, value_rows.T, preferred_element_type=jnp.float32)]
    all_to_all x2 -> x0, waiting for transfers between devices: 20.9 us -> none  [the longest x1 15.8 us: body(): lax.all_to_all(summed_half.reshape(2, tp_count, local_micro, block_len, h...]
    pallas_call x0 -> x11, Pallas kernels: none -> 12.9 us  [the longest x3 7.51 us: body(): pl.pallas_call(functools.partial(heads_kernel, section_count, chunk, widt...]
    lt x12 -> x0, other arithmetic: 7.59 us -> none  [the longest x6 3.84 us: head_pass(): jnp.arange(query_rows.shape[0], dtype=jnp.int32) < query_len]
    all_to_all x2 -> x0, starting transfers between devices: 7.47 us -> none  [the longest x1 3.85 us: body(): lax.all_to_all(picked, 'section', split_axis=1, concat_axis=1, tiled=True)]
    dynamic_update_slice x18 -> x0, local copies, waits for them, and re-layouts: 5.66 us -> none  [run_heads(): lax.map(one_head, (query_three.transpose(1, 0, 2), key_three.transpose(1,...]
  transfers between devices with their start and end apart: 2 -> 36, of which waited for: 2 -> 2; matrix products, arithmetic and copies ran while one was open for 3% -> 2% of each run, Pallas kernels for 0% -> 13%
where the time goes in v1:
time: 72.6 us; the launch traced here: 72.5 us
  starting transfers between devices  52.7 us (73%)
  Pallas kernels  12.9 us (18%)
  local copies, waits for them, and re-layouts  4.86 us (7%)
  waiting for transfers between devices  1.2 us (2%)
  between operations  0.86 us (1%)
    ppermute x36, starting transfers between devices, shift(): lax.ppermute(piece, axis, [(i, (i + step) % count) for i in range(count)])  52.7 us
    pallas_call x3, Pallas kernels, body(): pl.pallas_call(functools.partial(heads_kernel, section_count, chunk, widt...  7.51 us
    unnamed x16, local copies, waits for them, and re-layouts  4.86 us
    pallas_call x3, Pallas kernels, body(): pl.pallas_call(functools.partial(sum_kernel, tp_count, section_count), ou...  2.27 us
    pallas_call x3, Pallas kernels, body(): pl.pallas_call(functools.partial(pick_kernel, tp_count, section_count), o...  1.99 us
  transfers between devices with their start and end apart: 36, of which 2 were waited for; matrix products, arithmetic and copies ran while one was open for 2% of the time, Pallas kernels for 13%

profile of v1, /device:TPU:0, one launch (start us, length us, event | category | flops | bytes accessed | tf_op | source)
XLA Modules:
  0.0 72.5 jit_solution(10902072218473294612)
XLA Ops:
  0.6 1.1 %copy-done.2 = bf16[1,2,1,64,3072]{4,3,2,1,0:T(8,128)(2,1)S(1)} copy-done((bf16[1,2,1,64,3072]{4,3,2,1,0:T(8,128)(2,1)S(1)}, bf16[1,2,1,64,3072]{4,3,2,1,0:T(8,128)(2,1)}, u32[]{:S(2)}) %copy-start.2) | copy-done | bytes 786456
  1.9 3.1 %collective-permute-start.6 = (bf16[2,64,256]{2,1,0:T(8,128)(2,1)S(1)}, bf16[2,64,256]{2,1,0:T(8,128)(2,1)S(1)}, u32[]{:S(2)}, u32[]{:S(2)}) collective-permute-start(bf16[2,64,256]{2,1,0:T(8,128)(2,1)S(1)} %get-tuple-element.66), channel_id=1, source_target_pairs={{0,1},{1,2},{2,3},{3,0},{4,5},{5,6},{6,7},{7,4},{8,9},{9,10},{10,1... | collective-permute-start | bytes 196616 | tf_op jit(solution)/shard_map/ppermute | solution.py:28
  5.0 2.6 %collective-permute-start.7 = (bf16[2,64,256]{2,1,0:T(8,128)(2,1)S(1)}, bf16[2,64,256]{2,1,0:T(8,128)(2,1)S(1)}, u32[]{:S(2)}, u32[]{:S(2)}) collective-permute-start(bf16[2,64,256]{2,1,0:T(8,128)(2,1)S(1)} %get-tuple-element.67), channel_id=1, source_target_pairs={{0,2},{1,3},{2,0},{3,1},{4,6},{5,7},{6,4},{7,5},{8,10},{9,11},{10,... | collective-permute-start | bytes 196616 | tf_op jit(solution)/shard_map/ppermute | solution.py:28
  7.5 1.3 %collective-permute-start.8 = (bf16[2,64,256]{2,1,0:T(8,128)(2,1)S(1)}, bf16[2,64,256]{2,1,0:T(8,128)(2,1)S(1)}, u32[]{:S(2)}, u32[]{:S(2)}) collective-permute-start(bf16[2,64,256]{2,1,0:T(8,128)(2,1)S(1)} %get-tuple-element.68), channel_id=1, source_target_pairs={{0,3},{1,0},{2,1},{3,2},{4,7},{5,4},{6,5},{7,6},{8,11},{9,8},{10,9... | collective-permute-start | bytes 196616 | tf_op jit(solution)/shard_map/ppermute | solution.py:28
  8.9 0.7 collective-permute-start.12
  9.6 0.3 collective-permute-start.13
  9.9 2.8 %collective-permute-start.14 = (bf16[2,64,256]{2,1,0:T(8,128)(2,1)S(1)}, bf16[2,64,256]{2,1,0:T(8,128)(2,1)S(1)}, u32[]{:S(2)}, u32[]{:S(2)}) collective-permute-start(bf16[2,64,256]{2,1,0:T(8,128)(2,1)S(1)} %get-tuple-element.76), channel_id=1, source_target_pairs={{0,3},{1,0},{2,1},{3,2},{4,7},{5,4},{6,5},{7,6},{8,11},{9,8},{10,9... | collective-permute-start | bytes 196616 | tf_op jit(solution)/shard_map/ppermute | solution.py:28
  12.7 1.0 %collective-permute-start = (bf16[2,64,256]{2,1,0:T(8,128)(2,1)S(1)}, bf16[2,64,256]{2,1,0:T(8,128)(2,1)S(1)}, u32[]{:S(2)}, u32[]{:S(2)}) collective-permute-start(bf16[2,64,256]{2,1,0:T(8,128)(2,1)S(1)} %get-tuple-element.58), channel_id=1, source_target_pairs={{0,1},{1,2},{2,3},{3,0},{4,5},{5,6},{6,7},{7,4},{8,9},{9,10},{10,1... | collective-permute-start | bytes 196616 | tf_op jit(solution)/shard_map/ppermute | solution.py:28
  13.8 3.9 %collective-permute-start.1 = (bf16[2,64,256]{2,1,0:T(8,128)(2,1)S(1)}, bf16[2,64,256]{2,1,0:T(8,128)(2,1)S(1)}, u32[]{:S(2)}, u32[]{:S(2)}) collective-permute-start(bf16[2,64,256]{2,1,0:T(8,128)(2,1)S(1)} %get-tuple-element.59), channel_id=1, source_target_pairs={{0,2},{1,3},{2,0},{3,1},{4,6},{5,7},{6,4},{7,5},{8,10},{9,11},{10,... | collective-permute-start | bytes 196616 | tf_op jit(solution)/shard_map/ppermute | solution.py:28
  17.6 0.7 copy-done.3
  18.3 0.7 pick1.1
  19.0 1.6 %collective-permute-start.2 = (bf16[2,64,256]{2,1,0:T(8,128)(2,1)S(1)}, bf16[2,64,256]{2,1,0:T(8,128)(2,1)S(1)}, u32[]{:S(2)}, u32[]{:S(2)}) collective-permute-start(bf16[2,64,256]{2,1,0:T(8,128)(2,1)S(1)} %get-tuple-element.60), channel_id=1, source_target_pairs={{0,3},{1,0},{2,1},{3,2},{4,7},{5,4},{6,5},{7,6},{8,11},{9,8},{10,9... | collective-permute-start | bytes 196616 | tf_op jit(solution)/shard_map/ppermute | solution.py:28
  20.6 2.5 %collective-permute-start.9 = (bf16[2,64,256]{2,1,0:T(8,128)(2,1)S(1)}, bf16[2,64,256]{2,1,0:T(8,128)(2,1)S(1)}, u32[]{:S(2)}, u32[]{:S(2)}) collective-permute-start(bf16[2,64,256]{2,1,0:T(8,128)(2,1)S(1)} %get-tuple-element.70), channel_id=1, source_target_pairs={{0,8},{8,16},{16,24},{24,0},{1,9},{9,17},{17,25},{25,1},{2,10},{10... | collective-permute-start | bytes 196616 | tf_op jit(solution)/shard_map/ppermute | solution.py:28
  23.0 0.7 pick0.1
  23.7 1.5 %collective-permute-start.15 = (bf16[2,64,256]{2,1,0:T(8,128)(2,1)S(1)}, bf16[2,64,256]{2,1,0:T(8,128)(2,1)S(1)}, u32[]{:S(2)}, u32[]{:S(2)}) collective-permute-start(bf16[2,64,256]{2,1,0:T(8,128)(2,1)S(1)} %get-tuple-element.78), channel_id=1, source_target_pairs={{0,8},{8,16},{16,24},{24,0},{1,9},{9,17},{17,25},{25,1},{2,10},{10... | collective-permute-start | bytes 196616 | tf_op jit(solution)/shard_map/ppermute | solution.py:28
  25.4 2.8 %collective-permute-start.17 = (bf16[2,64,256]{2,1,0:T(8,128)(2,1)S(1)}, bf16[2,64,256]{2,1,0:T(8,128)(2,1)S(1)}, u32[]{:S(2)}, u32[]{:S(2)}) collective-permute-start(bf16[2,64,256]{2,1,0:T(8,128)(2,1)S(1)} %get-tuple-element.80), channel_id=1, source_target_pairs={{0,24},{8,0},{16,8},{24,16},{1,25},{9,1},{17,9},{25,17},{2,26},{10... | collective-permute-start | bytes 196616 | tf_op jit(solution)/shard_map/ppermute | solution.py:28
  28.2 0.5 collective-permute-start.10
  28.7 0.7 pick2.1
  29.6 1.9 %collective-permute-start.3 = (bf16[2,64,256]{2,1,0:T(8,128)(2,1)S(1)}, bf16[2,64,256]{2,1,0:T(8,128)(2,1)S(1)}, u32[]{:S(2)}, u32[]{:S(2)}) collective-permute-start(bf16[2,64,256]{2,1,0:T(8,128)(2,1)S(1)} %get-tuple-element.62), channel_id=1, source_target_pairs={{0,8},{8,16},{16,24},{24,0},{1,9},{9,17},{17,25},{25,1},{2,10},{10... | collective-permute-start | bytes 196616 | tf_op jit(solution)/shard_map/ppermute | solution.py:28
  31.5 1.5 %collective-permute-start.4 = (bf16[2,64,256]{2,1,0:T(8,128)(2,1)S(1)}, bf16[2,64,256]{2,1,0:T(8,128)(2,1)S(1)}, u32[]{:S(2)}, u32[]{:S(2)}) collective-permute-start(bf16[2,64,256]{2,1,0:T(8,128)(2,1)S(1)} %get-tuple-element.63), channel_id=1, source_target_pairs={{0,16},{8,24},{16,0},{24,8},{1,17},{9,25},{17,1},{25,9},{2,18},{10... | collective-permute-start | bytes 196616 | tf_op jit(solution)/shard_map/ppermute | solution.py:28
  33.0 1.4 %collective-permute-start.5 = (bf16[2,64,256]{2,1,0:T(8,128)(2,1)S(1)}, bf16[2,64,256]{2,1,0:T(8,128)(2,1)S(1)}, u32[]{:S(2)}, u32[]{:S(2)}) collective-permute-start(bf16[2,64,256]{2,1,0:T(8,128)(2,1)S(1)} %get-tuple-element.64), channel_id=1, source_target_pairs={{0,24},{8,0},{16,8},{24,16},{1,25},{9,1},{17,9},{25,17},{2,26},{10... | collective-permute-start | bytes 196616 | tf_op jit(solution)/shard_map/ppermute | solution.py:28
  34.5 0.6 copy-done.5
  35.1 2.5 %heads0.1 = (bf16[512,768]{1,0:T(8,128)(2,1)S(1)}, bf16[512,768]{1,0:T(8,128)(2,1)S(1)}, bf16[2,64,256]{2,1,0:T(8,128)(2,1)S(1)}, bf16[2,64,256]{2,1,0:T(8,128)(...) custom-call(s32[1,4]{1,0:T(1,128)S(1)} %copy-done.3, s32[1,4]{1,0:T(1,128)S(1)} %copy-done.5, ...), custom_call_target="tpu_custom_call" | custom-call | tf_op jit(solution)/shard_map/heads0/pallas_call | solution.py:171
  37.6 2.5 %heads1.1 = (bf16[512,768]{1,0:T(8,128)(2,1)S(1)}, bf16[512,768]{1,0:T(8,128)(2,1)S(1)}, bf16[2,64,256]{2,1,0:T(8,128)(2,1)S(1)}, bf16[2,64,256]{2,1,0:T(8,128)(...) custom-call(s32[1,4]{1,0:T(1,128)S(1)} %copy-done.3, ...), custom_call_target="tpu_custom_call", output_to_operand_aliasing={{0}: (9, {}), {1}: (10, {})} | custom-call | tf_op jit(solution)/shard_map/heads1/pallas_call | solution.py:171
  40.2 0.6 copy-done.4
  40.9 2.5 %heads2.1 = (bf16[512,768]{1,0:T(8,128)(2,1)S(1)}, bf16[512,768]{1,0:T(8,128)(2,1)S(1)}, bf16[2,64,256]{2,1,0:T(8,128)(2,1)S(1)}, bf16[2,64,256]{2,1,0:T(8,128)(...) custom-call(s32[1,4]{1,0:T(1,128)S(1)} %copy-done.4, ...), custom_call_target="tpu_custom_call", output_to_operand_aliasing={{0}: (9, {}), {1}: (10, {})} | custom-call | tf_op jit(solution)/shard_map/heads2/pallas_call | solution.py:171
  43.4 0.6 collective-permute-start.30
  43.9 1.5 %collective-permute-start.31 = (bf16[2,64,256]{2,1,0:T(8,128)(2,1)S(1)}, bf16[2,64,256]{2,1,0:T(8,128)(2,1)S(1)}, u32[]{:S(2)}, u32[]{:S(2)}) collective-permute-start(bf16[2,64,256]{2,1,0:T(8,128)(2,1)S(1)} %get-tuple-element.105), channel_id=1, source_target_pairs={{0,16},{8,24},{16,0},{24,8},{1,17},{9,25},{17,1},{25,9},{2,18},{10... | collective-permute-start | bytes 196616 | tf_op jit(solution)/shard_map/ppermute | solution.py:28
  45.5 2.8 %collective-permute-start.24 = (bf16[2,64,256]{2,1,0:T(8,128)(2,1)S(1)}, bf16[2,64,256]{2,1,0:T(8,128)(2,1)S(1)}, u32[]{:S(2)}, u32[]{:S(2)}) collective-permute-start(bf16[2,64,256]{2,1,0:T(8,128)(2,1)S(1)} %get-tuple-element.96), channel_id=1, source_target_pairs={{0,24},{8,0},{16,8},{24,16},{1,25},{9,1},{17,9},{25,17},{2,26},{10... | collective-permute-start | bytes 196616 | tf_op jit(solution)/shard_map/ppermute | solution.py:28
  48.4 0.5 collective-permute-start.25
  48.9 0.6 collective-permute-start.26
  49.5 2.3 %collective-permute-start.18 = (bf16[2,64,256]{2,1,0:T(8,128)(2,1)S(1)}, bf16[2,64,256]{2,1,0:T(8,128)(2,1)S(1)}, u32[]{:S(2)}, u32[]{:S(2)}) collective-permute-start(bf16[2,64,256]{2,1,0:T(8,128)(2,1)S(1)} %get-tuple-element.88), channel_id=1, source_target_pairs={{0,24},{8,0},{16,8},{24,16},{1,25},{9,1},{17,9},{25,17},{2,26},{10... | collective-permute-start | bytes 196616 | tf_op jit(solution)/shard_map/ppermute | solution.py:28
  51.8 1.5 %collective-permute-start.19 = (bf16[2,64,256]{2,1,0:T(8,128)(2,1)S(1)}, bf16[2,64,256]{2,1,0:T(8,128)(2,1)S(1)}, u32[]{:S(2)}, u32[]{:S(2)}) collective-permute-start(bf16[2,64,256]{2,1,0:T(8,128)(2,1)S(1)} %get-tuple-element.89), channel_id=1, source_target_pairs={{0,16},{8,24},{16,0},{24,8},{1,17},{9,25},{17,1},{25,9},{2,18},{10... | collective-permute-start | bytes 196616 | tf_op jit(solution)/shard_map/ppermute | solution.py:28
  53.3 0.8 %sum2.1 = (bf16[2,64,256]{2,1,0:T(8,128)(2,1)S(1)}, bf16[2,64,256]{2,1,0:T(8,128)(2,1)S(1)}, bf16[2,64,256]{2,1,0:T(8,128)(2,1)S(1)}, bf16[2,64,256]{2,1,0:T(8,128)(2,1)S(1)}) custom-call(s32[1,4]{1,0:T(1,128)S(1)} %copy-done.4, bf16[2,64,256]{2,1,0:T(8,128)(2,1)S(1)} %get-tuple-element.103.refs_0_, bf16[2,64,256]{2,1,0:T(8,128)(2,1)S(1)} %collective-permute-done.30.refs_1_, ...), custom_call_target="tpu_custom_call" | custom-call | tf_op jit(solution)/shard_map/sum2/pallas_call | solution.py:189
  54.3 1.4 %collective-permute-start.34 = (bf16[2,64,256]{2,1,0:T(8,128)(2,1)S(1)}, bf16[2,64,256]{2,1,0:T(8,128)(2,1)S(1)}, u32[]{:S(2)}, u32[]{:S(2)}) collective-permute-start(bf16[2,64,256]{2,1,0:T(8,128)(2,1)S(1)} %get-tuple-element.109), channel_id=1, source_target_pairs={{0,2},{1,3},{2,0},{3,1},{4,6},{5,7},{6,4},{7,5},{8,10},{9,11},{10,... | collective-permute-start | bytes 196616 | tf_op jit(solution)/shard_map/ppermute | solution.py:28
  55.6 0.8 %sum1.1 = (bf16[2,64,256]{2,1,0:T(8,128)(2,1)S(1)}, bf16[2,64,256]{2,1,0:T(8,128)(2,1)S(1)}, bf16[2,64,256]{2,1,0:T(8,128)(2,1)S(1)}, bf16[2,64,256]{2,1,0:T(8,128)(2,1)S(1)}) custom-call(s32[1,4]{1,0:T(1,128)S(1)} %copy-done.4, bf16[2,64,256]{2,1,0:T(8,128)(2,1)S(1)} %get-tuple-element.95.refs_0_, bf16[2,64,256]{2,1,0:T(8,128)(2,1)S(1)} %collective-permute-done.24.refs_1_, ...), custom_call_target="tpu_custom_call" | custom-call | tf_op jit(solution)/shard_map/sum1/pallas_call | solution.py:189
  56.4 2.5 %collective-permute-start.35 = (bf16[2,64,256]{2,1,0:T(8,128)(2,1)S(1)}, bf16[2,64,256]{2,1,0:T(8,128)(2,1)S(1)}, u32[]{:S(2)}, u32[]{:S(2)}) collective-permute-start(bf16[2,64,256]{2,1,0:T(8,128)(2,1)S(1)} %get-tuple-element.110), channel_id=1, source_target_pairs={{0,3},{1,0},{2,1},{3,2},{4,7},{5,4},{6,5},{7,6},{8,11},{9,8},{10,9... | collective-permute-start | bytes 196616 | tf_op jit(solution)/shard_map/ppermute | solution.py:28
  58.9 0.6 collective-permute-start.27
  59.5 1.5 %collective-permute-start.28 = (bf16[2,64,256]{2,1,0:T(8,128)(2,1)S(1)}, bf16[2,64,256]{2,1,0:T(8,128)(2,1)S(1)}, u32[]{:S(2)}, u32[]{:S(2)}) collective-permute-start(bf16[2,64,256]{2,1,0:T(8,128)(2,1)S(1)} %get-tuple-element.101), channel_id=1, source_target_pairs={{0,2},{1,3},{2,0},{3,1},{4,6},{5,7},{6,4},{7,5},{8,10},{9,11},{10,... | collective-permute-start | bytes 196616 | tf_op jit(solution)/shard_map/ppermute | solution.py:28
  61.0 0.8 %sum0.1 = (bf16[2,64,256]{2,1,0:T(8,128)(2,1)S(1)}, bf16[2,64,256]{2,1,0:T(8,128)(2,1)S(1)}, bf16[2,64,256]{2,1,0:T(8,128)(2,1)S(1)}, bf16[2,64,256]{2,1,0:T(8,128)(2,1)S(1)}) custom-call(s32[1,4]{1,0:T(1,128)S(1)} %copy-done.4, bf16[2,64,256]{2,1,0:T(8,128)(2,1)S(1)} %get-tuple-element.87.refs_0_, bf16[2,64,256]{2,1,0:T(8,128)(2,1)S(1)} %collective-permute-done.18.refs_1_, ...), custom_call_target="tpu_custom_call" | custom-call | tf_op jit(solution)/shard_map/sum0/pallas_call | solution.py:189
  61.8 2.9 %collective-permute-start.29 = (bf16[2,64,256]{2,1,0:T(8,128)(2,1)S(1)}, bf16[2,64,256]{2,1,0:T(8,128)(2,1)S(1)}, u32[]{:S(2)}, u32[]{:S(2)}) collective-permute-start(bf16[2,64,256]{2,1,0:T(8,128)(2,1)S(1)} %get-tuple-element.102), channel_id=1, source_target_pairs={{0,3},{1,0},{2,1},{3,2},{4,7},{5,4},{6,5},{7,6},{8,11},{9,8},{10,9... | collective-permute-start | bytes 196616 | tf_op jit(solution)/shard_map/ppermute | solution.py:28
  64.7 2.0 %collective-permute-start.22 = (bf16[2,64,256]{2,1,0:T(8,128)(2,1)S(1)}, bf16[2,64,256]{2,1,0:T(8,128)(2,1)S(1)}, u32[]{:S(2)}, u32[]{:S(2)}) collective-permute-start(bf16[2,64,256]{2,1,0:T(8,128)(2,1)S(1)} %get-tuple-element.93), channel_id=1, source_target_pairs={{0,2},{1,3},{2,0},{3,1},{4,6},{5,7},{6,4},{7,5},{8,10},{9,11},{10,... | collective-permute-start | bytes 196616 | tf_op jit(solution)/shard_map/ppermute | solution.py:28
  66.7 1.9 %collective-permute-start.23 = (bf16[2,64,256]{2,1,0:T(8,128)(2,1)S(1)}, bf16[2,64,256]{2,1,0:T(8,128)(2,1)S(1)}, u32[]{:S(2)}, u32[]{:S(2)}) collective-permute-start(bf16[2,64,256]{2,1,0:T(8,128)(2,1)S(1)} %get-tuple-element.94), channel_id=1, source_target_pairs={{0,3},{1,0},{2,1},{3,2},{4,7},{5,4},{6,5},{7,6},{8,11},{9,8},{10,9... | collective-permute-start | bytes 196616 | tf_op jit(solution)/shard_map/ppermute | solution.py:28
  68.6 0.9 %copy.18 = bf16[1,1,512,768]{3,2,1,0:T(8,128)(2,1)} copy(bf16[1,1,512,768]{3,2,1,0:T(8,128)(2,1)S(1)} %bitcast.8) | data formatting | bytes 1572864
  69.5 0.9 %copy.19 = bf16[1,1,512,768]{3,2,1,0:T(8,128)(2,1)} copy(bf16[1,1,512,768]{3,2,1,0:T(8,128)(2,1)S(1)} %bitcast.9) | data formatting | bytes 1572864
  70.4 0.4 collective-permute-done.21.refs_1_
  70.8 0.7 collective-permute-done.23.refs_3_
  71.5 1.0 %join.1 = bf16[2,64,3072]{2,1,0:T(8,128)(2,1)} custom-call(bf16[2,64,256]{2,1,0:T(8,128)(2,1)S(1)} %get-tuple-element.91.refs_0_, bf16[2,64,256]{2,1,0:T(8,128)(2,1)S(1)} %collective-permute-done.21.refs_1_, bf16[2,64,256]{2,1,0:T(8,128)(2,1)S(1)} %collective-permute-done.22.refs_2_, bf16[2,64,256]{2,1,0:T(8,128)(2,1)S(1)} %collective-permute-done.23.refs_3_, ...), custom_call_target="tpu_custom_call" | custom-call | tf_op jit(solution)/shard_map/join/pallas_call | solution.py:198
  (51 shorter events, 0.7 us)
Async XLA Ops:
  0.6 1.1 %copy-start.2 = (bf16[1,2,1,64,3072]{4,3,2,1,0:T(8,128)(2,1)S(1)}, bf16[1,2,1,64,3072]{4,3,2,1,0:T(8,128)(2,1)}, u32[]{:S(2)}) copy-start(bf16[1,2,1,64,3072]{4,3,2,1,0:T(8,128)(2,1)} %param.6) | copy-start | bytes 2359300
  1.8 32.7 %copy-start = (bf16[1,1,512,768]{3,2,1,0:T(8,128)(2,1)S(1)}, bf16[1,1,512,768]{3,2,1,0:T(8,128)(2,1)}, u32[]{:S(2)}) copy-start(bf16[1,1,512,768]{3,2,1,0:T(8,128)(2,1)} %param.7) | copy-start | bytes 2359300
  1.8 32.7 %copy-start.1 = (bf16[1,1,512,768]{3,2,1,0:T(8,128)(2,1)S(1)}, bf16[1,1,512,768]{3,2,1,0:T(8,128)(2,1)}, u32[]{:S(2)}) copy-start(bf16[1,1,512,768]{3,2,1,0:T(8,128)(2,1)} %param.8) | copy-start | bytes 2359300
  1.9 8.0 %collective-permute-start.6 = (bf16[2,64,256]{2,1,0:T(8,128)(2,1)S(1)}, bf16[2,64,256]{2,1,0:T(8,128)(2,1)S(1)}, u32[]{:S(2)}, u32[]{:S(2)}) collective-permute-start(bf16[2,64,256]{2,1,0:T(8,128)(2,1)S(1)} %get-tuple-element.66), channel_id=1, source_target_pairs={{0,1},{1,2},{2,3},{3,0},{4,5},{5,6},{6,7},{7,4},{8,9},{9,10},{10,1... | collective-permute-start | bytes 196616 | tf_op jit(solution)/shard_map/ppermute | solution.py:28
  5.0 7.8 %collective-permute-start.7 = (bf16[2,64,256]{2,1,0:T(8,128)(2,1)S(1)}, bf16[2,64,256]{2,1,0:T(8,128)(2,1)S(1)}, u32[]{:S(2)}, u32[]{:S(2)}) collective-permute-start(bf16[2,64,256]{2,1,0:T(8,128)(2,1)S(1)} %get-tuple-element.67), channel_id=1, source_target_pairs={{0,2},{1,3},{2,0},{3,1},{4,6},{5,7},{6,4},{7,5},{8,10},{9,11},{10,... | collective-permute-start | bytes 196616 | tf_op jit(solution)/shard_map/ppermute | solution.py:28
  7.5 6.2 %collective-permute-start.8 = (bf16[2,64,256]{2,1,0:T(8,128)(2,1)S(1)}, bf16[2,64,256]{2,1,0:T(8,128)(2,1)S(1)}, u32[]{:S(2)}, u32[]{:S(2)}) collective-permute-start(bf16[2,64,256]{2,1,0:T(8,128)(2,1)S(1)} %get-tuple-element.68), channel_id=1, source_target_pairs={{0,3},{1,0},{2,1},{3,2},{4,7},{5,4},{6,5},{7,6},{8,11},{9,8},{10,9... | collective-permute-start | bytes 196616 | tf_op jit(solution)/shard_map/ppermute | solution.py:28
  8.9 10.1 %collective-permute-start.12 = (bf16[2,64,256]{2,1,0:T(8,128)(2,1)S(1)}, bf16[2,64,256]{2,1,0:T(8,128)(2,1)S(1)}, u32[]{:S(2)}, u32[]{:S(2)}) collective-permute-start(bf16[2,64,256]{2,1,0:T(8,128)(2,1)S(1)} %get-tuple-element.74), channel_id=1, source_target_pairs={{0,1},{1,2},{2,3},{3,0},{4,5},{5,6},{6,7},{7,4},{8,9},{9,10},{10,1... | collective-permute-start | bytes 196616 | tf_op jit(solution)/shard_map/ppermute | solution.py:28
  9.6 11.0 %collective-permute-start.13 = (bf16[2,64,256]{2,1,0:T(8,128)(2,1)S(1)}, bf16[2,64,256]{2,1,0:T(8,128)(2,1)S(1)}, u32[]{:S(2)}, u32[]{:S(2)}) collective-permute-start(bf16[2,64,256]{2,1,0:T(8,128)(2,1)S(1)} %get-tuple-element.75), channel_id=1, source_target_pairs={{0,2},{1,3},{2,0},{3,1},{4,6},{5,7},{6,4},{7,5},{8,10},{9,11},{10,... | collective-permute-start | bytes 196616 | tf_op jit(solution)/shard_map/ppermute | solution.py:28
  9.9 13.1 %collective-permute-start.14 = (bf16[2,64,256]{2,1,0:T(8,128)(2,1)S(1)}, bf16[2,64,256]{2,1,0:T(8,128)(2,1)S(1)}, u32[]{:S(2)}, u32[]{:S(2)}) collective-permute-start(bf16[2,64,256]{2,1,0:T(8,128)(2,1)S(1)} %get-tuple-element.76), channel_id=1, source_target_pairs={{0,3},{1,0},{2,1},{3,2},{4,7},{5,4},{6,5},{7,6},{8,11},{9,8},{10,9... | collective-permute-start | bytes 196616 | tf_op jit(solution)/shard_map/ppermute | solution.py:28
  12.7 12.5 %collective-permute-start = (bf16[2,64,256]{2,1,0:T(8,128)(2,1)S(1)}, bf16[2,64,256]{2,1,0:T(8,128)(2,1)S(1)}, u32[]{:S(2)}, u32[]{:S(2)}) collective-permute-start(bf16[2,64,256]{2,1,0:T(8,128)(2,1)S(1)} %get-tuple-element.58), channel_id=1, source_target_pairs={{0,1},{1,2},{2,3},{3,0},{4,5},{5,6},{6,7},{7,4},{8,9},{9,10},{10,1... | collective-permute-start | bytes 196616 | tf_op jit(solution)/shard_map/ppermute | solution.py:28
  13.8 11.6 %collective-permute-start.1 = (bf16[2,64,256]{2,1,0:T(8,128)(2,1)S(1)}, bf16[2,64,256]{2,1,0:T(8,128)(2,1)S(1)}, u32[]{:S(2)}, u32[]{:S(2)}) collective-permute-start(bf16[2,64,256]{2,1,0:T(8,128)(2,1)S(1)} %get-tuple-element.59), channel_id=1, source_target_pairs={{0,2},{1,3},{2,0},{3,1},{4,6},{5,7},{6,4},{7,5},{8,10},{9,11},{10,... | collective-permute-start | bytes 196616 | tf_op jit(solution)/shard_map/ppermute | solution.py:28
  17.6 0.7 copy-start.3
  19.0 9.2 %collective-permute-start.2 = (bf16[2,64,256]{2,1,0:T(8,128)(2,1)S(1)}, bf16[2,64,256]{2,1,0:T(8,128)(2,1)S(1)}, u32[]{:S(2)}, u32[]{:S(2)}) collective-permute-start(bf16[2,64,256]{2,1,0:T(8,128)(2,1)S(1)} %get-tuple-element.60), channel_id=1, source_target_pairs={{0,3},{1,0},{2,1},{3,2},{4,7},{5,4},{6,5},{7,6},{8,11},{9,8},{10,9... | collective-permute-start | bytes 196616 | tf_op jit(solution)/shard_map/ppermute | solution.py:28
  20.6 8.8 %collective-permute-start.9 = (bf16[2,64,256]{2,1,0:T(8,128)(2,1)S(1)}, bf16[2,64,256]{2,1,0:T(8,128)(2,1)S(1)}, u32[]{:S(2)}, u32[]{:S(2)}) collective-permute-start(bf16[2,64,256]{2,1,0:T(8,128)(2,1)S(1)} %get-tuple-element.70), channel_id=1, source_target_pairs={{0,8},{8,16},{16,24},{24,0},{1,9},{9,17},{17,25},{25,1},{2,10},{10... | collective-permute-start | bytes 196616 | tf_op jit(solution)/shard_map/ppermute | solution.py:28
  23.7 5.9 %collective-permute-start.15 = (bf16[2,64,256]{2,1,0:T(8,128)(2,1)S(1)}, bf16[2,64,256]{2,1,0:T(8,128)(2,1)S(1)}, u32[]{:S(2)}, u32[]{:S(2)}) collective-permute-start(bf16[2,64,256]{2,1,0:T(8,128)(2,1)S(1)} %get-tuple-element.78), channel_id=1, source_target_pairs={{0,8},{8,16},{16,24},{24,0},{1,9},{9,17},{17,25},{25,1},{2,10},{10... | collective-permute-start | bytes 196616 | tf_op jit(solution)/shard_map/ppermute | solution.py:28
  25.2 6.2 %collective-permute-start.16 = (bf16[2,64,256]{2,1,0:T(8,128)(2,1)S(1)}, bf16[2,64,256]{2,1,0:T(8,128)(2,1)S(1)}, u32[]{:S(2)}, u32[]{:S(2)}) collective-permute-start(bf16[2,64,256]{2,1,0:T(8,128)(2,1)S(1)} %get-tuple-element.79), channel_id=1, source_target_pairs={{0,16},{8,24},{16,0},{24,8},{1,17},{9,25},{17,1},{25,9},{2,18},{10... | collective-permute-start | bytes 196616 | tf_op jit(solution)/shard_map/ppermute | solution.py:28
  25.4 7.6 %collective-permute-start.17 = (bf16[2,64,256]{2,1,0:T(8,128)(2,1)S(1)}, bf16[2,64,256]{2,1,0:T(8,128)(2,1)S(1)}, u32[]{:S(2)}, u32[]{:S(2)}) collective-permute-start(bf16[2,64,256]{2,1,0:T(8,128)(2,1)S(1)} %get-tuple-element.80), channel_id=1, source_target_pairs={{0,24},{8,0},{16,8},{24,16},{1,25},{9,1},{17,9},{25,17},{2,26},{10... | collective-permute-start | bytes 196616 | tf_op jit(solution)/shard_map/ppermute | solution.py:28
  28.2 9.4 %collective-permute-start.10 = (bf16[2,64,256]{2,1,0:T(8,128)(2,1)S(1)}, bf16[2,64,256]{2,1,0:T(8,128)(2,1)S(1)}, u32[]{:S(2)}, u32[]{:S(2)}) collective-permute-start(bf16[2,64,256]{2,1,0:T(8,128)(2,1)S(1)} %get-tuple-element.71), channel_id=1, source_target_pairs={{0,16},{8,24},{16,0},{24,8},{1,17},{9,25},{17,1},{25,9},{2,18},{10... | collective-permute-start | bytes 196616 | tf_op jit(solution)/shard_map/ppermute | solution.py:28
  29.4 8.2 %collective-permute-start.11 = (bf16[2,64,256]{2,1,0:T(8,128)(2,1)S(1)}, bf16[2,64,256]{2,1,0:T(8,128)(2,1)S(1)}, u32[]{:S(2)}, u32[]{:S(2)}) collective-permute-start(bf16[2,64,256]{2,1,0:T(8,128)(2,1)S(1)} %get-tuple-element.72), channel_id=1, source_target_pairs={{0,24},{8,0},{16,8},{24,16},{1,25},{9,1},{17,9},{25,17},{2,26},{10... | collective-permute-start | bytes 196616 | tf_op jit(solution)/shard_map/ppermute | solution.py:28
  29.6 10.6 %collective-permute-start.3 = (bf16[2,64,256]{2,1,0:T(8,128)(2,1)S(1)}, bf16[2,64,256]{2,1,0:T(8,128)(2,1)S(1)}, u32[]{:S(2)}, u32[]{:S(2)}) collective-permute-start(bf16[2,64,256]{2,1,0:T(8,128)(2,1)S(1)} %get-tuple-element.62), channel_id=1, source_target_pairs={{0,8},{8,16},{16,24},{24,0},{1,9},{9,17},{17,25},{25,1},{2,10},{10... | collective-permute-start | bytes 196616 | tf_op jit(solution)/shard_map/ppermute | solution.py:28
  31.5 8.7 %collective-permute-start.4 = (bf16[2,64,256]{2,1,0:T(8,128)(2,1)S(1)}, bf16[2,64,256]{2,1,0:T(8,128)(2,1)S(1)}, u32[]{:S(2)}, u32[]{:S(2)}) collective-permute-start(bf16[2,64,256]{2,1,0:T(8,128)(2,1)S(1)} %get-tuple-element.63), channel_id=1, source_target_pairs={{0,16},{8,24},{16,0},{24,8},{1,17},{9,25},{17,1},{25,9},{2,18},{10... | collective-permute-start | bytes 196616 | tf_op jit(solution)/shard_map/ppermute | solution.py:28
  33.0 7.2 %collective-permute-start.5 = (bf16[2,64,256]{2,1,0:T(8,128)(2,1)S(1)}, bf16[2,64,256]{2,1,0:T(8,128)(2,1)S(1)}, u32[]{:S(2)}, u32[]{:S(2)}) collective-permute-start(bf16[2,64,256]{2,1,0:T(8,128)(2,1)S(1)} %get-tuple-element.64), channel_id=1, source_target_pairs={{0,24},{8,0},{16,8},{24,16},{1,25},{9,1},{17,9},{25,17},{2,26},{10... | collective-permute-start | bytes 196616 | tf_op jit(solution)/shard_map/ppermute | solution.py:28
  34.4 0.7 copy-start.5
  34.4 0.7 copy-start.6
  40.2 0.7 copy-start.4
  43.4 5.5 %collective-permute-start.30 = (bf16[2,64,256]{2,1,0:T(8,128)(2,1)S(1)}, bf16[2,64,256]{2,1,0:T(8,128)(2,1)S(1)}, u32[]{:S(2)}, u32[]{:S(2)}) collective-permute-start(bf16[2,64,256]{2,1,0:T(8,128)(2,1)S(1)} %get-tuple-element.104), channel_id=1, source_target_pairs={{0,24},{8,0},{16,8},{24,16},{1,25},{9,1},{17,9},{25,17},{2,26},{10... | collective-permute-start | bytes 196616 | tf_op jit(solution)/shard_map/ppermute | solution.py:28
  43.9 5.6 %collective-permute-start.31 = (bf16[2,64,256]{2,1,0:T(8,128)(2,1)S(1)}, bf16[2,64,256]{2,1,0:T(8,128)(2,1)S(1)}, u32[]{:S(2)}, u32[]{:S(2)}) collective-permute-start(bf16[2,64,256]{2,1,0:T(8,128)(2,1)S(1)} %get-tuple-element.105), channel_id=1, source_target_pairs={{0,16},{8,24},{16,0},{24,8},{1,17},{9,25},{17,1},{25,9},{2,18},{10... | collective-permute-start | bytes 196616 | tf_op jit(solution)/shard_map/ppermute | solution.py:28
  45.5 6.4 %collective-permute-start.32 = (bf16[2,64,256]{2,1,0:T(8,128)(2,1)S(1)}, bf16[2,64,256]{2,1,0:T(8,128)(2,1)S(1)}, u32[]{:S(2)}, u32[]{:S(2)}) collective-permute-start(bf16[2,64,256]{2,1,0:T(8,128)(2,1)S(1)} %get-tuple-element.106), channel_id=1, source_target_pairs={{0,8},{8,16},{16,24},{24,0},{1,9},{9,17},{17,25},{25,1},{2,10},{10... | collective-permute-start | bytes 196616 | tf_op jit(solution)/shard_map/ppermute | solution.py:28
  45.5 8.6 %collective-permute-start.24 = (bf16[2,64,256]{2,1,0:T(8,128)(2,1)S(1)}, bf16[2,64,256]{2,1,0:T(8,128)(2,1)S(1)}, u32[]{:S(2)}, u32[]{:S(2)}) collective-permute-start(bf16[2,64,256]{2,1,0:T(8,128)(2,1)S(1)} %get-tuple-element.96), channel_id=1, source_target_pairs={{0,24},{8,0},{16,8},{24,16},{1,25},{9,1},{17,9},{25,17},{2,26},{10... | collective-permute-start | bytes 196616 | tf_op jit(solution)/shard_map/ppermute | solution.py:28
  48.4 5.8 %collective-permute-start.25 = (bf16[2,64,256]{2,1,0:T(8,128)(2,1)S(1)}, bf16[2,64,256]{2,1,0:T(8,128)(2,1)S(1)}, u32[]{:S(2)}, u32[]{:S(2)}) collective-permute-start(bf16[2,64,256]{2,1,0:T(8,128)(2,1)S(1)} %get-tuple-element.97), channel_id=1, source_target_pairs={{0,16},{8,24},{16,0},{24,8},{1,17},{9,25},{17,1},{25,9},{2,18},{10... | collective-permute-start | bytes 196616 | tf_op jit(solution)/shard_map/ppermute | solution.py:28
  48.9 5.4 %collective-permute-start.26 = (bf16[2,64,256]{2,1,0:T(8,128)(2,1)S(1)}, bf16[2,64,256]{2,1,0:T(8,128)(2,1)S(1)}, u32[]{:S(2)}, u32[]{:S(2)}) collective-permute-start(bf16[2,64,256]{2,1,0:T(8,128)(2,1)S(1)} %get-tuple-element.98), channel_id=1, source_target_pairs={{0,8},{8,16},{16,24},{24,0},{1,9},{9,17},{17,25},{25,1},{2,10},{10... | collective-permute-start | bytes 196616 | tf_op jit(solution)/shard_map/ppermute | solution.py:28
  49.5 6.9 %collective-permute-start.18 = (bf16[2,64,256]{2,1,0:T(8,128)(2,1)S(1)}, bf16[2,64,256]{2,1,0:T(8,128)(2,1)S(1)}, u32[]{:S(2)}, u32[]{:S(2)}) collective-permute-start(bf16[2,64,256]{2,1,0:T(8,128)(2,1)S(1)} %get-tuple-element.88), channel_id=1, source_target_pairs={{0,24},{8,0},{16,8},{24,16},{1,25},{9,1},{17,9},{25,17},{2,26},{10... | collective-permute-start | bytes 196616 | tf_op jit(solution)/shard_map/ppermute | solution.py:28
  51.8 7.1 %collective-permute-start.19 = (bf16[2,64,256]{2,1,0:T(8,128)(2,1)S(1)}, bf16[2,64,256]{2,1,0:T(8,128)(2,1)S(1)}, u32[]{:S(2)}, u32[]{:S(2)}) collective-permute-start(bf16[2,64,256]{2,1,0:T(8,128)(2,1)S(1)} %get-tuple-element.89), channel_id=1, source_target_pairs={{0,16},{8,24},{16,0},{24,8},{1,17},{9,25},{17,1},{25,9},{2,18},{10... | collective-permute-start | bytes 196616 | tf_op jit(solution)/shard_map/ppermute | solution.py:28
  54.1 5.4 %collective-permute-start.20 = (bf16[2,64,256]{2,1,0:T(8,128)(2,1)S(1)}, bf16[2,64,256]{2,1,0:T(8,128)(2,1)S(1)}, u32[]{:S(2)}, u32[]{:S(2)}) collective-permute-start(bf16[2,64,256]{2,1,0:T(8,128)(2,1)S(1)} %get-tuple-element.90), channel_id=1, source_target_pairs={{0,8},{8,16},{16,24},{24,0},{1,9},{9,17},{17,25},{25,1},{2,10},{10... | collective-permute-start | bytes 196616 | tf_op jit(solution)/shard_map/ppermute | solution.py:28
  54.2 7.6 %collective-permute-start.33 = (bf16[2,64,256]{2,1,0:T(8,128)(2,1)S(1)}, bf16[2,64,256]{2,1,0:T(8,128)(2,1)S(1)}, u32[]{:S(2)}, u32[]{:S(2)}) collective-permute-start(bf16[2,64,256]{2,1,0:T(8,128)(2,1)S(1)} %get-tuple-element.108), channel_id=1, source_target_pairs={{0,1},{1,2},{2,3},{3,0},{4,5},{5,6},{6,7},{7,4},{8,9},{9,10},{10,1... | collective-permute-start | bytes 196616 | tf_op jit(solution)/shard_map/ppermute | solution.py:28
  54.3 10.4 %collective-permute-start.34 = (bf16[2,64,256]{2,1,0:T(8,128)(2,1)S(1)}, bf16[2,64,256]{2,1,0:T(8,128)(2,1)S(1)}, u32[]{:S(2)}, u32[]{:S(2)}) collective-permute-start(bf16[2,64,256]{2,1,0:T(8,128)(2,1)S(1)} %get-tuple-element.109), channel_id=1, source_target_pairs={{0,2},{1,3},{2,0},{3,1},{4,6},{5,7},{6,4},{7,5},{8,10},{9,11},{10,... | collective-permute-start | bytes 196616 | tf_op jit(solution)/shard_map/ppermute | solution.py:28
  56.4 8.3 %collective-permute-start.35 = (bf16[2,64,256]{2,1,0:T(8,128)(2,1)S(1)}, bf16[2,64,256]{2,1,0:T(8,128)(2,1)S(1)}, u32[]{:S(2)}, u32[]{:S(2)}) collective-permute-start(bf16[2,64,256]{2,1,0:T(8,128)(2,1)S(1)} %get-tuple-element.110), channel_id=1, source_target_pairs={{0,3},{1,0},{2,1},{3,2},{4,7},{5,4},{6,5},{7,6},{8,11},{9,8},{10,9... | collective-permute-start | bytes 196616 | tf_op jit(solution)/shard_map/ppermute | solution.py:28
  58.9 7.8 %collective-permute-start.27 = (bf16[2,64,256]{2,1,0:T(8,128)(2,1)S(1)}, bf16[2,64,256]{2,1,0:T(8,128)(2,1)S(1)}, u32[]{:S(2)}, u32[]{:S(2)}) collective-permute-start(bf16[2,64,256]{2,1,0:T(8,128)(2,1)S(1)} %get-tuple-element.100), channel_id=1, source_target_pairs={{0,1},{1,2},{2,3},{3,0},{4,5},{5,6},{6,7},{7,4},{8,9},{9,10},{10,1... | collective-permute-start | bytes 196616 | tf_op jit(solution)/shard_map/ppermute | solution.py:28
  59.5 10.8 %collective-permute-start.28 = (bf16[2,64,256]{2,1,0:T(8,128)(2,1)S(1)}, bf16[2,64,256]{2,1,0:T(8,128)(2,1)S(1)}, u32[]{:S(2)}, u32[]{:S(2)}) collective-permute-start(bf16[2,64,256]{2,1,0:T(8,128)(2,1)S(1)} %get-tuple-element.101), channel_id=1, source_target_pairs={{0,2},{1,3},{2,0},{3,1},{4,6},{5,7},{6,4},{7,5},{8,10},{9,11},{10,... | collective-permute-start | bytes 196616 | tf_op jit(solution)/shard_map/ppermute | solution.py:28
  61.8 8.6 %collective-permute-start.29 = (bf16[2,64,256]{2,1,0:T(8,128)(2,1)S(1)}, bf16[2,64,256]{2,1,0:T(8,128)(2,1)S(1)}, u32[]{:S(2)}, u32[]{:S(2)}) collective-permute-start(bf16[2,64,256]{2,1,0:T(8,128)(2,1)S(1)} %get-tuple-element.102), channel_id=1, source_target_pairs={{0,3},{1,0},{2,1},{3,2},{4,7},{5,4},{6,5},{7,6},{8,11},{9,8},{10,9... | collective-permute-start | bytes 196616 | tf_op jit(solution)/shard_map/ppermute | solution.py:28
  64.7 6.1 %collective-permute-start.21 = (bf16[2,64,256]{2,1,0:T(8,128)(2,1)S(1)}, bf16[2,64,256]{2,1,0:T(8,128)(2,1)S(1)}, u32[]{:S(2)}, u32[]{:S(2)}) collective-permute-start(bf16[2,64,256]{2,1,0:T(8,128)(2,1)S(1)} %get-tuple-element.92), channel_id=1, source_target_pairs={{0,1},{1,2},{2,3},{3,0},{4,5},{5,6},{6,7},{7,4},{8,9},{9,10},{10,1... | collective-permute-start | bytes 196616 | tf_op jit(solution)/shard_map/ppermute | solution.py:28
  64.7 6.1 %collective-permute-start.22 = (bf16[2,64,256]{2,1,0:T(8,128)(2,1)S(1)}, bf16[2,64,256]{2,1,0:T(8,128)(2,1)S(1)}, u32[]{:S(2)}, u32[]{:S(2)}) collective-permute-start(bf16[2,64,256]{2,1,0:T(8,128)(2,1)S(1)} %get-tuple-element.93), channel_id=1, source_target_pairs={{0,2},{1,3},{2,0},{3,1},{4,6},{5,7},{6,4},{7,5},{8,10},{9,11},{10,... | collective-permute-start | bytes 196616 | tf_op jit(solution)/shard_map/ppermute | solution.py:28
  66.7 4.7 %collective-permute-start.23 = (bf16[2,64,256]{2,1,0:T(8,128)(2,1)S(1)}, bf16[2,64,256]{2,1,0:T(8,128)(2,1)S(1)}, u32[]{:S(2)}, u32[]{:S(2)}) collective-permute-start(bf16[2,64,256]{2,1,0:T(8,128)(2,1)S(1)} %get-tuple-element.94), channel_id=1, source_target_pairs={{0,3},{1,0},{2,1},{3,2},{4,7},{5,4},{6,5},{7,6},{8,11},{9,8},{10,9... | collective-permute-start | bytes 196616 | tf_op jit(solution)/shard_map/ppermute | solution.py:28

commit v2 on v1

v2 whole, which is shorter than its diff:
```python
import functools
import math

import jax
import jax.numpy as jnp
from jax import lax
from jax.experimental import pallas as pl
from jax.experimental.pallas import tpu as pltpu
from jax.sharding import PartitionSpec as P

HEAD_DIM = 128
CHUNKS = 2

SMEM = pl.BlockSpec(memory_space=pltpu.SMEM)
VMEM = pl.BlockSpec(memory_space=pltpu.VMEM)
ANY = pl.BlockSpec(memory_space=pl.ANY)


def ahead(index, step, count):
    return lax.rem(index + step, count)


def behind(index, step, count):
    return lax.rem(index + count - step, count)


def shift(piece, axis, count, step):
    return lax.ppermute(piece, axis, [(i, (i + step) % count) for i in range(count)])


def near(array):
    return pltpu.with_memory_space_constraint(array, pltpu.VMEM)


def split_kernel(tp_count, chunks, width, head_cols, plan_ref, key_len_ref, query_len_ref, memory_ref, facts_ref, *outs):
    me = lax.axis_index("tp")
    section_count = plan_ref.shape[1]
    for section in range(section_count):
        facts_ref[section] = plan_ref[0, section]
    micro = plan_ref[0, lax.axis_index("section")]
    facts_ref[section_count] = key_len_ref[0, micro]
    facts_ref[section_count + 1] = query_len_ref[0, micro]
    for chunk in range(chunks):
        for step in range(tp_count):
            start = ahead(me, step, tp_count) * head_cols + chunk * width
            outs[chunk * tp_count + step][...] = memory_ref[:, :, pl.ds(pl.multiple_of(start, 128), width)]


def pick_kernel(tp_count, section_count, facts_ref, *refs):
    pieces, outs = refs[:tp_count], refs[tp_count:]
    me, tp_me = lax.axis_index("section"), lax.axis_index("tp")
    for step in range(section_count):
        micro = facts_ref[ahead(me, step, section_count)]
        back = behind(tp_me, micro, tp_count)
        for which in range(tp_count):

            @pl.when(back == which)
            def _():
                outs[step][...] = pieces[which][...]


def heads_kernel(section_count, chunk, width, facts_ref, query_ref, grad_ref, *refs):
    blocks = refs[:section_count]
    attended_ref, grad_query_ref, *outs = refs[-2 - section_count :]
    me = lax.axis_index("section")
    key_len, query_len = facts_ref[section_count], facts_ref[section_count + 1]
    block_len = blocks[0].shape[1]
    tgt = query_ref.shape[0]
    scaling = HEAD_DIM ** (-0.5)
    scaling_two = scaling * math.log2(math.e)
    row = lax.broadcasted_iota(jnp.int32, (block_len, 1), 0)
    lefts = [key_len - behind(me, step, section_count) * block_len for step in range(section_count)]
    bias = jnp.concatenate([jnp.where(row < left, 0.0, -jnp.inf) for left in lefts], axis=0)
    query_valid = lax.broadcasted_iota(jnp.int32, (tgt, HEAD_DIM), 0) < query_len
    nt = (((1,), (1,)), ((), ()))
    tn = (((0,), (0,)), ((), ()))
    none = jnp.zeros((), jnp.bfloat16)
    for head in range(width // HEAD_DIM):
        cols = slice(head * HEAD_DIM, (head + 1) * HEAD_DIM)
        wide = slice(chunk * width + head * HEAD_DIM, chunk * width + (head + 1) * HEAD_DIM)
        query = query_ref[:, wide]
        grad = jnp.where(query_valid, grad_ref[:, wide], none)
        keys = jnp.concatenate([block[0, :, cols] for block in blocks], axis=0)
        values = jnp.concatenate([block[1, :, cols] for block in blocks], axis=0)
        scores = lax.dot_general(keys, query, nt, preferred_element_type=jnp.float32) + bias
        top = jnp.max(scores, axis=0, keepdims=True)
        expon = jnp.exp2((scores - top) * scaling_two)
        probs = expon * (1.0 / jnp.sum(expon, axis=0, keepdims=True))
        half = probs.astype(jnp.bfloat16)
        grad_probs = lax.dot_general(values, grad, nt, preferred_element_type=jnp.float32)
        row_dot = jnp.sum(probs * grad_probs, axis=0, keepdims=True)
        grad_scores = (probs * (grad_probs - row_dot)).astype(jnp.bfloat16)
        grad_value = jnp.dot(half, grad, preferred_element_type=jnp.float32).astype(jnp.bfloat16)
        grad_key = jnp.dot(grad_scores, query, preferred_element_type=jnp.float32) * scaling
        grad_key = grad_key.astype(jnp.bfloat16)
        context = lax.dot_general(values, half, tn, preferred_element_type=jnp.float32).astype(jnp.bfloat16).T
        attended_ref[:, wide] = jnp.where(query_valid, context, none)
        grad_query = lax.dot_general(keys, grad_scores, tn, preferred_element_type=jnp.float32) * scaling
        grad_query_ref[:, wide] = grad_query.astype(jnp.bfloat16).T
        for step in range(section_count):
            rows = slice(step * block_len, (step + 1) * block_len)
            outs[step][0, :, cols] = grad_key[rows]
            outs[step][1, :, cols] = grad_value[rows]


def sum_kernel(tp_count, section_count, facts_ref, *refs):
    pieces, outs = refs[:section_count], refs[section_count:]
    me, tp_me = lax.axis_index("section"), lax.axis_index("tp")
    for step in range(tp_count):
        micro = ahead(tp_me, step, tp_count)
        total = jnp.zeros(outs[step].shape, jnp.float32)
        for back in range(section_count):
            weight = jnp.where(facts_ref[ahead(me, back, section_count)] == micro, 1.0, 0.0)
            total = total + weight * pieces[back][...].astype(jnp.float32)
        outs[step][...] = total.astype(jnp.bfloat16)


def join_kernel(tp_count, chunks, width, head_cols, *refs):
    pieces, out_ref = refs[:-1], refs[-1]
    me = lax.axis_index("tp")
    for chunk in range(chunks):
        for step in range(tp_count):
            start = behind(me, step, tp_count) * head_cols + chunk * width
            out_ref[:, :, pl.ds(pl.multiple_of(start, 128), width)] = pieces[chunk * tp_count + step][...]


def body(enc_kv, queries, grad_out, plan, enc_lengths, tgt_lengths):
    section_count = lax.axis_size("section")
    tp_count = lax.axis_size("tp")
    memory = enc_kv[0, :, 0]
    query, grad = queries[0, 0], grad_out[0, 0]
    block_len, columns = memory.shape[1:]
    tgt, head_cols = query.shape
    heads = head_cols // HEAD_DIM
    chunks = math.gcd(CHUNKS, heads)
    width = head_cols // chunks
    piece = pltpu.VMEM((2, block_len, width), jnp.bfloat16)
    rows = pltpu.VMEM((tgt, head_cols), jnp.bfloat16)
    params = pltpu.CompilerParams(vmem_limit_bytes=16 * 1024 * 1024)

    facts, *split = pl.pallas_call(
        functools.partial(split_kernel, tp_count, chunks, width, head_cols),
        out_shape=[pltpu.SMEM((section_count + 2,), jnp.int32)] + [piece] * (tp_count * chunks),
        in_specs=[SMEM] * 3 + [VMEM],
        out_specs=[SMEM] + [VMEM] * (tp_count * chunks),
        compiler_params=params,
        name="split",
    )(plan, enc_lengths, tgt_lengths, memory)
    facts = pltpu.with_memory_space_constraint(facts, pltpu.SMEM)

    query, grad = near(query), near(grad)
    arrived = []
    for chunk in range(chunks):
        parts = split[chunk * tp_count : (chunk + 1) * tp_count]
        parts = [parts[0]] + [shift(parts[step], "tp", tp_count, step) for step in range(1, tp_count)]
        picked = pl.pallas_call(
            functools.partial(pick_kernel, tp_count, section_count),
            out_shape=[piece] * section_count,
            in_specs=[SMEM] + [VMEM] * tp_count,
            out_specs=[VMEM] * section_count,
            compiler_params=params,
            name=f"pick{chunk}",
        )(facts, *map(near, parts))
        arrived.append(
            [picked[0]] + [shift(picked[step], "section", section_count, step) for step in range(1, section_count)]
        )

    results, returned, gate = [], [], []
    for chunk in range(chunks):
        done = pl.pallas_call(
            functools.partial(heads_kernel, section_count, chunk, width),
            out_shape=[rows, rows] + [piece] * section_count,
            in_specs=[SMEM] + [VMEM] * (2 + section_count + len(results) + len(gate)),
            out_specs=[VMEM] * (2 + section_count),
            input_output_aliases={3 + section_count + i: i for i in range(len(results))},
            compiler_params=params,
            cost_estimate=pl.CostEstimate(
                flops=12 * tgt * block_len * section_count * width, bytes_accessed=12 * 1024 * 1024 // chunks * 2, transcendentals=0
            ),
            name=f"heads{chunk}",
        )(facts, query, grad, *map(near, arrived[chunk]), *map(near, results), *map(near, gate))
        results = list(done[:2])
        returned.append(
            [done[2]]
            + [shift(done[2 + step], "section", section_count, section_count - step) for step in range(1, section_count)]
        )
        gate = returned[chunk][1:2]

    joined = []
    for chunk in range(chunks):
        pieces = returned[chunk]
        summed = pl.pallas_call(
            functools.partial(sum_kernel, tp_count, section_count),
            out_shape=[piece] * tp_count,
            in_specs=[SMEM] + [VMEM] * section_count,
            out_specs=[VMEM] * tp_count,
            compiler_params=params,
            name=f"sum{chunk}",
        )(facts, *map(near, pieces))
        joined += [summed[0]] + [shift(summed[step], "tp", tp_count, step) for step in range(1, tp_count)]
    grad_memory = pl.pallas_call(
        functools.partial(join_kernel, tp_count, chunks, width, head_cols),
        out_shape=jax.ShapeDtypeStruct((2, block_len, columns), jnp.bfloat16),
        in_specs=[VMEM] * len(joined),
        out_specs=VMEM,
        compiler_params=params,
        name="join",
    )(*map(near, joined))
    return (results[0][None, None], results[1][None, None], grad_memory[None, :, None])


def solution(mesh):
    in_specs = (
        P("dp", None, "tp", "section", None),
        P("dp", "section", None, "tp"),
        P("dp", "section", None, "tp"),
        P("dp", None),
        P("dp", None),
        P("dp", None),
    )
    out_specs = (
        P("dp", "section", None, "tp"),
        P("dp", "section", None, "tp"),
        P("dp", None, "tp", "section", None),
    )
    return jax.shard_map(body, mesh=mesh, in_specs=in_specs, out_specs=out_specs, check_vma=False)
```

time: 72.6 us -> 60.3 us (0.83)
  starting transfers between devices: 52.7 us -> 37.8 us
  waiting for transfers between devices: 1.2 us -> 11.5 us
  Pallas kernels: 12.9 us -> 6.49 us
  local copies, waits for them, and re-layouts: 4.86 us -> 3.56 us
    ppermute x36 -> x24, starting transfers between devices: 52.7 us -> 37.8 us  [shift(): lax.ppermute(piece, axis, [(i, (i + step) % count) for i in range(count)])]
    ppermute x36 -> x24, waiting for transfers between devices: 1.2 us -> 11.5 us  [shift(): lax.ppermute(piece, axis, [(i, (i + step) % count) for i in range(count)])]
    pallas_call x3 -> x2, Pallas kernels: 7.51 us -> 4.03 us  [body(): pl.pallas_call(functools.partial(heads_kernel, section_count, chunk, widt...]
    pallas_call x3 -> x2, Pallas kernels: 1.99 us -> 0.22 us  [body(): pl.pallas_call(functools.partial(pick_kernel, tp_count, section_count), o...]
    pallas_call x3 -> x2, Pallas kernels: 2.27 us -> 0.64 us  [body(): pl.pallas_call(functools.partial(sum_kernel, tp_count, section_count), ou...]
    unnamed x16 -> x14, local copies, waits for them, and re-layouts: 4.86 us -> 3.56 us
  transfers between devices with their start and end apart: 36 -> 24, of which waited for: 2 -> 5; matrix products, arithmetic and copies ran while one was open for 2% -> 3% of each run, Pallas kernels for 13% -> 8%
where the time goes in v2:
time: 60.3 us; the launch traced here: 60.1 us
  starting transfers between devices  37.8 us (63%)
  waiting for transfers between devices  11.5 us (19%)
  Pallas kernels  6.49 us (11%)
  local copies, waits for them, and re-layouts  3.56 us (6%)
  between operations  0.75 us (1%)
    ppermute x24, starting transfers between devices, shift(): lax.ppermute(piece, axis, [(i, (i + step) % count) for i in range(count)])  37.8 us
    ppermute x24, waiting for transfers between devices, shift(): lax.ppermute(piece, axis, [(i, (i + step) % count) for i in range(count)])  11.5 us
    pallas_call x2, Pallas kernels, body(): pl.pallas_call(functools.partial(heads_kernel, section_count, chunk, widt...  4.03 us
    unnamed x14, local copies, waits for them, and re-layouts  3.56 us
  transfers between devices with their start and end apart: 24, of which 5 were waited for; matrix products, arithmetic and copies ran while one was open for 3% of the time, Pallas kernels for 8%

profile of v2, /device:TPU:0, one launch (start us, length us, event | category | flops | bytes accessed | tf_op | source)
XLA Modules:
  0.0 60.1 jit_solution(14240623239630825045)
XLA Ops:
  0.7 0.6 %copy-done.5 = s32[1,4]{1,0:T(1,128)S(1)} copy-done((s32[1,4]{1,0:T(1,128)S(1)}, s32[1,4]{1,0:T(1,128)}, u32[]{:S(2)}) %copy-start.5) | copy-done | bytes 40
  1.3 0.0 copy-done.4
  1.3 0.0 copy-done.3
  1.3 1.1 %copy-done = bf16[1,2,1,64,3072]{4,3,2,1,0:T(8,128)(2,1)S(1)} copy-done((bf16[1,2,1,64,3072]{4,3,2,1,0:T(8,128)(2,1)S(1)}, bf16[1,2,1,64,3072]{4,3,2,1,0:T(8,128)(2,1)}, u32[]{:S(2)}) %copy-start) | copy-done | bytes 786456
  2.5 0.6 %split.1 = (s32[6]{0:T(128)S(4)}, bf16[2,64,384]{2,1,0:T(8,128)(2,1)S(1)}, bf16[2,64,384]{2,1,0:T(8,128)(2,1)S(1)}, bf16[2,64,384]{2,1,0:T(8,128)(2,1)S(1)}, bf1...) custom-call(s32[1,4]{1,0:T(1,128)S(1)} %copy-done.3, ...), custom_call_target="tpu_custom_call" | custom-call | tf_op jit(solution)/shard_map/split/pallas_call | solution.py:141
  3.1 3.1 %collective-permute-start.6 = (bf16[2,64,384]{2,1,0:T(8,128)(2,1)S(1)}, bf16[2,64,384]{2,1,0:T(8,128)(2,1)S(1)}, u32[]{:S(2)}, u32[]{:S(2)}) collective-permute-start(bf16[2,64,384]{2,1,0:T(8,128)(2,1)S(1)} %get-tuple-element.50), channel_id=1, source_target_pairs={{0,1},{1,2},{2,3},{3,0},{4,5},{5,6},{6,7},{7,4},{8,9},{9,10},{10,1... | collective-permute-start | bytes 294920 | tf_op jit(solution)/shard_map/ppermute | solution.py:28
  6.2 2.6 %collective-permute-start.7 = (bf16[2,64,384]{2,1,0:T(8,128)(2,1)S(1)}, bf16[2,64,384]{2,1,0:T(8,128)(2,1)S(1)}, u32[]{:S(2)}, u32[]{:S(2)}) collective-permute-start(bf16[2,64,384]{2,1,0:T(8,128)(2,1)S(1)} %get-tuple-element.51), channel_id=1, source_target_pairs={{0,2},{1,3},{2,0},{3,1},{4,6},{5,7},{6,4},{7,5},{8,10},{9,11},{10,... | collective-permute-start | bytes 294920 | tf_op jit(solution)/shard_map/ppermute | solution.py:28
  8.8 1.3 %collective-permute-start.8 = (bf16[2,64,384]{2,1,0:T(8,128)(2,1)S(1)}, bf16[2,64,384]{2,1,0:T(8,128)(2,1)S(1)}, u32[]{:S(2)}, u32[]{:S(2)}) collective-permute-start(bf16[2,64,384]{2,1,0:T(8,128)(2,1)S(1)} %get-tuple-element.52), channel_id=1, source_target_pairs={{0,3},{1,0},{2,1},{3,2},{4,7},{5,4},{6,5},{7,6},{8,11},{9,8},{10,9... | collective-permute-start | bytes 294920 | tf_op jit(solution)/shard_map/ppermute | solution.py:28
  10.1 0.7 %collective-permute-start = (bf16[2,64,384]{2,1,0:T(8,128)(2,1)S(1)}, bf16[2,64,384]{2,1,0:T(8,128)(2,1)S(1)}, u32[]{:S(2)}, u32[]{:S(2)}) collective-permute-start(bf16[2,64,384]{2,1,0:T(8,128)(2,1)S(1)} %get-tuple-element.42), channel_id=1, source_target_pairs={{0,1},{1,2},{2,3},{3,0},{4,5},{5,6},{6,7},{7,4},{8,9},{9,10},{10,1... | collective-permute-start | bytes 294920 | tf_op jit(solution)/shard_map/ppermute | solution.py:28
  10.8 0.3 collective-permute-start.1
  11.1 0.7 %collective-permute-done.6.refs_1_ = bf16[2,64,384]{2,1,0:T(8,128)(2,1)S(1)} collective-permute-done((bf16[2,64,384]{2,1,0:T(8,128)(2,1)S(1)}, bf16[2,64,384]{2,1,0:T(8,128)(2,1)S(1)}, u32[]{:S(2)}, u32[]{:S(2)}) %collective-permute-start.6) | collective-permute-done | bytes 98336 | tf_op jit(solution)/shard_map/ppermute | solution.py:28
  11.9 3.1 %collective-permute-start.2 = (bf16[2,64,384]{2,1,0:T(8,128)(2,1)S(1)}, bf16[2,64,384]{2,1,0:T(8,128)(2,1)S(1)}, u32[]{:S(2)}, u32[]{:S(2)}) collective-permute-start(bf16[2,64,384]{2,1,0:T(8,128)(2,1)S(1)} %get-tuple-element.44), channel_id=1, source_target_pairs={{0,3},{1,0},{2,1},{3,2},{4,7},{5,4},{6,5},{7,6},{8,11},{9,8},{10,9... | collective-permute-start | bytes 294920 | tf_op jit(solution)/shard_map/ppermute | solution.py:28
  15.0 3.9 %collective-permute-done.7.refs_2_ = bf16[2,64,384]{2,1,0:T(8,128)(2,1)S(1)} collective-permute-done((bf16[2,64,384]{2,1,0:T(8,128)(2,1)S(1)}, bf16[2,64,384]{2,1,0:T(8,128)(2,1)S(1)}, u32[]{:S(2)}, u32[]{:S(2)}) %collective-permute-start.7) | collective-permute-done | bytes 98336 | tf_op jit(solution)/shard_map/ppermute | solution.py:28
  18.9 0.1 pick0.1
  19.0 1.5 %collective-permute-start.9 = (bf16[2,64,384]{2,1,0:T(8,128)(2,1)S(1)}, bf16[2,64,384]{2,1,0:T(8,128)(2,1)S(1)}, u32[]{:S(2)}, u32[]{:S(2)}) collective-permute-start(bf16[2,64,384]{2,1,0:T(8,128)(2,1)S(1)} %get-tuple-element.54), channel_id=1, source_target_pairs={{0,8},{8,16},{16,24},{24,0},{1,9},{9,17},{17,25},{25,1},{2,10},{10... | collective-permute-start | bytes 294920 | tf_op jit(solution)/shard_map/ppermute | solution.py:28
  20.5 1.5 %collective-permute-start.10 = (bf16[2,64,384]{2,1,0:T(8,128)(2,1)S(1)}, bf16[2,64,384]{2,1,0:T(8,128)(2,1)S(1)}, u32[]{:S(2)}, u32[]{:S(2)}) collective-permute-start(bf16[2,64,384]{2,1,0:T(8,128)(2,1)S(1)} %get-tuple-element.55), channel_id=1, source_target_pairs={{0,16},{8,24},{16,0},{24,8},{1,17},{9,25},{17,1},{25,9},{2,18},{10... | collective-permute-start | bytes 294920 | tf_op jit(solution)/shard_map/ppermute | solution.py:28
  22.1 0.0 collective-permute-done.refs_1_
  22.1 1.4 %collective-permute-start.11 = (bf16[2,64,384]{2,1,0:T(8,128)(2,1)S(1)}, bf16[2,64,384]{2,1,0:T(8,128)(2,1)S(1)}, u32[]{:S(2)}, u32[]{:S(2)}) collective-permute-start(bf16[2,64,384]{2,1,0:T(8,128)(2,1)S(1)} %get-tuple-element.56), channel_id=1, source_target_pairs={{0,24},{8,0},{16,8},{24,16},{1,25},{9,1},{17,9},{25,17},{2,26},{10... | collective-permute-start | bytes 294920 | tf_op jit(solution)/shard_map/ppermute | solution.py:28
  23.5 0.3 collective-permute-done.1.refs_2_
  23.8 0.1 pick1.1
  23.9 1.6 %collective-permute-start.3 = (bf16[2,64,384]{2,1,0:T(8,128)(2,1)S(1)}, bf16[2,64,384]{2,1,0:T(8,128)(2,1)S(1)}, u32[]{:S(2)}, u32[]{:S(2)}) collective-permute-start(bf16[2,64,384]{2,1,0:T(8,128)(2,1)S(1)} %get-tuple-element.46), channel_id=1, source_target_pairs={{0,8},{8,16},{16,24},{24,0},{1,9},{9,17},{17,25},{25,1},{2,10},{10... | collective-permute-start | bytes 294920 | tf_op jit(solution)/shard_map/ppermute | solution.py:28
  25.4 1.5 %collective-permute-start.4 = (bf16[2,64,384]{2,1,0:T(8,128)(2,1)S(1)}, bf16[2,64,384]{2,1,0:T(8,128)(2,1)S(1)}, u32[]{:S(2)}, u32[]{:S(2)}) collective-permute-start(bf16[2,64,384]{2,1,0:T(8,128)(2,1)S(1)} %get-tuple-element.47), channel_id=1, source_target_pairs={{0,16},{8,24},{16,0},{24,8},{1,17},{9,25},{17,1},{25,9},{2,18},{10... | collective-permute-start | bytes 294920 | tf_op jit(solution)/shard_map/ppermute | solution.py:28
  27.0 0.0 collective-permute-done.9.refs_1_
  27.0 1.4 %collective-permute-start.5 = (bf16[2,64,384]{2,1,0:T(8,128)(2,1)S(1)}, bf16[2,64,384]{2,1,0:T(8,128)(2,1)S(1)}, u32[]{:S(2)}, u32[]{:S(2)}) collective-permute-start(bf16[2,64,384]{2,1,0:T(8,128)(2,1)S(1)} %get-tuple-element.48), channel_id=1, source_target_pairs={{0,24},{8,0},{16,8},{24,16},{1,25},{9,1},{17,9},{25,17},{2,26},{10... | collective-permute-start | bytes 294920 | tf_op jit(solution)/shard_map/ppermute | solution.py:28
  28.4 2.0 %heads0.1 = (bf16[512,768]{1,0:T(8,128)(2,1)S(1)}, bf16[512,768]{1,0:T(8,128)(2,1)S(1)}, bf16[2,64,384]{2,1,0:T(8,128)(2,1)S(1)}, bf16[2,64,384]{2,1,0:T(8,128)(...) custom-call(s32[6]{0:T(128)S(4)} %get-tuple-element.40.facts_ref, ...), custom_call_target="tpu_custom_call" | custom-call | flops 603979776 | bytes 12582912 | tf_op jit(solution)/shard_map/heads0/pallas_call | solution.py:170
  30.5 0.8 %collective-permute-start.12 = (bf16[2,64,384]{2,1,0:T(8,128)(2,1)S(1)}, bf16[2,64,384]{2,1,0:T(8,128)(2,1)S(1)}, u32[]{:S(2)}, u32[]{:S(2)}) collective-permute-start(bf16[2,64,384]{2,1,0:T(8,128)(2,1)S(1)} %get-tuple-element.59), channel_id=1, source_target_pairs={{0,24},{8,0},{16,8},{24,16},{1,25},{9,1},{17,9},{25,17},{2,26},{10... | collective-permute-start | bytes 294920 | tf_op jit(solution)/shard_map/ppermute | solution.py:28
  31.3 1.3 %collective-permute-start.13 = (bf16[2,64,384]{2,1,0:T(8,128)(2,1)S(1)}, bf16[2,64,384]{2,1,0:T(8,128)(2,1)S(1)}, u32[]{:S(2)}, u32[]{:S(2)}) collective-permute-start(bf16[2,64,384]{2,1,0:T(8,128)(2,1)S(1)} %get-tuple-element.63), channel_id=1, source_target_pairs={{0,16},{8,24},{16,0},{24,8},{1,17},{9,25},{17,1},{25,9},{2,18},{10... | collective-permute-start | bytes 294920 | tf_op jit(solution)/shard_map/ppermute | solution.py:28
  32.6 0.0 collective-permute-done.3.refs_1_
  32.6 0.5 collective-permute-start.14
  33.0 2.7 %collective-permute-done.12.refs_6_.refs_1_ = bf16[2,64,384]{2,1,0:T(8,128)(2,1)S(1)} collective-permute-done((bf16[2,64,384]{2,1,0:T(8,128)(2,1)S(1)}, bf16[2,64,384]{2,1,0:T(8,128)(2,1)S(1)}, u32[]{:S(2)}, u32[]{:S(2)}) %collective-permute-start.12) | collective-permute-done | bytes 98336 | tf_op jit(solution)/shard_map/ppermute | solution.py:28
  35.7 2.0 %heads1.1 = (bf16[512,768]{1,0:T(8,128)(2,1)S(1)}, bf16[512,768]{1,0:T(8,128)(2,1)S(1)}, bf16[2,64,384]{2,1,0:T(8,128)(2,1)S(1)}, bf16[2,64,384]{2,1,0:T(8,128)(...) custom-call(s32[6]{0:T(128)S(4)} %get-tuple-element.40.facts_ref, ...), custom_call_target="tpu_custom_call", output_to_operand_aliasing={{0}: (7, {}), {1}: (8, {})} | custom-call | flops 603979776 | bytes 12582912 | tf_op jit(solution)/shard_map/heads1/pallas_call | solution.py:170
  37.8 1.5 %collective-permute-start.18 = (bf16[2,64,384]{2,1,0:T(8,128)(2,1)S(1)}, bf16[2,64,384]{2,1,0:T(8,128)(2,1)S(1)}, u32[]{:S(2)}, u32[]{:S(2)}) collective-permute-start(bf16[2,64,384]{2,1,0:T(8,128)(2,1)S(1)} %get-tuple-element.70), channel_id=1, source_target_pairs={{0,24},{8,0},{16,8},{24,16},{1,25},{9,1},{17,9},{25,17},{2,26},{10... | collective-permute-start | bytes 294920 | tf_op jit(solution)/shard_map/ppermute | solution.py:28
  39.3 1.5 %collective-permute-start.19 = (bf16[2,64,384]{2,1,0:T(8,128)(2,1)S(1)}, bf16[2,64,384]{2,1,0:T(8,128)(2,1)S(1)}, u32[]{:S(2)}, u32[]{:S(2)}) collective-permute-start(bf16[2,64,384]{2,1,0:T(8,128)(2,1)S(1)} %get-tuple-element.71), channel_id=1, source_target_pairs={{0,16},{8,24},{16,0},{24,8},{1,17},{9,25},{17,1},{25,9},{2,18},{10... | collective-permute-start | bytes 294920 | tf_op jit(solution)/shard_map/ppermute | solution.py:28
  40.8 0.0 collective-permute-start.20
  40.8 0.0 collective-permute-done.13.refs_2_
  40.8 0.0 collective-permute-done.14.refs_3_
  40.8 0.3 sum0.1
  41.1 2.9 %collective-permute-start.15 = (bf16[2,64,384]{2,1,0:T(8,128)(2,1)S(1)}, bf16[2,64,384]{2,1,0:T(8,128)(2,1)S(1)}, u32[]{:S(2)}, u32[]{:S(2)}) collective-permute-start(bf16[2,64,384]{2,1,0:T(8,128)(2,1)S(1)} %get-tuple-element.66), channel_id=1, source_target_pairs={{0,1},{1,2},{2,3},{3,0},{4,5},{5,6},{6,7},{7,4},{8,9},{9,10},{10,1... | collective-permute-start | bytes 294920 | tf_op jit(solution)/shard_map/ppermute | solution.py:28
  44.1 2.8 %collective-permute-start.16 = (bf16[2,64,384]{2,1,0:T(8,128)(2,1)S(1)}, bf16[2,64,384]{2,1,0:T(8,128)(2,1)S(1)}, u32[]{:S(2)}, u32[]{:S(2)}) collective-permute-start(bf16[2,64,384]{2,1,0:T(8,128)(2,1)S(1)} %get-tuple-element.67), channel_id=1, source_target_pairs={{0,2},{1,3},{2,0},{3,1},{4,6},{5,7},{6,4},{7,5},{8,10},{9,11},{10,... | collective-permute-start | bytes 294920 | tf_op jit(solution)/shard_map/ppermute | solution.py:28
  46.8 1.2 %collective-permute-start.17 = (bf16[2,64,384]{2,1,0:T(8,128)(2,1)S(1)}, bf16[2,64,384]{2,1,0:T(8,128)(2,1)S(1)}, u32[]{:S(2)}, u32[]{:S(2)}) collective-permute-start(bf16[2,64,384]{2,1,0:T(8,128)(2,1)S(1)} %get-tuple-element.68), channel_id=1, source_target_pairs={{0,3},{1,0},{2,1},{3,2},{4,7},{5,4},{6,5},{7,6},{8,11},{9,8},{10,9... | collective-permute-start | bytes 294920 | tf_op jit(solution)/shard_map/ppermute | solution.py:28
  48.0 0.3 sum1.1
  48.4 1.0 %collective-permute-start.21 = (bf16[2,64,384]{2,1,0:T(8,128)(2,1)S(1)}, bf16[2,64,384]{2,1,0:T(8,128)(2,1)S(1)}, u32[]{:S(2)}, u32[]{:S(2)}) collective-permute-start(bf16[2,64,384]{2,1,0:T(8,128)(2,1)S(1)} %get-tuple-element.74), channel_id=1, source_target_pairs={{0,1},{1,2},{2,3},{3,0},{4,5},{5,6},{6,7},{7,4},{8,9},{9,10},{10,1... | collective-permute-start | bytes 294920 | tf_op jit(solution)/shard_map/ppermute | solution.py:28
  49.4 3.0 %collective-permute-start.22 = (bf16[2,64,384]{2,1,0:T(8,128)(2,1)S(1)}, bf16[2,64,384]{2,1,0:T(8,128)(2,1)S(1)}, u32[]{:S(2)}, u32[]{:S(2)}) collective-permute-start(bf16[2,64,384]{2,1,0:T(8,128)(2,1)S(1)} %get-tuple-element.75), channel_id=1, source_target_pairs={{0,2},{1,3},{2,0},{3,1},{4,6},{5,7},{6,4},{7,5},{8,10},{9,11},{10,... | collective-permute-start | bytes 294920 | tf_op jit(solution)/shard_map/ppermute | solution.py:28
  52.3 1.2 %collective-permute-start.23 = (bf16[2,64,384]{2,1,0:T(8,128)(2,1)S(1)}, bf16[2,64,384]{2,1,0:T(8,128)(2,1)S(1)}, u32[]{:S(2)}, u32[]{:S(2)}) collective-permute-start(bf16[2,64,384]{2,1,0:T(8,128)(2,1)S(1)} %get-tuple-element.76), channel_id=1, source_target_pairs={{0,3},{1,0},{2,1},{3,2},{4,7},{5,4},{6,5},{7,6},{8,11},{9,8},{10,9... | collective-permute-start | bytes 294920 | tf_op jit(solution)/shard_map/ppermute | solution.py:28
  53.5 0.9 %copy.14 = bf16[1,1,512,768]{3,2,1,0:T(8,128)(2,1)} copy(bf16[1,1,512,768]{3,2,1,0:T(8,128)(2,1)S(1)} %bitcast.8) | data formatting | bytes 1572864
  54.4 0.9 %copy.15 = bf16[1,1,512,768]{3,2,1,0:T(8,128)(2,1)} copy(bf16[1,1,512,768]{3,2,1,0:T(8,128)(2,1)S(1)} %bitcast.9) | data formatting | bytes 1572864
  55.3 3.9 %collective-permute-done.22.refs_6_ = bf16[2,64,384]{2,1,0:T(8,128)(2,1)S(1)} collective-permute-done((bf16[2,64,384]{2,1,0:T(8,128)(2,1)S(1)}, bf16[2,64,384]{2,1,0:T(8,128)(2,1)S(1)}, u32[]{:S(2)}, u32[]{:S(2)}) %collective-permute-start.22) | collective-permute-done | bytes 98336 | tf_op jit(solution)/shard_map/ppermute | solution.py:28
  59.2 1.0 %join.1 = bf16[2,64,3072]{2,1,0:T(8,128)(2,1)} custom-call(bf16[2,64,384]{2,1,0:T(8,128)(2,1)S(1)} %get-tuple-element.65.refs_0_, bf16[2,64,384]{2,1,0:T(8,128)(2,1)S(1)} %collective-permute-done.15.refs_1_, bf16[2,64,384]{2,1,0:T(8,128)(2,1)S(1)} %collective-permute-done.16.refs_2_, bf16[2,64,384]{2,1,0:T(8,128)(2,1)S(1)} %collective-permute-done.17.refs_3_, ...), custom_call_target="tpu_custom_call" | custom-call | tf_op jit(solution)/shard_map/join/pallas_call | solution.py:201
  (22 shorter events, 0.1 us)
Async XLA Ops:
  0.6 0.7 %copy-start.5 = (s32[1,4]{1,0:T(1,128)S(1)}, s32[1,4]{1,0:T(1,128)}, u32[]{:S(2)}) copy-start(s32[1,4]{1,0:T(1,128)} %query_len_ref.1) | copy-start | bytes 52
  0.6 0.7 %copy-start.4 = (s32[1,4]{1,0:T(1,128)S(1)}, s32[1,4]{1,0:T(1,128)}, u32[]{:S(2)}) copy-start(s32[1,4]{1,0:T(1,128)} %key_len_ref.1) | copy-start | bytes 52
  0.7 0.7 %copy-start.3 = (s32[1,4]{1,0:T(1,128)S(1)}, s32[1,4]{1,0:T(1,128)}, u32[]{:S(2)}) copy-start(s32[1,4]{1,0:T(1,128)} %plan_ref.1) | copy-start | bytes 52
  1.3 1.1 %copy-start = (bf16[1,2,1,64,3072]{4,3,2,1,0:T(8,128)(2,1)S(1)}, bf16[1,2,1,64,3072]{4,3,2,1,0:T(8,128)(2,1)}, u32[]{:S(2)}) copy-start(bf16[1,2,1,64,3072]{4,3,2,1,0:T(8,128)(2,1)} %param.6) | copy-start | bytes 2359300
  2.5 26.0 %copy-start.1 = (bf16[1,1,512,768]{3,2,1,0:T(8,128)(2,1)S(1)}, bf16[1,1,512,768]{3,2,1,0:T(8,128)(2,1)}, u32[]{:S(2)}) copy-start(bf16[1,1,512,768]{3,2,1,0:T(8,128)(2,1)} %param.7) | copy-start | bytes 2359300
  2.5 26.0 %copy-start.2 = (bf16[1,1,512,768]{3,2,1,0:T(8,128)(2,1)S(1)}, bf16[1,1,512,768]{3,2,1,0:T(8,128)(2,1)}, u32[]{:S(2)}) copy-start(bf16[1,1,512,768]{3,2,1,0:T(8,128)(2,1)} %param.8) | copy-start | bytes 2359300
  3.1 8.8 %collective-permute-start.6 = (bf16[2,64,384]{2,1,0:T(8,128)(2,1)S(1)}, bf16[2,64,384]{2,1,0:T(8,128)(2,1)S(1)}, u32[]{:S(2)}, u32[]{:S(2)}) collective-permute-start(bf16[2,64,384]{2,1,0:T(8,128)(2,1)S(1)} %get-tuple-element.50), channel_id=1, source_target_pairs={{0,1},{1,2},{2,3},{3,0},{4,5},{5,6},{6,7},{7,4},{8,9},{9,10},{10,1... | collective-permute-start | bytes 294920 | tf_op jit(solution)/shard_map/ppermute | solution.py:28
  6.2 12.7 %collective-permute-start.7 = (bf16[2,64,384]{2,1,0:T(8,128)(2,1)S(1)}, bf16[2,64,384]{2,1,0:T(8,128)(2,1)S(1)}, u32[]{:S(2)}, u32[]{:S(2)}) collective-permute-start(bf16[2,64,384]{2,1,0:T(8,128)(2,1)S(1)} %get-tuple-element.51), channel_id=1, source_target_pairs={{0,2},{1,3},{2,0},{3,1},{4,6},{5,7},{6,4},{7,5},{8,10},{9,11},{10,... | collective-permute-start | bytes 294920 | tf_op jit(solution)/shard_map/ppermute | solution.py:28
  8.8 10.1 %collective-permute-start.8 = (bf16[2,64,384]{2,1,0:T(8,128)(2,1)S(1)}, bf16[2,64,384]{2,1,0:T(8,128)(2,1)S(1)}, u32[]{:S(2)}, u32[]{:S(2)}) collective-permute-start(bf16[2,64,384]{2,1,0:T(8,128)(2,1)S(1)} %get-tuple-element.52), channel_id=1, source_target_pairs={{0,3},{1,0},{2,1},{3,2},{4,7},{5,4},{6,5},{7,6},{8,11},{9,8},{10,9... | collective-permute-start | bytes 294920 | tf_op jit(solution)/shard_map/ppermute | solution.py:28
  10.1 12.0 %collective-permute-start = (bf16[2,64,384]{2,1,0:T(8,128)(2,1)S(1)}, bf16[2,64,384]{2,1,0:T(8,128)(2,1)S(1)}, u32[]{:S(2)}, u32[]{:S(2)}) collective-permute-start(bf16[2,64,384]{2,1,0:T(8,128)(2,1)S(1)} %get-tuple-element.42), channel_id=1, source_target_pairs={{0,1},{1,2},{2,3},{3,0},{4,5},{5,6},{6,7},{7,4},{8,9},{9,10},{10,1... | collective-permute-start | bytes 294920 | tf_op jit(solution)/shard_map/ppermute | solution.py:28
  10.8 13.0 %collective-permute-start.1 = (bf16[2,64,384]{2,1,0:T(8,128)(2,1)S(1)}, bf16[2,64,384]{2,1,0:T(8,128)(2,1)S(1)}, u32[]{:S(2)}, u32[]{:S(2)}) collective-permute-start(bf16[2,64,384]{2,1,0:T(8,128)(2,1)S(1)} %get-tuple-element.43), channel_id=1, source_target_pairs={{0,2},{1,3},{2,0},{3,1},{4,6},{5,7},{6,4},{7,5},{8,10},{9,11},{10,... | collective-permute-start | bytes 294920 | tf_op jit(solution)/shard_map/ppermute | solution.py:28
  11.9 11.9 %collective-permute-start.2 = (bf16[2,64,384]{2,1,0:T(8,128)(2,1)S(1)}, bf16[2,64,384]{2,1,0:T(8,128)(2,1)S(1)}, u32[]{:S(2)}, u32[]{:S(2)}) collective-permute-start(bf16[2,64,384]{2,1,0:T(8,128)(2,1)S(1)} %get-tuple-element.44), channel_id=1, source_target_pairs={{0,3},{1,0},{2,1},{3,2},{4,7},{5,4},{6,5},{7,6},{8,11},{9,8},{10,9... | collective-permute-start | bytes 294920 | tf_op jit(solution)/shard_map/ppermute | solution.py:28
  19.0 8.0 %collective-permute-start.9 = (bf16[2,64,384]{2,1,0:T(8,128)(2,1)S(1)}, bf16[2,64,384]{2,1,0:T(8,128)(2,1)S(1)}, u32[]{:S(2)}, u32[]{:S(2)}) collective-permute-start(bf16[2,64,384]{2,1,0:T(8,128)(2,1)S(1)} %get-tuple-element.54), channel_id=1, source_target_pairs={{0,8},{8,16},{16,24},{24,0},{1,9},{9,17},{17,25},{25,1},{2,10},{10... | collective-permute-start | bytes 294920 | tf_op jit(solution)/shard_map/ppermute | solution.py:28
  20.5 7.9 %collective-permute-start.10 = (bf16[2,64,384]{2,1,0:T(8,128)(2,1)S(1)}, bf16[2,64,384]{2,1,0:T(8,128)(2,1)S(1)}, u32[]{:S(2)}, u32[]{:S(2)}) collective-permute-start(bf16[2,64,384]{2,1,0:T(8,128)(2,1)S(1)} %get-tuple-element.55), channel_id=1, source_target_pairs={{0,16},{8,24},{16,0},{24,8},{1,17},{9,25},{17,1},{25,9},{2,18},{10... | collective-permute-start | bytes 294920 | tf_op jit(solution)/shard_map/ppermute | solution.py:28
  22.1 6.3 %collective-permute-start.11 = (bf16[2,64,384]{2,1,0:T(8,128)(2,1)S(1)}, bf16[2,64,384]{2,1,0:T(8,128)(2,1)S(1)}, u32[]{:S(2)}, u32[]{:S(2)}) collective-permute-start(bf16[2,64,384]{2,1,0:T(8,128)(2,1)S(1)} %get-tuple-element.56), channel_id=1, source_target_pairs={{0,24},{8,0},{16,8},{24,16},{1,25},{9,1},{17,9},{25,17},{2,26},{10... | collective-permute-start | bytes 294920 | tf_op jit(solution)/shard_map/ppermute | solution.py:28
  23.9 8.7 %collective-permute-start.3 = (bf16[2,64,384]{2,1,0:T(8,128)(2,1)S(1)}, bf16[2,64,384]{2,1,0:T(8,128)(2,1)S(1)}, u32[]{:S(2)}, u32[]{:S(2)}) collective-permute-start(bf16[2,64,384]{2,1,0:T(8,128)(2,1)S(1)} %get-tuple-element.46), channel_id=1, source_target_pairs={{0,8},{8,16},{16,24},{24,0},{1,9},{9,17},{17,25},{25,1},{2,10},{10... | collective-permute-start | bytes 294920 | tf_op jit(solution)/shard_map/ppermute | solution.py:28
  25.4 7.6 %collective-permute-start.4 = (bf16[2,64,384]{2,1,0:T(8,128)(2,1)S(1)}, bf16[2,64,384]{2,1,0:T(8,128)(2,1)S(1)}, u32[]{:S(2)}, u32[]{:S(2)}) collective-permute-start(bf16[2,64,384]{2,1,0:T(8,128)(2,1)S(1)} %get-tuple-element.47), channel_id=1, source_target_pairs={{0,16},{8,24},{16,0},{24,8},{1,17},{9,25},{17,1},{25,9},{2,18},{10... | collective-permute-start | bytes 294920 | tf_op jit(solution)/shard_map/ppermute | solution.py:28
  27.0 6.1 %collective-permute-start.5 = (bf16[2,64,384]{2,1,0:T(8,128)(2,1)S(1)}, bf16[2,64,384]{2,1,0:T(8,128)(2,1)S(1)}, u32[]{:S(2)}, u32[]{:S(2)}) collective-permute-start(bf16[2,64,384]{2,1,0:T(8,128)(2,1)S(1)} %get-tuple-element.48), channel_id=1, source_target_pairs={{0,24},{8,0},{16,8},{24,16},{1,25},{9,1},{17,9},{25,17},{2,26},{10... | collective-permute-start | bytes 294920 | tf_op jit(solution)/shard_map/ppermute | solution.py:28
  30.5 5.3 %collective-permute-start.12 = (bf16[2,64,384]{2,1,0:T(8,128)(2,1)S(1)}, bf16[2,64,384]{2,1,0:T(8,128)(2,1)S(1)}, u32[]{:S(2)}, u32[]{:S(2)}) collective-permute-start(bf16[2,64,384]{2,1,0:T(8,128)(2,1)S(1)} %get-tuple-element.59), channel_id=1, source_target_pairs={{0,24},{8,0},{16,8},{24,16},{1,25},{9,1},{17,9},{25,17},{2,26},{10... | collective-permute-start | bytes 294920 | tf_op jit(solution)/shard_map/ppermute | solution.py:28
  31.3 9.5 %collective-permute-start.13 = (bf16[2,64,384]{2,1,0:T(8,128)(2,1)S(1)}, bf16[2,64,384]{2,1,0:T(8,128)(2,1)S(1)}, u32[]{:S(2)}, u32[]{:S(2)}) collective-permute-start(bf16[2,64,384]{2,1,0:T(8,128)(2,1)S(1)} %get-tuple-element.63), channel_id=1, source_target_pairs={{0,16},{8,24},{16,0},{24,8},{1,17},{9,25},{17,1},{25,9},{2,18},{10... | collective-permute-start | bytes 294920 | tf_op jit(solution)/shard_map/ppermute | solution.py:28
  32.6 8.2 %collective-permute-start.14 = (bf16[2,64,384]{2,1,0:T(8,128)(2,1)S(1)}, bf16[2,64,384]{2,1,0:T(8,128)(2,1)S(1)}, u32[]{:S(2)}, u32[]{:S(2)}) collective-permute-start(bf16[2,64,384]{2,1,0:T(8,128)(2,1)S(1)} %get-tuple-element.64), channel_id=1, source_target_pairs={{0,8},{8,16},{16,24},{24,0},{1,9},{9,17},{17,25},{25,1},{2,10},{10... | collective-permute-start | bytes 294920 | tf_op jit(solution)/shard_map/ppermute | solution.py:28
  37.8 9.1 %collective-permute-start.18 = (bf16[2,64,384]{2,1,0:T(8,128)(2,1)S(1)}, bf16[2,64,384]{2,1,0:T(8,128)(2,1)S(1)}, u32[]{:S(2)}, u32[]{:S(2)}) collective-permute-start(bf16[2,64,384]{2,1,0:T(8,128)(2,1)S(1)} %get-tuple-element.70), channel_id=1, source_target_pairs={{0,24},{8,0},{16,8},{24,16},{1,25},{9,1},{17,9},{25,17},{2,26},{10... | collective-permute-start | bytes 294920 | tf_op jit(solution)/shard_map/ppermute | solution.py:28
  39.3 8.7 %collective-permute-start.19 = (bf16[2,64,384]{2,1,0:T(8,128)(2,1)S(1)}, bf16[2,64,384]{2,1,0:T(8,128)(2,1)S(1)}, u32[]{:S(2)}, u32[]{:S(2)}) collective-permute-start(bf16[2,64,384]{2,1,0:T(8,128)(2,1)S(1)} %get-tuple-element.71), channel_id=1, source_target_pairs={{0,16},{8,24},{16,0},{24,8},{1,17},{9,25},{17,1},{25,9},{2,18},{10... | collective-permute-start | bytes 294920 | tf_op jit(solution)/shard_map/ppermute | solution.py:28
  40.8 7.2 %collective-permute-start.20 = (bf16[2,64,384]{2,1,0:T(8,128)(2,1)S(1)}, bf16[2,64,384]{2,1,0:T(8,128)(2,1)S(1)}, u32[]{:S(2)}, u32[]{:S(2)}) collective-permute-start(bf16[2,64,384]{2,1,0:T(8,128)(2,1)S(1)} %get-tuple-element.72), channel_id=1, source_target_pairs={{0,8},{8,16},{16,24},{24,0},{1,9},{9,17},{17,25},{25,1},{2,10},{10... | collective-permute-start | bytes 294920 | tf_op jit(solution)/shard_map/ppermute | solution.py:28
  41.1 11.2 %collective-permute-start.15 = (bf16[2,64,384]{2,1,0:T(8,128)(2,1)S(1)}, bf16[2,64,384]{2,1,0:T(8,128)(2,1)S(1)}, u32[]{:S(2)}, u32[]{:S(2)}) collective-permute-start(bf16[2,64,384]{2,1,0:T(8,128)(2,1)S(1)} %get-tuple-element.66), channel_id=1, source_target_pairs={{0,1},{1,2},{2,3},{3,0},{4,5},{5,6},{6,7},{7,4},{8,9},{9,10},{10,1... | collective-permute-start | bytes 294920 | tf_op jit(solution)/shard_map/ppermute | solution.py:28
  44.1 11.2 %collective-permute-start.16 = (bf16[2,64,384]{2,1,0:T(8,128)(2,1)S(1)}, bf16[2,64,384]{2,1,0:T(8,128)(2,1)S(1)}, u32[]{:S(2)}, u32[]{:S(2)}) collective-permute-start(bf16[2,64,384]{2,1,0:T(8,128)(2,1)S(1)} %get-tuple-element.67), channel_id=1, source_target_pairs={{0,2},{1,3},{2,0},{3,1},{4,6},{5,7},{6,4},{7,5},{8,10},{9,11},{10,... | collective-permute-start | bytes 294920 | tf_op jit(solution)/shard_map/ppermute | solution.py:28
  46.8 8.5 %collective-permute-start.17 = (bf16[2,64,384]{2,1,0:T(8,128)(2,1)S(1)}, bf16[2,64,384]{2,1,0:T(8,128)(2,1)S(1)}, u32[]{:S(2)}, u32[]{:S(2)}) collective-permute-start(bf16[2,64,384]{2,1,0:T(8,128)(2,1)S(1)} %get-tuple-element.68), channel_id=1, source_target_pairs={{0,3},{1,0},{2,1},{3,2},{4,7},{5,4},{6,5},{7,6},{8,11},{9,8},{10,9... | collective-permute-start | bytes 294920 | tf_op jit(solution)/shard_map/ppermute | solution.py:28
  48.4 6.9 %collective-permute-start.21 = (bf16[2,64,384]{2,1,0:T(8,128)(2,1)S(1)}, bf16[2,64,384]{2,1,0:T(8,128)(2,1)S(1)}, u32[]{:S(2)}, u32[]{:S(2)}) collective-permute-start(bf16[2,64,384]{2,1,0:T(8,128)(2,1)S(1)} %get-tuple-element.74), channel_id=1, source_target_pairs={{0,1},{1,2},{2,3},{3,0},{4,5},{5,6},{6,7},{7,4},{8,9},{9,10},{10,1... | collective-permute-start | bytes 294920 | tf_op jit(solution)/shard_map/ppermute | solution.py:28
  49.4 9.8 %collective-permute-start.22 = (bf16[2,64,384]{2,1,0:T(8,128)(2,1)S(1)}, bf16[2,64,384]{2,1,0:T(8,128)(2,1)S(1)}, u32[]{:S(2)}, u32[]{:S(2)}) collective-permute-start(bf16[2,64,384]{2,1,0:T(8,128)(2,1)S(1)} %get-tuple-element.75), channel_id=1, source_target_pairs={{0,2},{1,3},{2,0},{3,1},{4,6},{5,7},{6,4},{7,5},{8,10},{9,11},{10,... | collective-permute-start | bytes 294920 | tf_op jit(solution)/shard_map/ppermute | solution.py:28
  52.3 6.8 %collective-permute-start.23 = (bf16[2,64,384]{2,1,0:T(8,128)(2,1)S(1)}, bf16[2,64,384]{2,1,0:T(8,128)(2,1)S(1)}, u32[]{:S(2)}, u32[]{:S(2)}) collective-permute-start(bf16[2,64,384]{2,1,0:T(8,128)(2,1)S(1)} %get-tuple-element.76), channel_id=1, source_target_pairs={{0,3},{1,0},{2,1},{3,2},{4,7},{5,4},{6,5},{7,6},{8,11},{9,8},{10,9... | collective-permute-start | bytes 294920 | tf_op jit(solution)/shard_map/ppermute | solution.py:28

commit v3 on v2

v3 whole, which is shorter than its diff:
```python
import functools
import math

import jax
import jax.numpy as jnp
from jax import lax
from jax.experimental import pallas as pl
from jax.experimental.pallas import tpu as pltpu
from jax.sharding import PartitionSpec as P

HEAD_DIM = 128
CHUNKS = 2

SMEM = pl.BlockSpec(memory_space=pltpu.SMEM)
VMEM = pl.BlockSpec(memory_space=pltpu.VMEM)
ANY = pl.BlockSpec(memory_space=pl.ANY)


def ahead(index, step, count):
    return lax.rem(index + step, count)


def behind(index, step, count):
    return lax.rem(index + count - step, count)


def swap(piece, step, count):
    return lax.ppermute(piece, "section", [(i, i ^ step) for i in range(count)])


def shift(piece, step, count):
    return lax.ppermute(piece, "tp", [(i, (i + step) % count) for i in range(count)])


def near(array):
    return pltpu.with_memory_space_constraint(array, pltpu.VMEM)


def columns_of(chunk, width, head_cols, owner):
    return pl.ds(pl.multiple_of(owner * head_cols + chunk * width, 128), width)


def run_copies(pairs, sem):
    copies = [pltpu.make_async_copy(source, target, sem.at[i]) for i, (source, target) in enumerate(pairs)]
    for copy in copies:
        copy.start()
    for copy in copies:
        copy.wait()


def split_kernel(tp_count, chunk, width, head_cols, memory_ref, *refs):
    me = lax.axis_index("tp")
    outs, sem = refs[:-1], refs[-1]
    owners = [ahead(me, step, tp_count) for step in range(tp_count)]
    run_copies([(memory_ref.at[:, :, columns_of(chunk, width, head_cols, o)], out) for o, out in zip(owners, outs)], sem)


def facts_kernel(section_count, plan_ref, key_len_ref, query_len_ref, facts_ref):
    for section in range(section_count):
        facts_ref[section] = plan_ref[0, section]
    micro = plan_ref[0, lax.axis_index("section")]
    facts_ref[section_count] = key_len_ref[0, micro]
    facts_ref[section_count + 1] = query_len_ref[0, micro]


def pick_kernel(tp_count, steps, facts_ref, *refs):
    pieces, outs = refs[:tp_count], refs[-len(steps) :]
    me, tp_me = lax.axis_index("section"), lax.axis_index("tp")
    for step, out_ref in zip(steps, outs):
        back = behind(tp_me, facts_ref[me ^ step], tp_count)
        for which in range(tp_count):

            @pl.when(back == which)
            def _():
                out_ref[...] = pieces[which][...]


def heads_kernel(section_count, chunk, width, facts_ref, query_ref, grad_ref, *refs):
    blocks = refs[:section_count]
    attended_ref, grad_query_ref, *outs = refs[-2 - section_count :]
    me = lax.axis_index("section")
    key_len, query_len = facts_ref[section_count], facts_ref[section_count + 1]
    block_len = blocks[0].shape[1]
    tgt = query_ref.shape[0]
    scaling = HEAD_DIM ** (-0.5)
    scaling_two = scaling * math.log2(math.e)
    row = lax.broadcasted_iota(jnp.int32, (block_len, 1), 0)
    lefts = [key_len - (me ^ step) * block_len for step in range(section_count)]
    bias = jnp.concatenate([jnp.where(row < left, 0.0, -jnp.inf) for left in lefts], axis=0)
    query_valid = lax.broadcasted_iota(jnp.int32, (tgt, HEAD_DIM), 0) < query_len
    nt = (((1,), (1,)), ((), ()))
    tn = (((0,), (0,)), ((), ()))
    none = jnp.zeros((), jnp.bfloat16)
    for head in range(width // HEAD_DIM):
        cols = slice(head * HEAD_DIM, (head + 1) * HEAD_DIM)
        wide = slice(chunk * width + head * HEAD_DIM, chunk * width + (head + 1) * HEAD_DIM)
        query = query_ref[:, wide]
        grad = jnp.where(query_valid, grad_ref[:, wide], none)
        keys = jnp.concatenate([block[0, :, cols] for block in blocks], axis=0)
        values = jnp.concatenate([block[1, :, cols] for block in blocks], axis=0)
        scores = lax.dot_general(keys, query, nt, preferred_element_type=jnp.float32) + bias
        top = jnp.max(scores, axis=0, keepdims=True)
        expon = jnp.exp2((scores - top) * scaling_two)
        probs = expon * (1.0 / jnp.sum(expon, axis=0, keepdims=True))
        half = probs.astype(jnp.bfloat16)
        grad_probs = lax.dot_general(values, grad, nt, preferred_element_type=jnp.float32)
        row_dot = jnp.sum(probs * grad_probs, axis=0, keepdims=True)
        grad_scores = (probs * (grad_probs - row_dot)).astype(jnp.bfloat16)
        grad_value = jnp.dot(half, grad, preferred_element_type=jnp.float32).astype(jnp.bfloat16)
        grad_key = jnp.dot(grad_scores, query, preferred_element_type=jnp.float32) * scaling
        grad_key = grad_key.astype(jnp.bfloat16)
        context = lax.dot_general(values, half, tn, preferred_element_type=jnp.float32).astype(jnp.bfloat16).T
        attended_ref[:, wide] = jnp.where(query_valid, context, none)
        grad_query = lax.dot_general(keys, grad_scores, tn, preferred_element_type=jnp.float32) * scaling
        grad_query_ref[:, wide] = grad_query.astype(jnp.bfloat16).T
        for step in range(section_count):
            rows = slice(step * block_len, (step + 1) * block_len)
            outs[step][0, :, cols] = grad_key[rows]
            outs[step][1, :, cols] = grad_value[rows]


def sum_kernel(tp_count, section_count, facts_ref, *refs):
    pieces, outs = refs[:section_count], refs[section_count:]
    me, tp_me = lax.axis_index("section"), lax.axis_index("tp")
    for step in range(tp_count):
        micro = ahead(tp_me, step, tp_count)
        total = jnp.zeros(outs[step].shape, jnp.float32)
        for back in range(section_count):
            weight = jnp.where(facts_ref[me ^ back] == micro, 1.0, 0.0)
            total = total + weight * pieces[back][...].astype(jnp.float32)
        outs[step][...] = total.astype(jnp.bfloat16)


def join_kernel(tp_count, chunk, width, head_cols, *refs):
    pieces, out_ref, sem = refs[:tp_count], refs[-2], refs[-1]
    me = lax.axis_index("tp")
    owners = [behind(me, step, tp_count) for step in range(tp_count)]
    run_copies([(piece, out_ref.at[:, :, columns_of(chunk, width, head_cols, o)]) for o, piece in zip(owners, pieces)], sem)


def body(enc_kv, queries, grad_out, plan, enc_lengths, tgt_lengths):
    section_count = lax.axis_size("section")
    tp_count = lax.axis_size("tp")
    memory = enc_kv[0, :, 0]
    query, grad = queries[0, 0], grad_out[0, 0]
    block_len, columns = memory.shape[1:]
    tgt, head_cols = query.shape
    heads = head_cols // HEAD_DIM
    chunks = math.gcd(CHUNKS, heads)
    width = head_cols // chunks
    piece = pltpu.VMEM((2, block_len, width), jnp.bfloat16)
    rows = pltpu.VMEM((tgt, head_cols), jnp.bfloat16)
    params = pltpu.CompilerParams(vmem_limit_bytes=16 * 1024 * 1024)

    memory = pltpu.with_memory_space_constraint(memory, pltpu.HBM)
    copy_sem = pltpu.SemaphoreType.DMA((tp_count,))
    parts = []
    for chunk in range(chunks):
        split = pl.pallas_call(
            functools.partial(split_kernel, tp_count, chunk, width, head_cols),
            out_shape=[piece] * tp_count,
            in_specs=[ANY],
            out_specs=[VMEM] * tp_count,
            scratch_shapes=[copy_sem],
            compiler_params=params,
            name=f"split{chunk}",
        )(memory)
        parts.append([split[0]] + [shift(split[step], step, tp_count) for step in range(1, tp_count)])
    facts = pl.pallas_call(
        functools.partial(facts_kernel, section_count),
        out_shape=pltpu.SMEM((section_count + 2,), jnp.int32),
        in_specs=[SMEM] * 3,
        out_specs=SMEM,
        compiler_params=params,
        name="facts",
    )(plan, enc_lengths, tgt_lengths)
    facts = pltpu.with_memory_space_constraint(facts, pltpu.SMEM)

    def pick(chunk, steps, gate):
        return pl.pallas_call(
            functools.partial(pick_kernel, tp_count, steps),
            out_shape=[piece] * len(steps),
            in_specs=[SMEM] + [VMEM] * (tp_count + len(gate)),
            out_specs=[VMEM] * len(steps),
            compiler_params=params,
            name=f"pick{chunk}",
        )(facts, *map(near, parts[chunk]), *map(near, gate))

    query, grad = near(query), near(grad)
    results, returned = [], []
    steps = list(range(section_count))
    for chunk in range(chunks):
        if chunk == 0:
            picked = pick(chunk, steps, [])
        else:
            picked = pick(chunk, steps[:-1], []) + pick(chunk, steps[-1:], [returned[-1][0]])
        arrived = [picked[0]] + [swap(picked[step], step, section_count) for step in steps[1:]]
        done = pl.pallas_call(
            functools.partial(heads_kernel, section_count, chunk, width),
            out_shape=[rows, rows] + [piece] * section_count,
            in_specs=[SMEM] + [VMEM] * (2 + section_count + len(results)),
            out_specs=[VMEM] * (2 + section_count),
            input_output_aliases={3 + section_count + i: i for i in range(len(results))},
            compiler_params=params,
            cost_estimate=pl.CostEstimate(
                flops=12 * tgt * block_len * section_count * width, bytes_accessed=8 * 2**20, transcendentals=0
            ),
            name=f"heads{chunk}",
        )(facts, query, grad, *map(near, arrived), *map(near, results))
        results = list(done[:2])
        returned.append([done[2]] + [swap(done[2 + step], step, section_count) for step in steps[1:]])

    whole = []
    for chunk in range(chunks):
        summed = pl.pallas_call(
            functools.partial(sum_kernel, tp_count, section_count),
            out_shape=[piece] * tp_count,
            in_specs=[SMEM] + [VMEM] * section_count,
            out_specs=[VMEM] * tp_count,
            compiler_params=params,
            name=f"sum{chunk}",
        )(facts, *map(near, returned[chunk]))
        pieces = [summed[0]] + [shift(summed[step], step, tp_count) for step in range(1, tp_count)]
        whole = [
            pl.pallas_call(
                functools.partial(join_kernel, tp_count, chunk, width, head_cols),
                out_shape=pltpu.HBM((2, block_len, columns), jnp.bfloat16),
                in_specs=[VMEM] * tp_count + [ANY] * len(whole),
                out_specs=ANY,
                scratch_shapes=[copy_sem],
                input_output_aliases={tp_count: 0} if whole else {},
                compiler_params=params,
                name=f"join{chunk}",
            )(*map(near, pieces), *whole)
        ]
    return (results[0][None, None], results[1][None, None], whole[0][None, :, None])


def solution(mesh):
    in_specs = (
        P("dp", None, "tp", "section", None),
        P("dp", "section", None, "tp"),
        P("dp", "section", None, "tp"),
        P("dp", None),
        P("dp", None),
        P("dp", None),
    )
    out_specs = (
        P("dp", "section", None, "tp"),
        P("dp", "section", None, "tp"),
        P("dp", None, "tp", "section", None),
    )
    return jax.shard_map(body, mesh=mesh, in_specs=in_specs, out_specs=out_specs, check_vma=False)
```

time: 60.3 us -> 58.8 us (0.975)
  Pallas kernels: 6.49 us -> 9.16 us
  local copies, waits for them, and re-layouts: 3.56 us -> 1.78 us
  starting transfers between devices: 37.8 us -> 36.5 us
  waiting for transfers between devices: 11.5 us -> 10.4 us
    pallas_call x4 -> x8, Pallas kernels: 1.82 us -> 4.5 us  [the longest x2 2.16 us: body(): pl.pallas_call(functools.partial(split_kernel, tp_count, chunk, width, he...]
    unnamed x14 -> x12, local copies, waits for them, and re-layouts: 3.56 us -> 1.78 us
    ppermute x24, starting transfers between devices: 37.8 us -> 36.5 us  [the longest x12 22.3 us: shift(): lax.ppermute(piece, 'tp', [(i, (i + step) % count) for i in range(count)])]
    ppermute x24, waiting for transfers between devices: 11.5 us -> 10.4 us  [the longest x12 7.72 us: shift(): lax.ppermute(piece, 'tp', [(i, (i + step) % count) for i in range(count)])]
  transfers between devices with their start and end apart: 24 -> 24, of which waited for: 5 -> 5; matrix products, arithmetic and copies ran while one was open for 3% -> 3% of each run, Pallas kernels for 8% -> 12%
where the time goes in v3:
time: 58.8 us; the launch traced here: 58.6 us
  starting transfers between devices  36.5 us (62%)
  waiting for transfers between devices  10.4 us (18%)
  Pallas kernels  9.16 us (16%)
  local copies, waits for them, and re-layouts  1.78 us (3%)
  between operations  0.8 us (1%)
    ppermute x12, starting transfers between devices, shift(): lax.ppermute(piece, 'tp', [(i, (i + step) % count) for i in range(count)])  22.3 us
    ppermute x12, starting transfers between devices, swap(): return lax.ppermute(piece, 'section', [(i, i ^ step) for i in range(count)])  14.2 us
    ppermute x12, waiting for transfers between devices, shift(): lax.ppermute(piece, 'tp', [(i, (i + step) % count) for i in range(count)])  7.72 us
    pallas_call x2, Pallas kernels, body(): pl.pallas_call(functools.partial(heads_kernel, section_count, chunk, widt...  4.03 us
    ppermute x12, waiting for transfers between devices, swap(): return lax.ppermute(piece, 'section', [(i, i ^ step) for i in range(count)])  2.66 us
    pallas_call x2, Pallas kernels, body(): pl.pallas_call(functools.partial(split_kernel, tp_count, chunk, width, he...  2.16 us
    unnamed x12, local copies, waits for them, and re-layouts  1.78 us
    pallas_call x2, Pallas kernels, body(): pl.pallas_call(functools.partial(join_kernel, tp_count, chunk, width, hea...  1.54 us
  transfers between devices with their start and end apart: 24, of which 5 were waited for; matrix products, arithmetic and copies ran while one was open for 3% of the time, Pallas kernels for 12%

profile of v3, /device:TPU:0, one launch (start us, length us, event | category | flops | bytes accessed | tf_op | source)
XLA Modules:
  0.0 58.6 jit_solution(5792119660853580989)
XLA Ops:
  0.7 1.1 %split0.1 = (bf16[2,64,384]{2,1,0:T(8,128)(2,1)S(1)}, bf16[2,64,384]{2,1,0:T(8,128)(2,1)S(1)}, bf16[2,64,384]{2,1,0:T(8,128)(2,1)S(1)}, bf16[2,64,384]{2,1,0:T(8,128)(2,1)S(1)}) custom-call(bf16[2,64,3072]{2,1,0:T(8,128)(2,1)} %bitcast.14), custom_call_target="tpu_custom_call" | custom-call | tf_op jit(solution)/shard_map/split0/pallas_call | solution.py:159
  1.8 3.1 %collective-permute-start.5 = (bf16[2,64,384]{2,1,0:T(8,128)(2,1)S(1)}, bf16[2,64,384]{2,1,0:T(8,128)(2,1)S(1)}, u32[]{:S(2)}, u32[]{:S(2)}) collective-permute-start(bf16[2,64,384]{2,1,0:T(8,128)(2,1)S(1)} %get-tuple-element.46), channel_id=1, source_target_pairs={{0,1},{1,2},{2,3},{3,0},{4,5},{5,6},{6,7},{7,4},{8,9},{9,10},{10,1... | collective-permute-start | bytes 294920 | tf_op jit(solution)/shard_map/ppermute | solution.py:32
  4.8 2.6 %collective-permute-start.6 = (bf16[2,64,384]{2,1,0:T(8,128)(2,1)S(1)}, bf16[2,64,384]{2,1,0:T(8,128)(2,1)S(1)}, u32[]{:S(2)}, u32[]{:S(2)}) collective-permute-start(bf16[2,64,384]{2,1,0:T(8,128)(2,1)S(1)} %get-tuple-element.47), channel_id=1, source_target_pairs={{0,2},{1,3},{2,0},{3,1},{4,6},{5,7},{6,4},{7,5},{8,10},{9,11},{10,... | collective-permute-start | bytes 294920 | tf_op jit(solution)/shard_map/ppermute | solution.py:32
  7.4 1.3 %collective-permute-start.7 = (bf16[2,64,384]{2,1,0:T(8,128)(2,1)S(1)}, bf16[2,64,384]{2,1,0:T(8,128)(2,1)S(1)}, u32[]{:S(2)}, u32[]{:S(2)}) collective-permute-start(bf16[2,64,384]{2,1,0:T(8,128)(2,1)S(1)} %get-tuple-element.48), channel_id=1, source_target_pairs={{0,3},{1,0},{2,1},{3,2},{4,7},{5,4},{6,5},{7,6},{8,11},{9,8},{10,9... | collective-permute-start | bytes 294920 | tf_op jit(solution)/shard_map/ppermute | solution.py:32
  8.8 1.1 %split1.1 = (bf16[2,64,384]{2,1,0:T(8,128)(2,1)S(1)}, bf16[2,64,384]{2,1,0:T(8,128)(2,1)S(1)}, bf16[2,64,384]{2,1,0:T(8,128)(2,1)S(1)}, bf16[2,64,384]{2,1,0:T(8,128)(2,1)S(1)}) custom-call(bf16[2,64,3072]{2,1,0:T(8,128)(2,1)} %bitcast.15), custom_call_target="tpu_custom_call" | custom-call | tf_op jit(solution)/shard_map/split1/pallas_call | solution.py:159
  9.9 0.7 %collective-permute-start = (bf16[2,64,384]{2,1,0:T(8,128)(2,1)S(1)}, bf16[2,64,384]{2,1,0:T(8,128)(2,1)S(1)}, u32[]{:S(2)}, u32[]{:S(2)}) collective-permute-start(bf16[2,64,384]{2,1,0:T(8,128)(2,1)S(1)} %get-tuple-element.39), channel_id=1, source_target_pairs={{0,1},{1,2},{2,3},{3,0},{4,5},{5,6},{6,7},{7,4},{8,9},{9,10},{10,1... | collective-permute-start | bytes 294920 | tf_op jit(solution)/shard_map/ppermute | solution.py:32
  10.6 0.4 collective-permute-start.1
  11.0 0.6 facts.1.facts_ref
  11.5 0.0 collective-permute-done.5.refs_1_
  11.6 2.8 %collective-permute-start.2 = (bf16[2,64,384]{2,1,0:T(8,128)(2,1)S(1)}, bf16[2,64,384]{2,1,0:T(8,128)(2,1)S(1)}, u32[]{:S(2)}, u32[]{:S(2)}) collective-permute-start(bf16[2,64,384]{2,1,0:T(8,128)(2,1)S(1)} %get-tuple-element.41), channel_id=1, source_target_pairs={{0,3},{1,0},{2,1},{3,2},{4,7},{5,4},{6,5},{7,6},{8,11},{9,8},{10,9... | collective-permute-start | bytes 294920 | tf_op jit(solution)/shard_map/ppermute | solution.py:32
  14.4 2.5 %collective-permute-done.6.refs_2_ = bf16[2,64,384]{2,1,0:T(8,128)(2,1)S(1)} collective-permute-done((bf16[2,64,384]{2,1,0:T(8,128)(2,1)S(1)}, bf16[2,64,384]{2,1,0:T(8,128)(2,1)S(1)}, u32[]{:S(2)}, u32[]{:S(2)}) %collective-permute-start.6) | collective-permute-done | bytes 98336 | tf_op jit(solution)/shard_map/ppermute | solution.py:32
  16.9 0.0 collective-permute-done.7.refs_3_
  16.9 0.1 pick0.1
  17.0 1.6 %collective-permute-start.8 = (bf16[2,64,384]{2,1,0:T(8,128)(2,1)S(1)}, bf16[2,64,384]{2,1,0:T(8,128)(2,1)S(1)}, u32[]{:S(2)}, u32[]{:S(2)}) collective-permute-start(bf16[2,64,384]{2,1,0:T(8,128)(2,1)S(1)} %get-tuple-element.50), channel_id=1, source_target_pairs={{0,8},{8,0},{16,24},{24,16},{1,9},{9,1},{17,25},{25,17},{2,10},{10... | collective-permute-start | bytes 294920 | tf_op jit(solution)/shard_map/ppermute | solution.py:28
  18.6 1.5 %collective-permute-start.9 = (bf16[2,64,384]{2,1,0:T(8,128)(2,1)S(1)}, bf16[2,64,384]{2,1,0:T(8,128)(2,1)S(1)}, u32[]{:S(2)}, u32[]{:S(2)}) collective-permute-start(bf16[2,64,384]{2,1,0:T(8,128)(2,1)S(1)} %get-tuple-element.51), channel_id=1, source_target_pairs={{0,16},{8,24},{16,0},{24,8},{1,17},{9,25},{17,1},{25,9},{2,18},{10... | collective-permute-start | bytes 294920 | tf_op jit(solution)/shard_map/ppermute | solution.py:28
  20.1 0.5 collective-permute-start.10
  20.6 1.9 %collective-permute-done.1.refs_2_ = bf16[2,64,384]{2,1,0:T(8,128)(2,1)S(1)} collective-permute-done((bf16[2,64,384]{2,1,0:T(8,128)(2,1)S(1)}, bf16[2,64,384]{2,1,0:T(8,128)(2,1)S(1)}, u32[]{:S(2)}, u32[]{:S(2)}) %collective-permute-start.1) | collective-permute-done | bytes 98336 | tf_op jit(solution)/shard_map/ppermute | solution.py:32
  22.4 0.0 collective-permute-done.2.refs_3_
  22.4 0.1 pick1.2
  22.5 1.6 %collective-permute-start.3 = (bf16[2,64,384]{2,1,0:T(8,128)(2,1)S(1)}, bf16[2,64,384]{2,1,0:T(8,128)(2,1)S(1)}, u32[]{:S(2)}, u32[]{:S(2)}) collective-permute-start(bf16[2,64,384]{2,1,0:T(8,128)(2,1)S(1)} %get-tuple-element.43), channel_id=1, source_target_pairs={{0,8},{8,0},{16,24},{24,16},{1,9},{9,1},{17,25},{25,17},{2,10},{10... | collective-permute-start | bytes 294920 | tf_op jit(solution)/shard_map/ppermute | solution.py:28
  24.1 1.5 %collective-permute-start.4 = (bf16[2,64,384]{2,1,0:T(8,128)(2,1)S(1)}, bf16[2,64,384]{2,1,0:T(8,128)(2,1)S(1)}, u32[]{:S(2)}, u32[]{:S(2)}) collective-permute-start(bf16[2,64,384]{2,1,0:T(8,128)(2,1)S(1)} %get-tuple-element.44), channel_id=1, source_target_pairs={{0,16},{8,24},{16,0},{24,8},{1,17},{9,25},{17,1},{25,9},{2,18},{10... | collective-permute-start | bytes 294920 | tf_op jit(solution)/shard_map/ppermute | solution.py:28
  25.6 0.0 collective-permute-done.9.refs_2_
  25.6 0.0 collective-permute-done.10.refs_3_
  25.6 2.0 %heads0.1 = (bf16[512,768]{1,0:T(8,128)(2,1)S(1)}, bf16[512,768]{1,0:T(8,128)(2,1)S(1)}, bf16[2,64,384]{2,1,0:T(8,128)(2,1)S(1)}, bf16[2,64,384]{2,1,0:T(8,128)(...) custom-call(s32[6]{0:T(128)S(4)} %facts.1.facts_ref, bf16[512,768]{1,0:T(8,128)(2,1)S(1)} %bitcast.10, ...), custom_call_target="tpu_custom_call" | custom-call | flops 603979776 | bytes 8388608 | tf_op jit(solution)/shard_map/heads0/pallas_call | solution.py:198
  27.7 0.6 collective-permute-start.11
  28.3 1.5 %collective-permute-start.18 = (bf16[2,64,384]{2,1,0:T(8,128)(2,1)S(1)}, bf16[2,64,384]{2,1,0:T(8,128)(2,1)S(1)}, u32[]{:S(2)}, u32[]{:S(2)}) collective-permute-start(bf16[2,64,384]{2,1,0:T(8,128)(2,1)S(1)} %get-tuple-element.66), channel_id=1, source_target_pairs={{0,8},{8,0},{16,24},{24,16},{1,9},{9,1},{17,25},{25,17},{2,10},{10... | collective-permute-start | bytes 294920 | tf_op jit(solution)/shard_map/ppermute | solution.py:28
  29.8 1.5 %collective-permute-start.19 = (bf16[2,64,384]{2,1,0:T(8,128)(2,1)S(1)}, bf16[2,64,384]{2,1,0:T(8,128)(2,1)S(1)}, u32[]{:S(2)}, u32[]{:S(2)}) collective-permute-start(bf16[2,64,384]{2,1,0:T(8,128)(2,1)S(1)} %get-tuple-element.67), channel_id=1, source_target_pairs={{0,16},{8,24},{16,0},{24,8},{1,17},{9,25},{17,1},{25,9},{2,18},{10... | collective-permute-start | bytes 294920 | tf_op jit(solution)/shard_map/ppermute | solution.py:28
  31.3 0.5 collective-permute-start.20
  31.8 2.6 %collective-permute-done.11.refs_3_ = bf16[2,64,384]{2,1,0:T(8,128)(2,1)S(1)} collective-permute-done((bf16[2,64,384]{2,1,0:T(8,128)(2,1)S(1)}, bf16[2,64,384]{2,1,0:T(8,128)(2,1)S(1)}, u32[]{:S(2)}, u32[]{:S(2)}) %collective-permute-start.11) | collective-permute-done | bytes 98336 | tf_op jit(solution)/shard_map/ppermute | solution.py:28
  34.4 2.0 %heads1.1 = (bf16[512,768]{1,0:T(8,128)(2,1)S(1)}, bf16[512,768]{1,0:T(8,128)(2,1)S(1)}, bf16[2,64,384]{2,1,0:T(8,128)(2,1)S(1)}, bf16[2,64,384]{2,1,0:T(8,128)(...) custom-call(s32[6]{0:T(128)S(4)} %facts.1.facts_ref, ...), custom_call_target="tpu_custom_call", output_to_operand_aliasing={{0}: (7, {}), {1}: (8, {})} | custom-call | flops 603979776 | bytes 8388608 | tf_op jit(solution)/shard_map/heads1/pallas_call | solution.py:198
  36.4 0.5 collective-permute-start.12
  36.9 0.5 collective-permute-start.13
  37.4 0.0 collective-permute-done.18.refs_1_
  37.4 2.5 %collective-permute-start.14 = (bf16[2,64,384]{2,1,0:T(8,128)(2,1)S(1)}, bf16[2,64,384]{2,1,0:T(8,128)(2,1)S(1)}, u32[]{:S(2)}, u32[]{:S(2)}) collective-permute-start(bf16[2,64,384]{2,1,0:T(8,128)(2,1)S(1)} %get-tuple-element.61), channel_id=1, source_target_pairs={{0,24},{8,16},{16,8},{24,0},{1,25},{9,17},{17,9},{25,1},{2,26},{10... | collective-permute-start | bytes 294920 | tf_op jit(solution)/shard_map/ppermute | solution.py:28
  40.0 0.3 sum0.1
  40.3 4.0 %collective-permute-start.21 = (bf16[2,64,384]{2,1,0:T(8,128)(2,1)S(1)}, bf16[2,64,384]{2,1,0:T(8,128)(2,1)S(1)}, u32[]{:S(2)}, u32[]{:S(2)}) collective-permute-start(bf16[2,64,384]{2,1,0:T(8,128)(2,1)S(1)} %get-tuple-element.70), channel_id=1, source_target_pairs={{0,1},{1,2},{2,3},{3,0},{4,5},{5,6},{6,7},{7,4},{8,9},{9,10},{10,1... | collective-permute-start | bytes 294920 | tf_op jit(solution)/shard_map/ppermute | solution.py:32
  44.3 2.3 %collective-permute-start.22 = (bf16[2,64,384]{2,1,0:T(8,128)(2,1)S(1)}, bf16[2,64,384]{2,1,0:T(8,128)(2,1)S(1)}, u32[]{:S(2)}, u32[]{:S(2)}) collective-permute-start(bf16[2,64,384]{2,1,0:T(8,128)(2,1)S(1)} %get-tuple-element.71), channel_id=1, source_target_pairs={{0,2},{1,3},{2,0},{3,1},{4,6},{5,7},{6,4},{7,5},{8,10},{9,11},{10,... | collective-permute-start | bytes 294920 | tf_op jit(solution)/shard_map/ppermute | solution.py:32
  46.6 0.2 collective-permute-start.23
  46.8 0.3 sum1.1
  47.1 1.9 %collective-permute-start.15 = (bf16[2,64,384]{2,1,0:T(8,128)(2,1)S(1)}, bf16[2,64,384]{2,1,0:T(8,128)(2,1)S(1)}, u32[]{:S(2)}, u32[]{:S(2)}) collective-permute-start(bf16[2,64,384]{2,1,0:T(8,128)(2,1)S(1)} %get-tuple-element.63), channel_id=1, source_target_pairs={{0,1},{1,2},{2,3},{3,0},{4,5},{5,6},{6,7},{7,4},{8,9},{9,10},{10,1... | collective-permute-start | bytes 294920 | tf_op jit(solution)/shard_map/ppermute | solution.py:32
  49.0 0.6 %collective-permute-start.16 = (bf16[2,64,384]{2,1,0:T(8,128)(2,1)S(1)}, bf16[2,64,384]{2,1,0:T(8,128)(2,1)S(1)}, u32[]{:S(2)}, u32[]{:S(2)}) collective-permute-start(bf16[2,64,384]{2,1,0:T(8,128)(2,1)S(1)} %get-tuple-element.64), channel_id=1, source_target_pairs={{0,2},{1,3},{2,0},{3,1},{4,6},{5,7},{6,4},{7,5},{8,10},{9,11},{10,... | collective-permute-start | bytes 294920 | tf_op jit(solution)/shard_map/ppermute | solution.py:32
  49.6 0.1 collective-permute-done.21.refs_1_
  49.8 2.3 %collective-permute-start.17 = (bf16[2,64,384]{2,1,0:T(8,128)(2,1)S(1)}, bf16[2,64,384]{2,1,0:T(8,128)(2,1)S(1)}, u32[]{:S(2)}, u32[]{:S(2)}) collective-permute-start(bf16[2,64,384]{2,1,0:T(8,128)(2,1)S(1)} %get-tuple-element.65), channel_id=1, source_target_pairs={{0,3},{1,0},{2,1},{3,2},{4,7},{5,4},{6,5},{7,6},{8,11},{9,8},{10,9... | collective-permute-start | bytes 294920 | tf_op jit(solution)/shard_map/ppermute | solution.py:32
  52.1 0.9 %copy.16 = bf16[1,1,512,768]{3,2,1,0:T(8,128)(2,1)} copy(bf16[1,1,512,768]{3,2,1,0:T(8,128)(2,1)S(1)} %bitcast.8) | data formatting | bytes 1572864
  53.0 0.9 %copy.17 = bf16[1,1,512,768]{3,2,1,0:T(8,128)(2,1)} copy(bf16[1,1,512,768]{3,2,1,0:T(8,128)(2,1)S(1)} %bitcast.9) | data formatting | bytes 1572864
  53.8 0.8 %join0.1.refs_4_ = bf16[2,64,3072]{2,1,0:T(8,128)(2,1)} custom-call(bf16[2,64,384]{2,1,0:T(8,128)(2,1)S(1)} %get-tuple-element.69.refs_0_, bf16[2,64,384]{2,1,0:T(8,128)(2,1)S(1)} %collective-permute-done.21.refs_1_, bf16[2,64,384]{2,1,0:T(8,128)(2,1)S(1)} %collective-permute-done.22.refs_2_, bf16[2,64,384]{2,1,0:T(8,128)(2,1)S(1)} %collective-permute-done.23.refs_3_), custom_call_target="tpu_custom_call" | custom-call | tf_op jit(solution)/shard_map/join0/pallas_call | solution.py:225
  54.6 3.2 %collective-permute-done.16.refs_2_ = bf16[2,64,384]{2,1,0:T(8,128)(2,1)S(1)} collective-permute-done((bf16[2,64,384]{2,1,0:T(8,128)(2,1)S(1)}, bf16[2,64,384]{2,1,0:T(8,128)(2,1)S(1)}, u32[]{:S(2)}, u32[]{:S(2)}) %collective-permute-start.16) | collective-permute-done | bytes 98336 | tf_op jit(solution)/shard_map/ppermute | solution.py:32
  57.9 0.8 %join1.1 = bf16[2,64,3072]{2,1,0:T(8,128)(2,1)} custom-call(bf16[2,64,384]{2,1,0:T(8,128)(2,1)S(1)} %get-tuple-element.62.refs_0_, bf16[2,64,384]{2,1,0:T(8,128)(2,1)S(1)} %collective-permute-done.15.refs_1_, bf16[2,64,384]{2,1,0:T(8,128)(2,1)S(1)} %collective-permute-done.16.refs_2_, ...), custom_call_target="tpu_custom_call", output_to_operand_aliasing={{}: (4, {})} | custom-call | tf_op jit(solution)/shard_map/join1/pallas_call | solution.py:225
  (24 shorter events, 0.1 us)
Async XLA Ops:
  0.6 10.3 %copy-start.2 = (s32[1,4]{1,0:T(1,128)S(1)}, s32[1,4]{1,0:T(1,128)}, u32[]{:S(2)}) copy-start(s32[1,4]{1,0:T(1,128)} %plan_ref.1) | copy-start | bytes 52
  0.6 10.3 %copy-start.3 = (s32[1,4]{1,0:T(1,128)S(1)}, s32[1,4]{1,0:T(1,128)}, u32[]{:S(2)}) copy-start(s32[1,4]{1,0:T(1,128)} %key_len_ref.1) | copy-start | bytes 52
  0.7 10.3 %copy-start.4 = (s32[1,4]{1,0:T(1,128)S(1)}, s32[1,4]{1,0:T(1,128)}, u32[]{:S(2)}) copy-start(s32[1,4]{1,0:T(1,128)} %query_len_ref.1) | copy-start | bytes 52
  1.8 9.8 %collective-permute-start.5 = (bf16[2,64,384]{2,1,0:T(8,128)(2,1)S(1)}, bf16[2,64,384]{2,1,0:T(8,128)(2,1)S(1)}, u32[]{:S(2)}, u32[]{:S(2)}) collective-permute-start(bf16[2,64,384]{2,1,0:T(8,128)(2,1)S(1)} %get-tuple-element.46), channel_id=1, source_target_pairs={{0,1},{1,2},{2,3},{3,0},{4,5},{5,6},{6,7},{7,4},{8,9},{9,10},{10,1... | collective-permute-start | bytes 294920 | tf_op jit(solution)/shard_map/ppermute | solution.py:32
  4.8 12.1 %collective-permute-start.6 = (bf16[2,64,384]{2,1,0:T(8,128)(2,1)S(1)}, bf16[2,64,384]{2,1,0:T(8,128)(2,1)S(1)}, u32[]{:S(2)}, u32[]{:S(2)}) collective-permute-start(bf16[2,64,384]{2,1,0:T(8,128)(2,1)S(1)} %get-tuple-element.47), channel_id=1, source_target_pairs={{0,2},{1,3},{2,0},{3,1},{4,6},{5,7},{6,4},{7,5},{8,10},{9,11},{10,... | collective-permute-start | bytes 294920 | tf_op jit(solution)/shard_map/ppermute | solution.py:32
  7.4 18.2 %copy-start = (bf16[1,1,512,768]{3,2,1,0:T(8,128)(2,1)S(1)}, bf16[1,1,512,768]{3,2,1,0:T(8,128)(2,1)}, u32[]{:S(2)}) copy-start(bf16[1,1,512,768]{3,2,1,0:T(8,128)(2,1)} %param.7) | copy-start | bytes 2359300
  7.4 18.2 %copy-start.1 = (bf16[1,1,512,768]{3,2,1,0:T(8,128)(2,1)S(1)}, bf16[1,1,512,768]{3,2,1,0:T(8,128)(2,1)}, u32[]{:S(2)}) copy-start(bf16[1,1,512,768]{3,2,1,0:T(8,128)(2,1)} %param.8) | copy-start | bytes 2359300
  7.4 9.5 %collective-permute-start.7 = (bf16[2,64,384]{2,1,0:T(8,128)(2,1)S(1)}, bf16[2,64,384]{2,1,0:T(8,128)(2,1)S(1)}, u32[]{:S(2)}, u32[]{:S(2)}) collective-permute-start(bf16[2,64,384]{2,1,0:T(8,128)(2,1)S(1)} %get-tuple-element.48), channel_id=1, source_target_pairs={{0,3},{1,0},{2,1},{3,2},{4,7},{5,4},{6,5},{7,6},{8,11},{9,8},{10,9... | collective-permute-start | bytes 294920 | tf_op jit(solution)/shard_map/ppermute | solution.py:32
  9.9 10.2 %collective-permute-start = (bf16[2,64,384]{2,1,0:T(8,128)(2,1)S(1)}, bf16[2,64,384]{2,1,0:T(8,128)(2,1)S(1)}, u32[]{:S(2)}, u32[]{:S(2)}) collective-permute-start(bf16[2,64,384]{2,1,0:T(8,128)(2,1)S(1)} %get-tuple-element.39), channel_id=1, source_target_pairs={{0,1},{1,2},{2,3},{3,0},{4,5},{5,6},{6,7},{7,4},{8,9},{9,10},{10,1... | collective-permute-start | bytes 294920 | tf_op jit(solution)/shard_map/ppermute | solution.py:32
  10.6 11.8 %collective-permute-start.1 = (bf16[2,64,384]{2,1,0:T(8,128)(2,1)S(1)}, bf16[2,64,384]{2,1,0:T(8,128)(2,1)S(1)}, u32[]{:S(2)}, u32[]{:S(2)}) collective-permute-start(bf16[2,64,384]{2,1,0:T(8,128)(2,1)S(1)} %get-tuple-element.40), channel_id=1, source_target_pairs={{0,2},{1,3},{2,0},{3,1},{4,6},{5,7},{6,4},{7,5},{8,10},{9,11},{10,... | collective-permute-start | bytes 294920 | tf_op jit(solution)/shard_map/ppermute | solution.py:32
  11.6 10.9 %collective-permute-start.2 = (bf16[2,64,384]{2,1,0:T(8,128)(2,1)S(1)}, bf16[2,64,384]{2,1,0:T(8,128)(2,1)S(1)}, u32[]{:S(2)}, u32[]{:S(2)}) collective-permute-start(bf16[2,64,384]{2,1,0:T(8,128)(2,1)S(1)} %get-tuple-element.41), channel_id=1, source_target_pairs={{0,3},{1,0},{2,1},{3,2},{4,7},{5,4},{6,5},{7,6},{8,11},{9,8},{10,9... | collective-permute-start | bytes 294920 | tf_op jit(solution)/shard_map/ppermute | solution.py:32
  17.0 8.6 %collective-permute-start.8 = (bf16[2,64,384]{2,1,0:T(8,128)(2,1)S(1)}, bf16[2,64,384]{2,1,0:T(8,128)(2,1)S(1)}, u32[]{:S(2)}, u32[]{:S(2)}) collective-permute-start(bf16[2,64,384]{2,1,0:T(8,128)(2,1)S(1)} %get-tuple-element.50), channel_id=1, source_target_pairs={{0,8},{8,0},{16,24},{24,16},{1,9},{9,1},{17,25},{25,17},{2,10},{10... | collective-permute-start | bytes 294920 | tf_op jit(solution)/shard_map/ppermute | solution.py:28
  18.6 7.0 %collective-permute-start.9 = (bf16[2,64,384]{2,1,0:T(8,128)(2,1)S(1)}, bf16[2,64,384]{2,1,0:T(8,128)(2,1)S(1)}, u32[]{:S(2)}, u32[]{:S(2)}) collective-permute-start(bf16[2,64,384]{2,1,0:T(8,128)(2,1)S(1)} %get-tuple-element.51), channel_id=1, source_target_pairs={{0,16},{8,24},{16,0},{24,8},{1,17},{9,25},{17,1},{25,9},{2,18},{10... | collective-permute-start | bytes 294920 | tf_op jit(solution)/shard_map/ppermute | solution.py:28
  20.1 5.5 %collective-permute-start.10 = (bf16[2,64,384]{2,1,0:T(8,128)(2,1)S(1)}, bf16[2,64,384]{2,1,0:T(8,128)(2,1)S(1)}, u32[]{:S(2)}, u32[]{:S(2)}) collective-permute-start(bf16[2,64,384]{2,1,0:T(8,128)(2,1)S(1)} %get-tuple-element.52), channel_id=1, source_target_pairs={{0,24},{8,16},{16,8},{24,0},{1,25},{9,17},{17,9},{25,1},{2,26},{10... | collective-permute-start | bytes 294920 | tf_op jit(solution)/shard_map/ppermute | solution.py:28
  22.5 8.7 %collective-permute-start.3 = (bf16[2,64,384]{2,1,0:T(8,128)(2,1)S(1)}, bf16[2,64,384]{2,1,0:T(8,128)(2,1)S(1)}, u32[]{:S(2)}, u32[]{:S(2)}) collective-permute-start(bf16[2,64,384]{2,1,0:T(8,128)(2,1)S(1)} %get-tuple-element.43), channel_id=1, source_target_pairs={{0,8},{8,0},{16,24},{24,16},{1,9},{9,1},{17,25},{25,17},{2,10},{10... | collective-permute-start | bytes 294920 | tf_op jit(solution)/shard_map/ppermute | solution.py:28
  24.1 7.7 %collective-permute-start.4 = (bf16[2,64,384]{2,1,0:T(8,128)(2,1)S(1)}, bf16[2,64,384]{2,1,0:T(8,128)(2,1)S(1)}, u32[]{:S(2)}, u32[]{:S(2)}) collective-permute-start(bf16[2,64,384]{2,1,0:T(8,128)(2,1)S(1)} %get-tuple-element.44), channel_id=1, source_target_pairs={{0,16},{8,24},{16,0},{24,8},{1,17},{9,25},{17,1},{25,9},{2,18},{10... | collective-permute-start | bytes 294920 | tf_op jit(solution)/shard_map/ppermute | solution.py:28
  27.7 6.7 %collective-permute-start.11 = (bf16[2,64,384]{2,1,0:T(8,128)(2,1)S(1)}, bf16[2,64,384]{2,1,0:T(8,128)(2,1)S(1)}, u32[]{:S(2)}, u32[]{:S(2)}) collective-permute-start(bf16[2,64,384]{2,1,0:T(8,128)(2,1)S(1)} %pick1.3), channel_id=1, source_target_pairs={{0,24},{8,16},{16,8},{24,0},{1,25},{9,17},{17,9},{25,1},{2,26},{10... | collective-permute-start | bytes 294920 | tf_op jit(solution)/shard_map/ppermute | solution.py:28
  28.3 9.2 %collective-permute-start.18 = (bf16[2,64,384]{2,1,0:T(8,128)(2,1)S(1)}, bf16[2,64,384]{2,1,0:T(8,128)(2,1)S(1)}, u32[]{:S(2)}, u32[]{:S(2)}) collective-permute-start(bf16[2,64,384]{2,1,0:T(8,128)(2,1)S(1)} %get-tuple-element.66), channel_id=1, source_target_pairs={{0,8},{8,0},{16,24},{24,16},{1,9},{9,1},{17,25},{25,17},{2,10},{10... | collective-permute-start | bytes 294920 | tf_op jit(solution)/shard_map/ppermute | solution.py:28
  29.8 10.2 %collective-permute-start.19 = (bf16[2,64,384]{2,1,0:T(8,128)(2,1)S(1)}, bf16[2,64,384]{2,1,0:T(8,128)(2,1)S(1)}, u32[]{:S(2)}, u32[]{:S(2)}) collective-permute-start(bf16[2,64,384]{2,1,0:T(8,128)(2,1)S(1)} %get-tuple-element.67), channel_id=1, source_target_pairs={{0,16},{8,24},{16,0},{24,8},{1,17},{9,25},{17,1},{25,9},{2,18},{10... | collective-permute-start | bytes 294920 | tf_op jit(solution)/shard_map/ppermute | solution.py:28
  31.3 8.7 %collective-permute-start.20 = (bf16[2,64,384]{2,1,0:T(8,128)(2,1)S(1)}, bf16[2,64,384]{2,1,0:T(8,128)(2,1)S(1)}, u32[]{:S(2)}, u32[]{:S(2)}) collective-permute-start(bf16[2,64,384]{2,1,0:T(8,128)(2,1)S(1)} %get-tuple-element.68), channel_id=1, source_target_pairs={{0,24},{8,16},{16,8},{24,0},{1,25},{9,17},{17,9},{25,1},{2,26},{10... | collective-permute-start | bytes 294920 | tf_op jit(solution)/shard_map/ppermute | solution.py:28
  36.4 10.2 %collective-permute-start.12 = (bf16[2,64,384]{2,1,0:T(8,128)(2,1)S(1)}, bf16[2,64,384]{2,1,0:T(8,128)(2,1)S(1)}, u32[]{:S(2)}, u32[]{:S(2)}) collective-permute-start(bf16[2,64,384]{2,1,0:T(8,128)(2,1)S(1)} %get-tuple-element.59), channel_id=1, source_target_pairs={{0,8},{8,0},{16,24},{24,16},{1,9},{9,1},{17,25},{25,17},{2,10},{10... | collective-permute-start | bytes 294920 | tf_op jit(solution)/shard_map/ppermute | solution.py:28
  36.9 9.8 %collective-permute-start.13 = (bf16[2,64,384]{2,1,0:T(8,128)(2,1)S(1)}, bf16[2,64,384]{2,1,0:T(8,128)(2,1)S(1)}, u32[]{:S(2)}, u32[]{:S(2)}) collective-permute-start(bf16[2,64,384]{2,1,0:T(8,128)(2,1)S(1)} %get-tuple-element.60), channel_id=1, source_target_pairs={{0,16},{8,24},{16,0},{24,8},{1,17},{9,25},{17,1},{25,9},{2,18},{10... | collective-permute-start | bytes 294920 | tf_op jit(solution)/shard_map/ppermute | solution.py:28
  37.4 9.3 %collective-permute-start.14 = (bf16[2,64,384]{2,1,0:T(8,128)(2,1)S(1)}, bf16[2,64,384]{2,1,0:T(8,128)(2,1)S(1)}, u32[]{:S(2)}, u32[]{:S(2)}) collective-permute-start(bf16[2,64,384]{2,1,0:T(8,128)(2,1)S(1)} %get-tuple-element.61), channel_id=1, source_target_pairs={{0,24},{8,16},{16,8},{24,0},{1,25},{9,17},{17,9},{25,1},{2,26},{10... | collective-permute-start | bytes 294920 | tf_op jit(solution)/shard_map/ppermute | solution.py:28
  40.3 9.5 %collective-permute-start.21 = (bf16[2,64,384]{2,1,0:T(8,128)(2,1)S(1)}, bf16[2,64,384]{2,1,0:T(8,128)(2,1)S(1)}, u32[]{:S(2)}, u32[]{:S(2)}) collective-permute-start(bf16[2,64,384]{2,1,0:T(8,128)(2,1)S(1)} %get-tuple-element.70), channel_id=1, source_target_pairs={{0,1},{1,2},{2,3},{3,0},{4,5},{5,6},{6,7},{7,4},{8,9},{9,10},{10,1... | collective-permute-start | bytes 294920 | tf_op jit(solution)/shard_map/ppermute | solution.py:32
  44.3 9.5 %collective-permute-start.22 = (bf16[2,64,384]{2,1,0:T(8,128)(2,1)S(1)}, bf16[2,64,384]{2,1,0:T(8,128)(2,1)S(1)}, u32[]{:S(2)}, u32[]{:S(2)}) collective-permute-start(bf16[2,64,384]{2,1,0:T(8,128)(2,1)S(1)} %get-tuple-element.71), channel_id=1, source_target_pairs={{0,2},{1,3},{2,0},{3,1},{4,6},{5,7},{6,4},{7,5},{8,10},{9,11},{10,... | collective-permute-start | bytes 294920 | tf_op jit(solution)/shard_map/ppermute | solution.py:32
  46.6 7.3 %collective-permute-start.23 = (bf16[2,64,384]{2,1,0:T(8,128)(2,1)S(1)}, bf16[2,64,384]{2,1,0:T(8,128)(2,1)S(1)}, u32[]{:S(2)}, u32[]{:S(2)}) collective-permute-start(bf16[2,64,384]{2,1,0:T(8,128)(2,1)S(1)} %get-tuple-element.72), channel_id=1, source_target_pairs={{0,3},{1,0},{2,1},{3,2},{4,7},{5,4},{6,5},{7,6},{8,11},{9,8},{10,9... | collective-permute-start | bytes 294920 | tf_op jit(solution)/shard_map/ppermute | solution.py:32
  47.1 7.5 %collective-permute-start.15 = (bf16[2,64,384]{2,1,0:T(8,128)(2,1)S(1)}, bf16[2,64,384]{2,1,0:T(8,128)(2,1)S(1)}, u32[]{:S(2)}, u32[]{:S(2)}) collective-permute-start(bf16[2,64,384]{2,1,0:T(8,128)(2,1)S(1)} %get-tuple-element.63), channel_id=1, source_target_pairs={{0,1},{1,2},{2,3},{3,0},{4,5},{5,6},{6,7},{7,4},{8,9},{9,10},{10,1... | collective-permute-start | bytes 294920 | tf_op jit(solution)/shard_map/ppermute | solution.py:32
  49.0 8.9 %collective-permute-start.16 = (bf16[2,64,384]{2,1,0:T(8,128)(2,1)S(1)}, bf16[2,64,384]{2,1,0:T(8,128)(2,1)S(1)}, u32[]{:S(2)}, u32[]{:S(2)}) collective-permute-start(bf16[2,64,384]{2,1,0:T(8,128)(2,1)S(1)} %get-tuple-element.64), channel_id=1, source_target_pairs={{0,2},{1,3},{2,0},{3,1},{4,6},{5,7},{6,4},{7,5},{8,10},{9,11},{10,... | collective-permute-start | bytes 294920 | tf_op jit(solution)/shard_map/ppermute | solution.py:32
  49.8 8.1 %collective-permute-start.17 = (bf16[2,64,384]{2,1,0:T(8,128)(2,1)S(1)}, bf16[2,64,384]{2,1,0:T(8,128)(2,1)S(1)}, u32[]{:S(2)}, u32[]{:S(2)}) collective-permute-start(bf16[2,64,384]{2,1,0:T(8,128)(2,1)S(1)} %get-tuple-element.65), channel_id=1, source_target_pairs={{0,3},{1,0},{2,1},{3,2},{4,7},{5,4},{6,5},{7,6},{8,11},{9,8},{10,9... | collective-permute-start | bytes 294920 | tf_op jit(solution)/shard_map/ppermute | solution.py:32

commit v4 on v3

--- a/solution.py
+++ b/solution.py
@@ -50,7 +50,7 @@
 
 def split_kernel(tp_count, chunk, width, head_cols, memory_ref, *refs):
     me = lax.axis_index("tp")
-    outs, sem = refs[:-1], refs[-1]
+    outs, sem = refs[-1 - tp_count : -1], refs[-1]
     owners = [ahead(me, step, tp_count) for step in range(tp_count)]
     run_copies([(memory_ref.at[:, :, columns_of(chunk, width, head_cols, o)], out) for o, out in zip(owners, outs)], sem)
 
@@ -156,15 +156,16 @@
     copy_sem = pltpu.SemaphoreType.DMA((tp_count,))
     parts = []
     for chunk in range(chunks):
+        gate = [parts[-1][2]] if parts else []
         split = pl.pallas_call(
             functools.partial(split_kernel, tp_count, chunk, width, head_cols),
             out_shape=[piece] * tp_count,
-            in_specs=[ANY],
+            in_specs=[ANY] * (1 + len(gate)),
             out_specs=[VMEM] * tp_count,
             scratch_shapes=[copy_sem],
             compiler_params=params,
             name=f"split{chunk}",
-        )(memory)
+        )(memory, *gate)
         parts.append([split[0]] + [shift(split[step], step, tp_count) for step in range(1, tp_count)])
     facts = pl.pallas_call(
         functools.partial(facts_kernel, section_count),

time: 58.8 us -> 58.3 us (level)
  waiting for transfers between devices: 10.4 us -> 9.45 us
    ppermute x12, starting transfers between devices: 14.2 us -> 16 us  [swap(): return lax.ppermute(piece, 'section', [(i, i ^ step) for i in range(count)])]
    ppermute x12, starting transfers between devices: 22.3 us -> 20.9 us  [shift(): lax.ppermute(piece, 'tp', [(i, (i + step) % count) for i in range(count)])]
    ppermute x12, waiting for transfers between devices: 2.66 us -> 1.53 us  [swap(): return lax.ppermute(piece, 'section', [(i, i ^ step) for i in range(count)])]
  transfers between devices with their start and end apart: 24 -> 24, of which waited for: 5 -> 7; matrix products, arithmetic and copies ran while one was open for 3% -> 3% of each run, Pallas kernels for 12% -> 13%
where the time goes in v4:
time: 58.3 us; the launch traced here: 58.2 us
  starting transfers between devices  37 us (63%)
  waiting for transfers between devices  9.45 us (16%)
  Pallas kernels  9.18 us (16%)
  local copies, waits for them, and re-layouts  1.78 us (3%)
  between operations  0.79 us (1%)
    ppermute x12, starting transfers between devices, shift(): lax.ppermute(piece, 'tp', [(i, (i + step) % count) for i in range(count)])  20.9 us
    ppermute x12, starting transfers between devices, swap(): return lax.ppermute(piece, 'section', [(i, i ^ step) for i in range(count)])  16 us
    ppermute x12, waiting for transfers between devices, shift(): lax.ppermute(piece, 'tp', [(i, (i + step) % count) for i in range(count)])  7.93 us
    pallas_call x2, Pallas kernels, body(): pl.pallas_call(functools.partial(heads_kernel, section_count, chunk, widt...  4.03 us
    pallas_call x2, Pallas kernels, body(): pl.pallas_call(functools.partial(split_kernel, tp_count, chunk, width, he...  2.16 us
    unnamed x12, local copies, waits for them, and re-layouts  1.78 us
    pallas_call x2, Pallas kernels, body(): pl.pallas_call(functools.partial(join_kernel, tp_count, chunk, width, hea...  1.54 us
    ppermute x12, waiting for transfers between devices, swap(): return lax.ppermute(piece, 'section', [(i, i ^ step) for i in range(count)])  1.53 us
  transfers between devices with their start and end apart: 24, of which 7 were waited for; matrix products, arithmetic and copies ran while one was open for 3% of the time, Pallas kernels for 13%

profile of v4, /device:TPU:0, one launch (start us, length us, event | category | flops | bytes accessed | tf_op | source)
XLA Modules:
  0.0 58.2 jit_solution(15061409359930476155)
XLA Ops:
  0.7 1.1 %split0.1 = (bf16[2,64,384]{2,1,0:T(8,128)(2,1)S(1)}, bf16[2,64,384]{2,1,0:T(8,128)(2,1)S(1)}, bf16[2,64,384]{2,1,0:T(8,128)(2,1)S(1)}, bf16[2,64,384]{2,1,0:T(8,128)(2,1)S(1)}) custom-call(bf16[2,64,3072]{2,1,0:T(8,128)(2,1)} %bitcast.14), custom_call_target="tpu_custom_call" | custom-call | tf_op jit(solution)/shard_map/split0/pallas_call | solution.py:160
  1.8 4.1 %collective-permute-start = (bf16[2,64,384]{2,1,0:T(8,128)(2,1)S(1)}, bf16[2,64,384]{2,1,0:T(8,128)(2,1)S(1)}, u32[]{:S(2)}, u32[]{:S(2)}) collective-permute-start(bf16[2,64,384]{2,1,0:T(8,128)(2,1)S(1)} %get-tuple-element.38), channel_id=1, source_target_pairs={{0,2},{1,3},{2,0},{3,1},{4,6},{5,7},{6,4},{7,5},{8,10},{9,11},{10,... | collective-permute-start | bytes 294920 | tf_op jit(solution)/shard_map/ppermute | solution.py:32
  5.9 1.6 %collective-permute-start.6 = (bf16[2,64,384]{2,1,0:T(8,128)(2,1)S(1)}, bf16[2,64,384]{2,1,0:T(8,128)(2,1)S(1)}, u32[]{:S(2)}, u32[]{:S(2)}) collective-permute-start(bf16[2,64,384]{2,1,0:T(8,128)(2,1)S(1)} %get-tuple-element.47), channel_id=1, source_target_pairs={{0,1},{1,2},{2,3},{3,0},{4,5},{5,6},{6,7},{7,4},{8,9},{9,10},{10,1... | collective-permute-start | bytes 294920 | tf_op jit(solution)/shard_map/ppermute | solution.py:32
  7.4 2.2 %collective-permute-start.7 = (bf16[2,64,384]{2,1,0:T(8,128)(2,1)S(1)}, bf16[2,64,384]{2,1,0:T(8,128)(2,1)S(1)}, u32[]{:S(2)}, u32[]{:S(2)}) collective-permute-start(bf16[2,64,384]{2,1,0:T(8,128)(2,1)S(1)} %get-tuple-element.48), channel_id=1, source_target_pairs={{0,3},{1,0},{2,1},{3,2},{4,7},{5,4},{6,5},{7,6},{8,11},{9,8},{10,9... | collective-permute-start | bytes 294920 | tf_op jit(solution)/shard_map/ppermute | solution.py:32
  9.7 4.1 %collective-permute-done.refs_0_.refs_2_ = bf16[2,64,384]{2,1,0:T(8,128)(2,1)S(1)} collective-permute-done((bf16[2,64,384]{2,1,0:T(8,128)(2,1)S(1)}, bf16[2,64,384]{2,1,0:T(8,128)(2,1)S(1)}, u32[]{:S(2)}, u32[]{:S(2)}) %collective-permute-start) | collective-permute-done | bytes 98336 | tf_op jit(solution)/shard_map/ppermute | solution.py:32
  13.7 1.1 %split1.1 = (bf16[2,64,384]{2,1,0:T(8,128)(2,1)S(1)}, bf16[2,64,384]{2,1,0:T(8,128)(2,1)S(1)}, bf16[2,64,384]{2,1,0:T(8,128)(2,1)S(1)}, bf16[2,64,384]{2,1,0:T(8,128)(2,1)S(1)}) custom-call(bf16[2,64,3072]{2,1,0:T(8,128)(2,1)} %bitcast.15, bf16[2,64,384]{2,1,0:T(8,128)(2,1)S(1)} %collective-permute-done.refs_0_.refs_2_), custom_call_target="tpu_custom_call" | custom-call | tf_op jit(solution)/shard_map/split1/pallas_call | solution.py:160
  14.8 0.1 collective-permute-start.1
  14.9 0.6 facts.1.facts_ref
  15.5 3.4 %collective-permute-start.2 = (bf16[2,64,384]{2,1,0:T(8,128)(2,1)S(1)}, bf16[2,64,384]{2,1,0:T(8,128)(2,1)S(1)}, u32[]{:S(2)}, u32[]{:S(2)}) collective-permute-start(bf16[2,64,384]{2,1,0:T(8,128)(2,1)S(1)} %get-tuple-element.41), channel_id=1, source_target_pairs={{0,2},{1,3},{2,0},{3,1},{4,6},{5,7},{6,4},{7,5},{8,10},{9,11},{10,... | collective-permute-start | bytes 294920 | tf_op jit(solution)/shard_map/ppermute | solution.py:32
  18.8 0.6 collective-permute-start.3
  19.4 0.1 pick0.1
  19.5 1.8 %collective-permute-start.8 = (bf16[2,64,384]{2,1,0:T(8,128)(2,1)S(1)}, bf16[2,64,384]{2,1,0:T(8,128)(2,1)S(1)}, u32[]{:S(2)}, u32[]{:S(2)}) collective-permute-start(bf16[2,64,384]{2,1,0:T(8,128)(2,1)S(1)} %get-tuple-element.50), channel_id=1, source_target_pairs={{0,8},{8,0},{16,24},{24,16},{1,9},{9,1},{17,25},{25,17},{2,10},{10... | collective-permute-start | bytes 294920 | tf_op jit(solution)/shard_map/ppermute | solution.py:28
  21.3 1.5 %collective-permute-start.9 = (bf16[2,64,384]{2,1,0:T(8,128)(2,1)S(1)}, bf16[2,64,384]{2,1,0:T(8,128)(2,1)S(1)}, u32[]{:S(2)}, u32[]{:S(2)}) collective-permute-start(bf16[2,64,384]{2,1,0:T(8,128)(2,1)S(1)} %get-tuple-element.51), channel_id=1, source_target_pairs={{0,16},{8,24},{16,0},{24,8},{1,17},{9,25},{17,1},{25,9},{2,18},{10... | collective-permute-start | bytes 294920 | tf_op jit(solution)/shard_map/ppermute | solution.py:28
  22.8 0.0 collective-permute-done.1.refs_1_
  22.8 1.3 %collective-permute-start.10 = (bf16[2,64,384]{2,1,0:T(8,128)(2,1)S(1)}, bf16[2,64,384]{2,1,0:T(8,128)(2,1)S(1)}, u32[]{:S(2)}, u32[]{:S(2)}) collective-permute-start(bf16[2,64,384]{2,1,0:T(8,128)(2,1)S(1)} %get-tuple-element.52), channel_id=1, source_target_pairs={{0,24},{8,16},{16,8},{24,0},{1,25},{9,17},{17,9},{25,1},{2,26},{10... | collective-permute-start | bytes 294920 | tf_op jit(solution)/shard_map/ppermute | solution.py:28
  24.1 0.4 collective-permute-done.2.refs_2_
  24.5 0.0 collective-permute-done.3.refs_3_
  24.5 0.1 pick1.2
  24.6 1.5 %collective-permute-start.4 = (bf16[2,64,384]{2,1,0:T(8,128)(2,1)S(1)}, bf16[2,64,384]{2,1,0:T(8,128)(2,1)S(1)}, u32[]{:S(2)}, u32[]{:S(2)}) collective-permute-start(bf16[2,64,384]{2,1,0:T(8,128)(2,1)S(1)} %get-tuple-element.44), channel_id=1, source_target_pairs={{0,8},{8,0},{16,24},{24,16},{1,9},{9,1},{17,25},{25,17},{2,10},{10... | collective-permute-start | bytes 294920 | tf_op jit(solution)/shard_map/ppermute | solution.py:28
  26.1 1.5 %collective-permute-start.5 = (bf16[2,64,384]{2,1,0:T(8,128)(2,1)S(1)}, bf16[2,64,384]{2,1,0:T(8,128)(2,1)S(1)}, u32[]{:S(2)}, u32[]{:S(2)}) collective-permute-start(bf16[2,64,384]{2,1,0:T(8,128)(2,1)S(1)} %get-tuple-element.45), channel_id=1, source_target_pairs={{0,16},{8,24},{16,0},{24,8},{1,17},{9,25},{17,1},{25,9},{2,18},{10... | collective-permute-start | bytes 294920 | tf_op jit(solution)/shard_map/ppermute | solution.py:28
  27.6 0.0 collective-permute-done.8.refs_1_
  27.6 0.0 collective-permute-done.9.refs_2_
  27.7 0.8 %collective-permute-done.10.refs_3_ = bf16[2,64,384]{2,1,0:T(8,128)(2,1)S(1)} collective-permute-done((bf16[2,64,384]{2,1,0:T(8,128)(2,1)S(1)}, bf16[2,64,384]{2,1,0:T(8,128)(2,1)S(1)}, u32[]{:S(2)}, u32[]{:S(2)}) %collective-permute-start.10) | collective-permute-done | bytes 98336 | tf_op jit(solution)/shard_map/ppermute | solution.py:28
  28.5 2.0 %heads0.1 = (bf16[512,768]{1,0:T(8,128)(2,1)S(1)}, bf16[512,768]{1,0:T(8,128)(2,1)S(1)}, bf16[2,64,384]{2,1,0:T(8,128)(2,1)S(1)}, bf16[2,64,384]{2,1,0:T(8,128)(...) custom-call(s32[6]{0:T(128)S(4)} %facts.1.facts_ref, bf16[512,768]{1,0:T(8,128)(2,1)S(1)} %bitcast.10, ...), custom_call_target="tpu_custom_call" | custom-call | flops 603979776 | bytes 8388608 | tf_op jit(solution)/shard_map/heads0/pallas_call | solution.py:199
  30.5 1.4 %collective-permute-start.11 = (bf16[2,64,384]{2,1,0:T(8,128)(2,1)S(1)}, bf16[2,64,384]{2,1,0:T(8,128)(2,1)S(1)}, u32[]{:S(2)}, u32[]{:S(2)}) collective-permute-start(bf16[2,64,384]{2,1,0:T(8,128)(2,1)S(1)} %pick1.3), channel_id=1, source_target_pairs={{0,24},{8,16},{16,8},{24,0},{1,25},{9,17},{17,9},{25,1},{2,26},{10... | collective-permute-start | bytes 294920 | tf_op jit(solution)/shard_map/ppermute | solution.py:28
  31.9 0.6 %collective-permute-start.18 = (bf16[2,64,384]{2,1,0:T(8,128)(2,1)S(1)}, bf16[2,64,384]{2,1,0:T(8,128)(2,1)S(1)}, u32[]{:S(2)}, u32[]{:S(2)}) collective-permute-start(bf16[2,64,384]{2,1,0:T(8,128)(2,1)S(1)} %get-tuple-element.66), channel_id=1, source_target_pairs={{0,8},{8,0},{16,24},{24,16},{1,9},{9,1},{17,25},{25,17},{2,10},{10... | collective-permute-start | bytes 294920 | tf_op jit(solution)/shard_map/ppermute | solution.py:28
  32.6 1.5 %collective-permute-start.19 = (bf16[2,64,384]{2,1,0:T(8,128)(2,1)S(1)}, bf16[2,64,384]{2,1,0:T(8,128)(2,1)S(1)}, u32[]{:S(2)}, u32[]{:S(2)}) collective-permute-start(bf16[2,64,384]{2,1,0:T(8,128)(2,1)S(1)} %get-tuple-element.67), channel_id=1, source_target_pairs={{0,16},{8,24},{16,0},{24,8},{1,17},{9,25},{17,1},{25,9},{2,18},{10... | collective-permute-start | bytes 294920 | tf_op jit(solution)/shard_map/ppermute | solution.py:28
  34.1 1.3 %collective-permute-start.20 = (bf16[2,64,384]{2,1,0:T(8,128)(2,1)S(1)}, bf16[2,64,384]{2,1,0:T(8,128)(2,1)S(1)}, u32[]{:S(2)}, u32[]{:S(2)}) collective-permute-start(bf16[2,64,384]{2,1,0:T(8,128)(2,1)S(1)} %get-tuple-element.68), channel_id=1, source_target_pairs={{0,24},{8,16},{16,8},{24,0},{1,25},{9,17},{17,9},{25,1},{2,26},{10... | collective-permute-start | bytes 294920 | tf_op jit(solution)/shard_map/ppermute | solution.py:28
  35.4 0.7 %collective-permute-done.11.refs_3_ = bf16[2,64,384]{2,1,0:T(8,128)(2,1)S(1)} collective-permute-done((bf16[2,64,384]{2,1,0:T(8,128)(2,1)S(1)}, bf16[2,64,384]{2,1,0:T(8,128)(2,1)S(1)}, u32[]{:S(2)}, u32[]{:S(2)}) %collective-permute-start.11) | collective-permute-done | bytes 98336 | tf_op jit(solution)/shard_map/ppermute | solution.py:28
  36.1 2.0 %heads1.1 = (bf16[512,768]{1,0:T(8,128)(2,1)S(1)}, bf16[512,768]{1,0:T(8,128)(2,1)S(1)}, bf16[2,64,384]{2,1,0:T(8,128)(2,1)S(1)}, bf16[2,64,384]{2,1,0:T(8,128)(...) custom-call(s32[6]{0:T(128)S(4)} %facts.1.facts_ref, ...), custom_call_target="tpu_custom_call", output_to_operand_aliasing={{0}: (7, {}), {1}: (8, {})} | custom-call | flops 603979776 | bytes 8388608 | tf_op jit(solution)/shard_map/heads1/pallas_call | solution.py:199
  38.1 1.4 %collective-permute-start.12 = (bf16[2,64,384]{2,1,0:T(8,128)(2,1)S(1)}, bf16[2,64,384]{2,1,0:T(8,128)(2,1)S(1)}, u32[]{:S(2)}, u32[]{:S(2)}) collective-permute-start(bf16[2,64,384]{2,1,0:T(8,128)(2,1)S(1)} %get-tuple-element.59), channel_id=1, source_target_pairs={{0,8},{8,0},{16,24},{24,16},{1,9},{9,1},{17,25},{25,17},{2,10},{10... | collective-permute-start | bytes 294920 | tf_op jit(solution)/shard_map/ppermute | solution.py:28
  39.6 0.5 collective-permute-start.13
  40.1 1.6 %collective-permute-start.14 = (bf16[2,64,384]{2,1,0:T(8,128)(2,1)S(1)}, bf16[2,64,384]{2,1,0:T(8,128)(2,1)S(1)}, u32[]{:S(2)}, u32[]{:S(2)}) collective-permute-start(bf16[2,64,384]{2,1,0:T(8,128)(2,1)S(1)} %get-tuple-element.61), channel_id=1, source_target_pairs={{0,24},{8,16},{16,8},{24,0},{1,25},{9,17},{17,9},{25,1},{2,26},{10... | collective-permute-start | bytes 294920 | tf_op jit(solution)/shard_map/ppermute | solution.py:28
  41.7 0.3 sum0.1
  42.0 2.3 %collective-permute-start.21 = (bf16[2,64,384]{2,1,0:T(8,128)(2,1)S(1)}, bf16[2,64,384]{2,1,0:T(8,128)(2,1)S(1)}, u32[]{:S(2)}, u32[]{:S(2)}) collective-permute-start(bf16[2,64,384]{2,1,0:T(8,128)(2,1)S(1)} %get-tuple-element.70), channel_id=1, source_target_pairs={{0,1},{1,2},{2,3},{3,0},{4,5},{5,6},{6,7},{7,4},{8,9},{9,10},{10,1... | collective-permute-start | bytes 294920 | tf_op jit(solution)/shard_map/ppermute | solution.py:32
  44.3 0.2 collective-permute-start.22
  44.6 2.7 %collective-permute-start.23 = (bf16[2,64,384]{2,1,0:T(8,128)(2,1)S(1)}, bf16[2,64,384]{2,1,0:T(8,128)(2,1)S(1)}, u32[]{:S(2)}, u32[]{:S(2)}) collective-permute-start(bf16[2,64,384]{2,1,0:T(8,128)(2,1)S(1)} %get-tuple-element.72), channel_id=1, source_target_pairs={{0,3},{1,0},{2,1},{3,2},{4,7},{5,4},{6,5},{7,6},{8,11},{9,8},{10,9... | collective-permute-start | bytes 294920 | tf_op jit(solution)/shard_map/ppermute | solution.py:32
  47.2 0.3 sum1.1
  47.6 0.2 collective-permute-start.15
  47.8 1.8 %collective-permute-start.16 = (bf16[2,64,384]{2,1,0:T(8,128)(2,1)S(1)}, bf16[2,64,384]{2,1,0:T(8,128)(2,1)S(1)}, u32[]{:S(2)}, u32[]{:S(2)}) collective-permute-start(bf16[2,64,384]{2,1,0:T(8,128)(2,1)S(1)} %get-tuple-element.64), channel_id=1, source_target_pairs={{0,2},{1,3},{2,0},{3,1},{4,6},{5,7},{6,4},{7,5},{8,10},{9,11},{10,... | collective-permute-start | bytes 294920 | tf_op jit(solution)/shard_map/ppermute | solution.py:32
  49.6 0.1 collective-permute-done.21.refs_1_
  49.7 1.7 %collective-permute-start.17 = (bf16[2,64,384]{2,1,0:T(8,128)(2,1)S(1)}, bf16[2,64,384]{2,1,0:T(8,128)(2,1)S(1)}, u32[]{:S(2)}, u32[]{:S(2)}) collective-permute-start(bf16[2,64,384]{2,1,0:T(8,128)(2,1)S(1)} %get-tuple-element.65), channel_id=1, source_target_pairs={{0,3},{1,0},{2,1},{3,2},{4,7},{5,4},{6,5},{7,6},{8,11},{9,8},{10,9... | collective-permute-start | bytes 294920 | tf_op jit(solution)/shard_map/ppermute | solution.py:32
  51.4 0.9 %copy.16 = bf16[1,1,512,768]{3,2,1,0:T(8,128)(2,1)} copy(bf16[1,1,512,768]{3,2,1,0:T(8,128)(2,1)S(1)} %bitcast.8) | data formatting | bytes 1572864
  52.3 0.9 %copy.17 = bf16[1,1,512,768]{3,2,1,0:T(8,128)(2,1)} copy(bf16[1,1,512,768]{3,2,1,0:T(8,128)(2,1)S(1)} %bitcast.9) | data formatting | bytes 1572864
  53.2 0.8 %join0.1.refs_4_ = bf16[2,64,3072]{2,1,0:T(8,128)(2,1)} custom-call(bf16[2,64,384]{2,1,0:T(8,128)(2,1)S(1)} %get-tuple-element.69.refs_0_, bf16[2,64,384]{2,1,0:T(8,128)(2,1)S(1)} %collective-permute-done.21.refs_1_, bf16[2,64,384]{2,1,0:T(8,128)(2,1)S(1)} %collective-permute-done.22.refs_2_, bf16[2,64,384]{2,1,0:T(8,128)(2,1)S(1)} %collective-permute-done.23.refs_3_), custom_call_target="tpu_custom_call" | custom-call | tf_op jit(solution)/shard_map/join0/pallas_call | solution.py:226
  54.0 0.2 collective-permute-done.15.refs_1_
  54.2 3.2 %collective-permute-done.16.refs_2_ = bf16[2,64,384]{2,1,0:T(8,128)(2,1)S(1)} collective-permute-done((bf16[2,64,384]{2,1,0:T(8,128)(2,1)S(1)}, bf16[2,64,384]{2,1,0:T(8,128)(2,1)S(1)}, u32[]{:S(2)}, u32[]{:S(2)}) %collective-permute-start.16) | collective-permute-done | bytes 98336 | tf_op jit(solution)/shard_map/ppermute | solution.py:32
  57.4 0.8 %join1.1 = bf16[2,64,3072]{2,1,0:T(8,128)(2,1)} custom-call(bf16[2,64,384]{2,1,0:T(8,128)(2,1)S(1)} %get-tuple-element.62.refs_0_, bf16[2,64,384]{2,1,0:T(8,128)(2,1)S(1)} %collective-permute-done.15.refs_1_, bf16[2,64,384]{2,1,0:T(8,128)(2,1)S(1)} %collective-permute-done.16.refs_2_, ...), custom_call_target="tpu_custom_call", output_to_operand_aliasing={{}: (4, {})} | custom-call | tf_op jit(solution)/shard_map/join1/pallas_call | solution.py:226
  (24 shorter events, 0.1 us)
Async XLA Ops:
  0.6 14.3 %copy-start.2 = (s32[1,4]{1,0:T(1,128)S(1)}, s32[1,4]{1,0:T(1,128)}, u32[]{:S(2)}) copy-start(s32[1,4]{1,0:T(1,128)} %plan_ref.1) | copy-start | bytes 52
  0.6 14.3 %copy-start.3 = (s32[1,4]{1,0:T(1,128)S(1)}, s32[1,4]{1,0:T(1,128)}, u32[]{:S(2)}) copy-start(s32[1,4]{1,0:T(1,128)} %key_len_ref.1) | copy-start | bytes 52
  0.7 14.3 %copy-start.4 = (s32[1,4]{1,0:T(1,128)S(1)}, s32[1,4]{1,0:T(1,128)}, u32[]{:S(2)}) copy-start(s32[1,4]{1,0:T(1,128)} %query_len_ref.1) | copy-start | bytes 52
  1.8 12.0 %collective-permute-start = (bf16[2,64,384]{2,1,0:T(8,128)(2,1)S(1)}, bf16[2,64,384]{2,1,0:T(8,128)(2,1)S(1)}, u32[]{:S(2)}, u32[]{:S(2)}) collective-permute-start(bf16[2,64,384]{2,1,0:T(8,128)(2,1)S(1)} %get-tuple-element.38), channel_id=1, source_target_pairs={{0,2},{1,3},{2,0},{3,1},{4,6},{5,7},{6,4},{7,5},{8,10},{9,11},{10,... | collective-permute-start | bytes 294920 | tf_op jit(solution)/shard_map/ppermute | solution.py:32
  5.9 13.6 %collective-permute-start.6 = (bf16[2,64,384]{2,1,0:T(8,128)(2,1)S(1)}, bf16[2,64,384]{2,1,0:T(8,128)(2,1)S(1)}, u32[]{:S(2)}, u32[]{:S(2)}) collective-permute-start(bf16[2,64,384]{2,1,0:T(8,128)(2,1)S(1)} %get-tuple-element.47), channel_id=1, source_target_pairs={{0,1},{1,2},{2,3},{3,0},{4,5},{5,6},{6,7},{7,4},{8,9},{9,10},{10,1... | collective-permute-start | bytes 294920 | tf_op jit(solution)/shard_map/ppermute | solution.py:32
  7.4 21.0 %copy-start = (bf16[1,1,512,768]{3,2,1,0:T(8,128)(2,1)S(1)}, bf16[1,1,512,768]{3,2,1,0:T(8,128)(2,1)}, u32[]{:S(2)}) copy-start(bf16[1,1,512,768]{3,2,1,0:T(8,128)(2,1)} %param.7) | copy-start | bytes 2359300
  7.4 21.0 %copy-start.1 = (bf16[1,1,512,768]{3,2,1,0:T(8,128)(2,1)S(1)}, bf16[1,1,512,768]{3,2,1,0:T(8,128)(2,1)}, u32[]{:S(2)}) copy-start(bf16[1,1,512,768]{3,2,1,0:T(8,128)(2,1)} %param.8) | copy-start | bytes 2359300
  7.4 12.0 %collective-permute-start.7 = (bf16[2,64,384]{2,1,0:T(8,128)(2,1)S(1)}, bf16[2,64,384]{2,1,0:T(8,128)(2,1)S(1)}, u32[]{:S(2)}, u32[]{:S(2)}) collective-permute-start(bf16[2,64,384]{2,1,0:T(8,128)(2,1)S(1)} %get-tuple-element.48), channel_id=1, source_target_pairs={{0,3},{1,0},{2,1},{3,2},{4,7},{5,4},{6,5},{7,6},{8,11},{9,8},{10,9... | collective-permute-start | bytes 294920 | tf_op jit(solution)/shard_map/ppermute | solution.py:32
  14.8 8.0 %collective-permute-start.1 = (bf16[2,64,384]{2,1,0:T(8,128)(2,1)S(1)}, bf16[2,64,384]{2,1,0:T(8,128)(2,1)S(1)}, u32[]{:S(2)}, u32[]{:S(2)}) collective-permute-start(bf16[2,64,384]{2,1,0:T(8,128)(2,1)S(1)} %get-tuple-element.40), channel_id=1, source_target_pairs={{0,1},{1,2},{2,3},{3,0},{4,5},{5,6},{6,7},{7,4},{8,9},{9,10},{10,1... | collective-permute-start | bytes 294920 | tf_op jit(solution)/shard_map/ppermute | solution.py:32
  15.5 9.0 %collective-permute-start.2 = (bf16[2,64,384]{2,1,0:T(8,128)(2,1)S(1)}, bf16[2,64,384]{2,1,0:T(8,128)(2,1)S(1)}, u32[]{:S(2)}, u32[]{:S(2)}) collective-permute-start(bf16[2,64,384]{2,1,0:T(8,128)(2,1)S(1)} %get-tuple-element.41), channel_id=1, source_target_pairs={{0,2},{1,3},{2,0},{3,1},{4,6},{5,7},{6,4},{7,5},{8,10},{9,11},{10,... | collective-permute-start | bytes 294920 | tf_op jit(solution)/shard_map/ppermute | solution.py:32
  18.8 5.7 %collective-permute-start.3 = (bf16[2,64,384]{2,1,0:T(8,128)(2,1)S(1)}, bf16[2,64,384]{2,1,0:T(8,128)(2,1)S(1)}, u32[]{:S(2)}, u32[]{:S(2)}) collective-permute-start(bf16[2,64,384]{2,1,0:T(8,128)(2,1)S(1)} %get-tuple-element.42), channel_id=1, source_target_pairs={{0,3},{1,0},{2,1},{3,2},{4,7},{5,4},{6,5},{7,6},{8,11},{9,8},{10,9... | collective-permute-start | bytes 294920 | tf_op jit(solution)/shard_map/ppermute | solution.py:32
  19.5 8.1 %collective-permute-start.8 = (bf16[2,64,384]{2,1,0:T(8,128)(2,1)S(1)}, bf16[2,64,384]{2,1,0:T(8,128)(2,1)S(1)}, u32[]{:S(2)}, u32[]{:S(2)}) collective-permute-start(bf16[2,64,384]{2,1,0:T(8,128)(2,1)S(1)} %get-tuple-element.50), channel_id=1, source_target_pairs={{0,8},{8,0},{16,24},{24,16},{1,9},{9,1},{17,25},{25,17},{2,10},{10... | collective-permute-start | bytes 294920 | tf_op jit(solution)/shard_map/ppermute | solution.py:28
  21.3 6.3 %collective-permute-start.9 = (bf16[2,64,384]{2,1,0:T(8,128)(2,1)S(1)}, bf16[2,64,384]{2,1,0:T(8,128)(2,1)S(1)}, u32[]{:S(2)}, u32[]{:S(2)}) collective-permute-start(bf16[2,64,384]{2,1,0:T(8,128)(2,1)S(1)} %get-tuple-element.51), channel_id=1, source_target_pairs={{0,16},{8,24},{16,0},{24,8},{1,17},{9,25},{17,1},{25,9},{2,18},{10... | collective-permute-start | bytes 294920 | tf_op jit(solution)/shard_map/ppermute | solution.py:28
  22.8 5.6 %collective-permute-start.10 = (bf16[2,64,384]{2,1,0:T(8,128)(2,1)S(1)}, bf16[2,64,384]{2,1,0:T(8,128)(2,1)S(1)}, u32[]{:S(2)}, u32[]{:S(2)}) collective-permute-start(bf16[2,64,384]{2,1,0:T(8,128)(2,1)S(1)} %get-tuple-element.52), channel_id=1, source_target_pairs={{0,24},{8,16},{16,8},{24,0},{1,25},{9,17},{17,9},{25,1},{2,26},{10... | collective-permute-start | bytes 294920 | tf_op jit(solution)/shard_map/ppermute | solution.py:28
  24.6 9.5 %collective-permute-start.4 = (bf16[2,64,384]{2,1,0:T(8,128)(2,1)S(1)}, bf16[2,64,384]{2,1,0:T(8,128)(2,1)S(1)}, u32[]{:S(2)}, u32[]{:S(2)}) collective-permute-start(bf16[2,64,384]{2,1,0:T(8,128)(2,1)S(1)} %get-tuple-element.44), channel_id=1, source_target_pairs={{0,8},{8,0},{16,24},{24,16},{1,9},{9,1},{17,25},{25,17},{2,10},{10... | collective-permute-start | bytes 294920 | tf_op jit(solution)/shard_map/ppermute | solution.py:28
  26.1 9.3 %collective-permute-start.5 = (bf16[2,64,384]{2,1,0:T(8,128)(2,1)S(1)}, bf16[2,64,384]{2,1,0:T(8,128)(2,1)S(1)}, u32[]{:S(2)}, u32[]{:S(2)}) collective-permute-start(bf16[2,64,384]{2,1,0:T(8,128)(2,1)S(1)} %get-tuple-element.45), channel_id=1, source_target_pairs={{0,16},{8,24},{16,0},{24,8},{1,17},{9,25},{17,1},{25,9},{2,18},{10... | collective-permute-start | bytes 294920 | tf_op jit(solution)/shard_map/ppermute | solution.py:28
  30.5 5.6 %collective-permute-start.11 = (bf16[2,64,384]{2,1,0:T(8,128)(2,1)S(1)}, bf16[2,64,384]{2,1,0:T(8,128)(2,1)S(1)}, u32[]{:S(2)}, u32[]{:S(2)}) collective-permute-start(bf16[2,64,384]{2,1,0:T(8,128)(2,1)S(1)} %pick1.3), channel_id=1, source_target_pairs={{0,24},{8,16},{16,8},{24,0},{1,25},{9,17},{17,9},{25,1},{2,26},{10... | collective-permute-start | bytes 294920 | tf_op jit(solution)/shard_map/ppermute | solution.py:28
  31.9 8.2 %collective-permute-start.18 = (bf16[2,64,384]{2,1,0:T(8,128)(2,1)S(1)}, bf16[2,64,384]{2,1,0:T(8,128)(2,1)S(1)}, u32[]{:S(2)}, u32[]{:S(2)}) collective-permute-start(bf16[2,64,384]{2,1,0:T(8,128)(2,1)S(1)} %get-tuple-element.66), channel_id=1, source_target_pairs={{0,8},{8,0},{16,24},{24,16},{1,9},{9,1},{17,25},{25,17},{2,10},{10... | collective-permute-start | bytes 294920 | tf_op jit(solution)/shard_map/ppermute | solution.py:28
  32.6 9.1 %collective-permute-start.19 = (bf16[2,64,384]{2,1,0:T(8,128)(2,1)S(1)}, bf16[2,64,384]{2,1,0:T(8,128)(2,1)S(1)}, u32[]{:S(2)}, u32[]{:S(2)}) collective-permute-start(bf16[2,64,384]{2,1,0:T(8,128)(2,1)S(1)} %get-tuple-element.67), channel_id=1, source_target_pairs={{0,16},{8,24},{16,0},{24,8},{1,17},{9,25},{17,1},{25,9},{2,18},{10... | collective-permute-start | bytes 294920 | tf_op jit(solution)/shard_map/ppermute | solution.py:28
  34.1 7.6 %collective-permute-start.20 = (bf16[2,64,384]{2,1,0:T(8,128)(2,1)S(1)}, bf16[2,64,384]{2,1,0:T(8,128)(2,1)S(1)}, u32[]{:S(2)}, u32[]{:S(2)}) collective-permute-start(bf16[2,64,384]{2,1,0:T(8,128)(2,1)S(1)} %get-tuple-element.68), channel_id=1, source_target_pairs={{0,24},{8,16},{16,8},{24,0},{1,25},{9,17},{17,9},{25,1},{2,26},{10... | collective-permute-start | bytes 294920 | tf_op jit(solution)/shard_map/ppermute | solution.py:28
  38.1 6.4 %collective-permute-start.12 = (bf16[2,64,384]{2,1,0:T(8,128)(2,1)S(1)}, bf16[2,64,384]{2,1,0:T(8,128)(2,1)S(1)}, u32[]{:S(2)}, u32[]{:S(2)}) collective-permute-start(bf16[2,64,384]{2,1,0:T(8,128)(2,1)S(1)} %get-tuple-element.59), channel_id=1, source_target_pairs={{0,8},{8,0},{16,24},{24,16},{1,9},{9,1},{17,25},{25,17},{2,10},{10... | collective-permute-start | bytes 294920 | tf_op jit(solution)/shard_map/ppermute | solution.py:28
  39.6 7.7 %collective-permute-start.13 = (bf16[2,64,384]{2,1,0:T(8,128)(2,1)S(1)}, bf16[2,64,384]{2,1,0:T(8,128)(2,1)S(1)}, u32[]{:S(2)}, u32[]{:S(2)}) collective-permute-start(bf16[2,64,384]{2,1,0:T(8,128)(2,1)S(1)} %get-tuple-element.60), channel_id=1, source_target_pairs={{0,16},{8,24},{16,0},{24,8},{1,17},{9,25},{17,1},{25,9},{2,18},{10... | collective-permute-start | bytes 294920 | tf_op jit(solution)/shard_map/ppermute | solution.py:28
  40.1 7.1 %collective-permute-start.14 = (bf16[2,64,384]{2,1,0:T(8,128)(2,1)S(1)}, bf16[2,64,384]{2,1,0:T(8,128)(2,1)S(1)}, u32[]{:S(2)}, u32[]{:S(2)}) collective-permute-start(bf16[2,64,384]{2,1,0:T(8,128)(2,1)S(1)} %get-tuple-element.61), channel_id=1, source_target_pairs={{0,24},{8,16},{16,8},{24,0},{1,25},{9,17},{17,9},{25,1},{2,26},{10... | collective-permute-start | bytes 294920 | tf_op jit(solution)/shard_map/ppermute | solution.py:28
  42.0 7.7 %collective-permute-start.21 = (bf16[2,64,384]{2,1,0:T(8,128)(2,1)S(1)}, bf16[2,64,384]{2,1,0:T(8,128)(2,1)S(1)}, u32[]{:S(2)}, u32[]{:S(2)}) collective-permute-start(bf16[2,64,384]{2,1,0:T(8,128)(2,1)S(1)} %get-tuple-element.70), channel_id=1, source_target_pairs={{0,1},{1,2},{2,3},{3,0},{4,5},{5,6},{6,7},{7,4},{8,9},{9,10},{10,1... | collective-permute-start | bytes 294920 | tf_op jit(solution)/shard_map/ppermute | solution.py:32
  44.3 8.9 %collective-permute-start.22 = (bf16[2,64,384]{2,1,0:T(8,128)(2,1)S(1)}, bf16[2,64,384]{2,1,0:T(8,128)(2,1)S(1)}, u32[]{:S(2)}, u32[]{:S(2)}) collective-permute-start(bf16[2,64,384]{2,1,0:T(8,128)(2,1)S(1)} %get-tuple-element.71), channel_id=1, source_target_pairs={{0,2},{1,3},{2,0},{3,1},{4,6},{5,7},{6,4},{7,5},{8,10},{9,11},{10,... | collective-permute-start | bytes 294920 | tf_op jit(solution)/shard_map/ppermute | solution.py:32
  44.6 8.6 %collective-permute-start.23 = (bf16[2,64,384]{2,1,0:T(8,128)(2,1)S(1)}, bf16[2,64,384]{2,1,0:T(8,128)(2,1)S(1)}, u32[]{:S(2)}, u32[]{:S(2)}) collective-permute-start(bf16[2,64,384]{2,1,0:T(8,128)(2,1)S(1)} %get-tuple-element.72), channel_id=1, source_target_pairs={{0,3},{1,0},{2,1},{3,2},{4,7},{5,4},{6,5},{7,6},{8,11},{9,8},{10,9... | collective-permute-start | bytes 294920 | tf_op jit(solution)/shard_map/ppermute | solution.py:32
  47.6 6.6 %collective-permute-start.15 = (bf16[2,64,384]{2,1,0:T(8,128)(2,1)S(1)}, bf16[2,64,384]{2,1,0:T(8,128)(2,1)S(1)}, u32[]{:S(2)}, u32[]{:S(2)}) collective-permute-start(bf16[2,64,384]{2,1,0:T(8,128)(2,1)S(1)} %get-tuple-element.63), channel_id=1, source_target_pairs={{0,1},{1,2},{2,3},{3,0},{4,5},{5,6},{6,7},{7,4},{8,9},{9,10},{10,1... | collective-permute-start | bytes 294920 | tf_op jit(solution)/shard_map/ppermute | solution.py:32
  47.8 9.6 %collective-permute-start.16 = (bf16[2,64,384]{2,1,0:T(8,128)(2,1)S(1)}, bf16[2,64,384]{2,1,0:T(8,128)(2,1)S(1)}, u32[]{:S(2)}, u32[]{:S(2)}) collective-permute-start(bf16[2,64,384]{2,1,0:T(8,128)(2,1)S(1)} %get-tuple-element.64), channel_id=1, source_target_pairs={{0,2},{1,3},{2,0},{3,1},{4,6},{5,7},{6,4},{7,5},{8,10},{9,11},{10,... | collective-permute-start | bytes 294920 | tf_op jit(solution)/shard_map/ppermute | solution.py:32
  49.7 7.7 %collective-permute-start.17 = (bf16[2,64,384]{2,1,0:T(8,128)(2,1)S(1)}, bf16[2,64,384]{2,1,0:T(8,128)(2,1)S(1)}, u32[]{:S(2)}, u32[]{:S(2)}) collective-permute-start(bf16[2,64,384]{2,1,0:T(8,128)(2,1)S(1)} %get-tuple-element.65), channel_id=1, source_target_pairs={{0,3},{1,0},{2,1},{3,2},{4,7},{5,4},{6,5},{7,6},{8,11},{9,8},{10,9... | collective-permute-start | bytes 294920 | tf_op jit(solution)/shard_map/ppermute | solution.py:32

commit v5 on v4

--- a/solution.py
+++ b/solution.py
@@ -91,7 +91,9 @@
     nt = (((1,), (1,)), ((), ()))
     tn = (((0,), (0,)), ((), ()))
     none = jnp.zeros((), jnp.bfloat16)
-    for head in range(width // HEAD_DIM):
+    heads = width // HEAD_DIM
+
+    def load(head):
         cols = slice(head * HEAD_DIM, (head + 1) * HEAD_DIM)
         wide = slice(chunk * width + head * HEAD_DIM, chunk * width + (head + 1) * HEAD_DIM)
         query = query_ref[:, wide]
@@ -99,11 +101,18 @@
         keys = jnp.concatenate([block[0, :, cols] for block in blocks], axis=0)
         values = jnp.concatenate([block[1, :, cols] for block in blocks], axis=0)
         scores = lax.dot_general(keys, query, nt, preferred_element_type=jnp.float32) + bias
+        grad_probs = lax.dot_general(values, grad, nt, preferred_element_type=jnp.float32)
+        return cols, wide, query, grad, keys, values, scores, grad_probs
+
+    loaded = load(0)
+    for head in range(heads):
+        cols, wide, query, grad, keys, values, scores, grad_probs = loaded
+        if head + 1 < heads:
+            loaded = load(head + 1)
         top = jnp.max(scores, axis=0, keepdims=True)
         expon = jnp.exp2((scores - top) * scaling_two)
         probs = expon * (1.0 / jnp.sum(expon, axis=0, keepdims=True))
         half = probs.astype(jnp.bfloat16)
-        grad_probs = lax.dot_general(values, grad, nt, preferred_element_type=jnp.float32)
         row_dot = jnp.sum(probs * grad_probs, axis=0, keepdims=True)
         grad_scores = (probs * (grad_probs - row_dot)).astype(jnp.bfloat16)
         grad_value = jnp.dot(half, grad, preferred_element_type=jnp.float32).astype(jnp.bfloat16)
@@ -156,7 +165,7 @@
     copy_sem = pltpu.SemaphoreType.DMA((tp_count,))
     parts = []
     for chunk in range(chunks):
-        gate = [parts[-1][2]] if parts else []
+        gate = [parts[-1][1]] if parts else []
         split = pl.pallas_call(
             functools.partial(split_kernel, tp_count, chunk, width, head_cols),
             out_shape=[piece] * tp_count,

time: 58.3 us -> 57.7 us (0.990)
  waiting for transfers between devices: 9.45 us -> 7.81 us
  starting transfers between devices: 37 us -> 38.5 us
    ppermute x12, waiting for transfers between devices: 7.93 us -> 3.97 us  [shift(): lax.ppermute(piece, 'tp', [(i, (i + step) % count) for i in range(count)])]
    ppermute x12, starting transfers between devices: 20.9 us -> 23.9 us  [shift(): lax.ppermute(piece, 'tp', [(i, (i + step) % count) for i in range(count)])]
    ppermute x12, waiting for transfers between devices: 1.53 us -> 3.84 us  [swap(): return lax.ppermute(piece, 'section', [(i, i ^ step) for i in range(count)])]
    ppermute x12, starting transfers between devices: 16 us -> 14.6 us  [swap(): return lax.ppermute(piece, 'section', [(i, i ^ step) for i in range(count)])]
  transfers between devices with their start and end apart: 24 -> 24, of which waited for: 7 -> 5; matrix products, arithmetic and copies ran while one was open for 3% -> 3% of each run, Pallas kernels for 13% -> 12%
where the time goes in v5:
time: 57.7 us; the launch traced here: 57.5 us
  starting transfers between devices  38.5 us (67%)
  Pallas kernels  8.67 us (15%)
  waiting for transfers between devices  7.81 us (14%)
  local copies, waits for them, and re-layouts  1.78 us (3%)
  between operations  0.78 us (1%)
    ppermute x12, starting transfers between devices, shift(): lax.ppermute(piece, 'tp', [(i, (i + step) % count) for i in range(count)])  23.9 us
    ppermute x12, starting transfers between devices, swap(): return lax.ppermute(piece, 'section', [(i, i ^ step) for i in range(count)])  14.6 us
    ppermute x12, waiting for transfers between devices, shift(): lax.ppermute(piece, 'tp', [(i, (i + step) % count) for i in range(count)])  3.97 us
    ppermute x12, waiting for transfers between devices, swap(): return lax.ppermute(piece, 'section', [(i, i ^ step) for i in range(count)])  3.84 us
    pallas_call x2, Pallas kernels, body(): pl.pallas_call(functools.partial(heads_kernel, section_count, chunk, widt...  3.55 us
    pallas_call x2, Pallas kernels, body(): pl.pallas_call(functools.partial(split_kernel, tp_count, chunk, width, he...  2.16 us
    unnamed x12, local copies, waits for them, and re-layouts  1.78 us
    pallas_call x2, Pallas kernels, body(): pl.pallas_call(functools.partial(join_kernel, tp_count, chunk, width, hea...  1.54 us
  transfers between devices with their start and end apart: 24, of which 5 were waited for; matrix products, arithmetic and copies ran while one was open for 3% of the time, Pallas kernels for 12%

profile of v5, /device:TPU:0, one launch (start us, length us, event | category | flops | bytes accessed | tf_op | source)
XLA Modules:
  0.0 57.5 jit_solution(8855000026063997101)
XLA Ops:
  0.7 1.1 %split0.1 = (bf16[2,64,384]{2,1,0:T(8,128)(2,1)S(1)}, bf16[2,64,384]{2,1,0:T(8,128)(2,1)S(1)}, bf16[2,64,384]{2,1,0:T(8,128)(2,1)S(1)}, bf16[2,64,384]{2,1,0:T(8,128)(2,1)S(1)}) custom-call(bf16[2,64,3072]{2,1,0:T(8,128)(2,1)} %bitcast.14), custom_call_target="tpu_custom_call" | custom-call | tf_op jit(solution)/shard_map/split0/pallas_call | solution.py:169
  1.8 3.1 %collective-permute-start = (bf16[2,64,384]{2,1,0:T(8,128)(2,1)S(1)}, bf16[2,64,384]{2,1,0:T(8,128)(2,1)S(1)}, u32[]{:S(2)}, u32[]{:S(2)}) collective-permute-start(bf16[2,64,384]{2,1,0:T(8,128)(2,1)S(1)} %get-tuple-element.38), channel_id=1, source_target_pairs={{0,1},{1,2},{2,3},{3,0},{4,5},{5,6},{6,7},{7,4},{8,9},{9,10},{10,1... | collective-permute-start | bytes 294920 | tf_op jit(solution)/shard_map/ppermute | solution.py:32
  4.8 2.6 %collective-permute-start.6 = (bf16[2,64,384]{2,1,0:T(8,128)(2,1)S(1)}, bf16[2,64,384]{2,1,0:T(8,128)(2,1)S(1)}, u32[]{:S(2)}, u32[]{:S(2)}) collective-permute-start(bf16[2,64,384]{2,1,0:T(8,128)(2,1)S(1)} %get-tuple-element.47), channel_id=1, source_target_pairs={{0,2},{1,3},{2,0},{3,1},{4,6},{5,7},{6,4},{7,5},{8,10},{9,11},{10,... | collective-permute-start | bytes 294920 | tf_op jit(solution)/shard_map/ppermute | solution.py:32
  7.4 1.3 %collective-permute-start.7 = (bf16[2,64,384]{2,1,0:T(8,128)(2,1)S(1)}, bf16[2,64,384]{2,1,0:T(8,128)(2,1)S(1)}, u32[]{:S(2)}, u32[]{:S(2)}) collective-permute-start(bf16[2,64,384]{2,1,0:T(8,128)(2,1)S(1)} %get-tuple-element.48), channel_id=1, source_target_pairs={{0,3},{1,0},{2,1},{3,2},{4,7},{5,4},{6,5},{7,6},{8,11},{9,8},{10,9... | collective-permute-start | bytes 294920 | tf_op jit(solution)/shard_map/ppermute | solution.py:32
  8.8 1.7 %collective-permute-done.refs_0_.refs_1_ = bf16[2,64,384]{2,1,0:T(8,128)(2,1)S(1)} collective-permute-done((bf16[2,64,384]{2,1,0:T(8,128)(2,1)S(1)}, bf16[2,64,384]{2,1,0:T(8,128)(2,1)S(1)}, u32[]{:S(2)}, u32[]{:S(2)}) %collective-permute-start) | collective-permute-done | bytes 98336 | tf_op jit(solution)/shard_map/ppermute | solution.py:32
  10.5 1.1 %split1.1 = (bf16[2,64,384]{2,1,0:T(8,128)(2,1)S(1)}, bf16[2,64,384]{2,1,0:T(8,128)(2,1)S(1)}, bf16[2,64,384]{2,1,0:T(8,128)(2,1)S(1)}, bf16[2,64,384]{2,1,0:T(8,128)(2,1)S(1)}) custom-call(bf16[2,64,3072]{2,1,0:T(8,128)(2,1)} %bitcast.15, bf16[2,64,384]{2,1,0:T(8,128)(2,1)S(1)} %collective-permute-done.refs_0_.refs_1_), custom_call_target="tpu_custom_call" | custom-call | tf_op jit(solution)/shard_map/split1/pallas_call | solution.py:169
  11.6 3.3 %collective-permute-start.1 = (bf16[2,64,384]{2,1,0:T(8,128)(2,1)S(1)}, bf16[2,64,384]{2,1,0:T(8,128)(2,1)S(1)}, u32[]{:S(2)}, u32[]{:S(2)}) collective-permute-start(bf16[2,64,384]{2,1,0:T(8,128)(2,1)S(1)} %get-tuple-element.40), channel_id=1, source_target_pairs={{0,1},{1,2},{2,3},{3,0},{4,5},{5,6},{6,7},{7,4},{8,9},{9,10},{10,1... | collective-permute-start | bytes 294920 | tf_op jit(solution)/shard_map/ppermute | solution.py:32
  14.9 0.6 facts.1.facts_ref
  15.5 2.1 %collective-permute-start.2 = (bf16[2,64,384]{2,1,0:T(8,128)(2,1)S(1)}, bf16[2,64,384]{2,1,0:T(8,128)(2,1)S(1)}, u32[]{:S(2)}, u32[]{:S(2)}) collective-permute-start(bf16[2,64,384]{2,1,0:T(8,128)(2,1)S(1)} %get-tuple-element.41), channel_id=1, source_target_pairs={{0,2},{1,3},{2,0},{3,1},{4,6},{5,7},{6,4},{7,5},{8,10},{9,11},{10,... | collective-permute-start | bytes 294920 | tf_op jit(solution)/shard_map/ppermute | solution.py:32
  17.5 2.9 %collective-permute-start.3 = (bf16[2,64,384]{2,1,0:T(8,128)(2,1)S(1)}, bf16[2,64,384]{2,1,0:T(8,128)(2,1)S(1)}, u32[]{:S(2)}, u32[]{:S(2)}) collective-permute-start(bf16[2,64,384]{2,1,0:T(8,128)(2,1)S(1)} %get-tuple-element.42), channel_id=1, source_target_pairs={{0,3},{1,0},{2,1},{3,2},{4,7},{5,4},{6,5},{7,6},{8,11},{9,8},{10,9... | collective-permute-start | bytes 294920 | tf_op jit(solution)/shard_map/ppermute | solution.py:32
  20.4 0.0 collective-permute-done.6.refs_2_
  20.4 0.0 collective-permute-done.7.refs_3_
  20.4 0.1 pick0.1
  20.6 1.3 %collective-permute-start.8 = (bf16[2,64,384]{2,1,0:T(8,128)(2,1)S(1)}, bf16[2,64,384]{2,1,0:T(8,128)(2,1)S(1)}, u32[]{:S(2)}, u32[]{:S(2)}) collective-permute-start(bf16[2,64,384]{2,1,0:T(8,128)(2,1)S(1)} %get-tuple-element.50), channel_id=1, source_target_pairs={{0,8},{8,0},{16,24},{24,16},{1,9},{9,1},{17,25},{25,17},{2,10},{10... | collective-permute-start | bytes 294920 | tf_op jit(solution)/shard_map/ppermute | solution.py:28
  21.8 1.5 %collective-permute-start.9 = (bf16[2,64,384]{2,1,0:T(8,128)(2,1)S(1)}, bf16[2,64,384]{2,1,0:T(8,128)(2,1)S(1)}, u32[]{:S(2)}, u32[]{:S(2)}) collective-permute-start(bf16[2,64,384]{2,1,0:T(8,128)(2,1)S(1)} %get-tuple-element.51), channel_id=1, source_target_pairs={{0,16},{8,24},{16,0},{24,8},{1,17},{9,25},{17,1},{25,9},{2,18},{10... | collective-permute-start | bytes 294920 | tf_op jit(solution)/shard_map/ppermute | solution.py:28
  23.4 0.0 collective-permute-done.1.refs_1_
  23.4 0.7 %collective-permute-start.10 = (bf16[2,64,384]{2,1,0:T(8,128)(2,1)S(1)}, bf16[2,64,384]{2,1,0:T(8,128)(2,1)S(1)}, u32[]{:S(2)}, u32[]{:S(2)}) collective-permute-start(bf16[2,64,384]{2,1,0:T(8,128)(2,1)S(1)} %get-tuple-element.52), channel_id=1, source_target_pairs={{0,24},{8,16},{16,8},{24,0},{1,25},{9,17},{17,9},{25,1},{2,26},{10... | collective-permute-start | bytes 294920 | tf_op jit(solution)/shard_map/ppermute | solution.py:28
  24.1 0.0 collective-permute-done.2.refs_2_
  24.1 0.0 collective-permute-done.3.refs_3_
  24.1 0.1 pick1.2
  24.2 1.3 %collective-permute-start.4 = (bf16[2,64,384]{2,1,0:T(8,128)(2,1)S(1)}, bf16[2,64,384]{2,1,0:T(8,128)(2,1)S(1)}, u32[]{:S(2)}, u32[]{:S(2)}) collective-permute-start(bf16[2,64,384]{2,1,0:T(8,128)(2,1)S(1)} %get-tuple-element.44), channel_id=1, source_target_pairs={{0,8},{8,0},{16,24},{24,16},{1,9},{9,1},{17,25},{25,17},{2,10},{10... | collective-permute-start | bytes 294920 | tf_op jit(solution)/shard_map/ppermute | solution.py:28
  25.5 1.5 %collective-permute-start.5 = (bf16[2,64,384]{2,1,0:T(8,128)(2,1)S(1)}, bf16[2,64,384]{2,1,0:T(8,128)(2,1)S(1)}, u32[]{:S(2)}, u32[]{:S(2)}) collective-permute-start(bf16[2,64,384]{2,1,0:T(8,128)(2,1)S(1)} %get-tuple-element.45), channel_id=1, source_target_pairs={{0,16},{8,24},{16,0},{24,8},{1,17},{9,25},{17,1},{25,9},{2,18},{10... | collective-permute-start | bytes 294920 | tf_op jit(solution)/shard_map/ppermute | solution.py:28
  27.0 1.9 %collective-permute-done.10.refs_3_ = bf16[2,64,384]{2,1,0:T(8,128)(2,1)S(1)} collective-permute-done((bf16[2,64,384]{2,1,0:T(8,128)(2,1)S(1)}, bf16[2,64,384]{2,1,0:T(8,128)(2,1)S(1)}, u32[]{:S(2)}, u32[]{:S(2)}) %collective-permute-start.10) | collective-permute-done | bytes 98336 | tf_op jit(solution)/shard_map/ppermute | solution.py:28
  28.9 1.8 %heads0.1 = (bf16[512,768]{1,0:T(8,128)(2,1)S(1)}, bf16[512,768]{1,0:T(8,128)(2,1)S(1)}, bf16[2,64,384]{2,1,0:T(8,128)(2,1)S(1)}, bf16[2,64,384]{2,1,0:T(8,128)(...) custom-call(s32[6]{0:T(128)S(4)} %facts.1.facts_ref, bf16[512,768]{1,0:T(8,128)(2,1)S(1)} %bitcast.10, ...), custom_call_target="tpu_custom_call" | custom-call | flops 603979776 | bytes 8388608 | tf_op jit(solution)/shard_map/heads0/pallas_call | solution.py:208
  30.7 1.2 %collective-permute-start.11 = (bf16[2,64,384]{2,1,0:T(8,128)(2,1)S(1)}, bf16[2,64,384]{2,1,0:T(8,128)(2,1)S(1)}, u32[]{:S(2)}, u32[]{:S(2)}) collective-permute-start(bf16[2,64,384]{2,1,0:T(8,128)(2,1)S(1)} %pick1.3), channel_id=1, source_target_pairs={{0,24},{8,16},{16,8},{24,0},{1,25},{9,17},{17,9},{25,1},{2,26},{10... | collective-permute-start | bytes 294920 | tf_op jit(solution)/shard_map/ppermute | solution.py:28
  31.9 1.1 %collective-permute-start.18 = (bf16[2,64,384]{2,1,0:T(8,128)(2,1)S(1)}, bf16[2,64,384]{2,1,0:T(8,128)(2,1)S(1)}, u32[]{:S(2)}, u32[]{:S(2)}) collective-permute-start(bf16[2,64,384]{2,1,0:T(8,128)(2,1)S(1)} %get-tuple-element.66), channel_id=1, source_target_pairs={{0,8},{8,0},{16,24},{24,16},{1,9},{9,1},{17,25},{25,17},{2,10},{10... | collective-permute-start | bytes 294920 | tf_op jit(solution)/shard_map/ppermute | solution.py:28
  33.0 1.2 %collective-permute-start.19 = (bf16[2,64,384]{2,1,0:T(8,128)(2,1)S(1)}, bf16[2,64,384]{2,1,0:T(8,128)(2,1)S(1)}, u32[]{:S(2)}, u32[]{:S(2)}) collective-permute-start(bf16[2,64,384]{2,1,0:T(8,128)(2,1)S(1)} %get-tuple-element.67), channel_id=1, source_target_pairs={{0,16},{8,24},{16,0},{24,8},{1,17},{9,25},{17,1},{25,9},{2,18},{10... | collective-permute-start | bytes 294920 | tf_op jit(solution)/shard_map/ppermute | solution.py:28
  34.3 0.0 collective-permute-done.4.refs_1_
  34.3 1.1 %collective-permute-start.20 = (bf16[2,64,384]{2,1,0:T(8,128)(2,1)S(1)}, bf16[2,64,384]{2,1,0:T(8,128)(2,1)S(1)}, u32[]{:S(2)}, u32[]{:S(2)}) collective-permute-start(bf16[2,64,384]{2,1,0:T(8,128)(2,1)S(1)} %get-tuple-element.68), channel_id=1, source_target_pairs={{0,24},{8,16},{16,8},{24,0},{1,25},{9,17},{17,9},{25,1},{2,26},{10... | collective-permute-start | bytes 294920 | tf_op jit(solution)/shard_map/ppermute | solution.py:28
  35.4 1.9 %collective-permute-done.11.refs_3_ = bf16[2,64,384]{2,1,0:T(8,128)(2,1)S(1)} collective-permute-done((bf16[2,64,384]{2,1,0:T(8,128)(2,1)S(1)}, bf16[2,64,384]{2,1,0:T(8,128)(2,1)S(1)}, u32[]{:S(2)}, u32[]{:S(2)}) %collective-permute-start.11) | collective-permute-done | bytes 98336 | tf_op jit(solution)/shard_map/ppermute | solution.py:28
  37.4 1.8 %heads1.1 = (bf16[512,768]{1,0:T(8,128)(2,1)S(1)}, bf16[512,768]{1,0:T(8,128)(2,1)S(1)}, bf16[2,64,384]{2,1,0:T(8,128)(2,1)S(1)}, bf16[2,64,384]{2,1,0:T(8,128)(...) custom-call(s32[6]{0:T(128)S(4)} %facts.1.facts_ref, ...), custom_call_target="tpu_custom_call", output_to_operand_aliasing={{0}: (7, {}), {1}: (8, {})} | custom-call | flops 603979776 | bytes 8388608 | tf_op jit(solution)/shard_map/heads1/pallas_call | solution.py:208
  39.1 0.5 collective-permute-start.12
  39.7 1.0 %collective-permute-start.13 = (bf16[2,64,384]{2,1,0:T(8,128)(2,1)S(1)}, bf16[2,64,384]{2,1,0:T(8,128)(2,1)S(1)}, u32[]{:S(2)}, u32[]{:S(2)}) collective-permute-start(bf16[2,64,384]{2,1,0:T(8,128)(2,1)S(1)} %get-tuple-element.60), channel_id=1, source_target_pairs={{0,16},{8,24},{16,0},{24,8},{1,17},{9,25},{17,1},{25,9},{2,18},{10... | collective-permute-start | bytes 294920 | tf_op jit(solution)/shard_map/ppermute | solution.py:28
  40.7 2.0 %collective-permute-start.14 = (bf16[2,64,384]{2,1,0:T(8,128)(2,1)S(1)}, bf16[2,64,384]{2,1,0:T(8,128)(2,1)S(1)}, u32[]{:S(2)}, u32[]{:S(2)}) collective-permute-start(bf16[2,64,384]{2,1,0:T(8,128)(2,1)S(1)} %get-tuple-element.61), channel_id=1, source_target_pairs={{0,24},{8,16},{16,8},{24,0},{1,25},{9,17},{17,9},{25,1},{2,26},{10... | collective-permute-start | bytes 294920 | tf_op jit(solution)/shard_map/ppermute | solution.py:28
  42.7 0.3 sum0.1
  43.0 0.1 collective-permute-start.21
  43.1 1.2 %collective-permute-start.22 = (bf16[2,64,384]{2,1,0:T(8,128)(2,1)S(1)}, bf16[2,64,384]{2,1,0:T(8,128)(2,1)S(1)}, u32[]{:S(2)}, u32[]{:S(2)}) collective-permute-start(bf16[2,64,384]{2,1,0:T(8,128)(2,1)S(1)} %get-tuple-element.71), channel_id=1, source_target_pairs={{0,2},{1,3},{2,0},{3,1},{4,6},{5,7},{6,4},{7,5},{8,10},{9,11},{10,... | collective-permute-start | bytes 294920 | tf_op jit(solution)/shard_map/ppermute | solution.py:32
  44.3 2.6 %collective-permute-start.23 = (bf16[2,64,384]{2,1,0:T(8,128)(2,1)S(1)}, bf16[2,64,384]{2,1,0:T(8,128)(2,1)S(1)}, u32[]{:S(2)}, u32[]{:S(2)}) collective-permute-start(bf16[2,64,384]{2,1,0:T(8,128)(2,1)S(1)} %get-tuple-element.72), channel_id=1, source_target_pairs={{0,3},{1,0},{2,1},{3,2},{4,7},{5,4},{6,5},{7,6},{8,11},{9,8},{10,9... | collective-permute-start | bytes 294920 | tf_op jit(solution)/shard_map/ppermute | solution.py:32
  46.9 0.3 sum1.1
  47.2 0.6 %collective-permute-start.15 = (bf16[2,64,384]{2,1,0:T(8,128)(2,1)S(1)}, bf16[2,64,384]{2,1,0:T(8,128)(2,1)S(1)}, u32[]{:S(2)}, u32[]{:S(2)}) collective-permute-start(bf16[2,64,384]{2,1,0:T(8,128)(2,1)S(1)} %get-tuple-element.63), channel_id=1, source_target_pairs={{0,1},{1,2},{2,3},{3,0},{4,5},{5,6},{6,7},{7,4},{8,9},{9,10},{10,1... | collective-permute-start | bytes 294920 | tf_op jit(solution)/shard_map/ppermute | solution.py:32
  47.9 1.5 %collective-permute-start.16 = (bf16[2,64,384]{2,1,0:T(8,128)(2,1)S(1)}, bf16[2,64,384]{2,1,0:T(8,128)(2,1)S(1)}, u32[]{:S(2)}, u32[]{:S(2)}) collective-permute-start(bf16[2,64,384]{2,1,0:T(8,128)(2,1)S(1)} %get-tuple-element.64), channel_id=1, source_target_pairs={{0,2},{1,3},{2,0},{3,1},{4,6},{5,7},{6,4},{7,5},{8,10},{9,11},{10,... | collective-permute-start | bytes 294920 | tf_op jit(solution)/shard_map/ppermute | solution.py:32
  49.4 0.3 collective-permute-done.21.refs_1_
  49.7 2.6 %collective-permute-start.17 = (bf16[2,64,384]{2,1,0:T(8,128)(2,1)S(1)}, bf16[2,64,384]{2,1,0:T(8,128)(2,1)S(1)}, u32[]{:S(2)}, u32[]{:S(2)}) collective-permute-start(bf16[2,64,384]{2,1,0:T(8,128)(2,1)S(1)} %get-tuple-element.65), channel_id=1, source_target_pairs={{0,3},{1,0},{2,1},{3,2},{4,7},{5,4},{6,5},{7,6},{8,11},{9,8},{10,9... | collective-permute-start | bytes 294920 | tf_op jit(solution)/shard_map/ppermute | solution.py:32
  52.2 0.9 %copy.16 = bf16[1,1,512,768]{3,2,1,0:T(8,128)(2,1)} copy(bf16[1,1,512,768]{3,2,1,0:T(8,128)(2,1)S(1)} %bitcast.8) | data formatting | bytes 1572864
  53.1 0.9 %copy.17 = bf16[1,1,512,768]{3,2,1,0:T(8,128)(2,1)} copy(bf16[1,1,512,768]{3,2,1,0:T(8,128)(2,1)S(1)} %bitcast.9) | data formatting | bytes 1572864
  54.0 0.8 %join0.1.refs_4_ = bf16[2,64,3072]{2,1,0:T(8,128)(2,1)} custom-call(bf16[2,64,384]{2,1,0:T(8,128)(2,1)S(1)} %get-tuple-element.69.refs_0_, bf16[2,64,384]{2,1,0:T(8,128)(2,1)S(1)} %collective-permute-done.21.refs_1_, bf16[2,64,384]{2,1,0:T(8,128)(2,1)S(1)} %collective-permute-done.22.refs_2_, bf16[2,64,384]{2,1,0:T(8,128)(2,1)S(1)} %collective-permute-done.23.refs_3_), custom_call_target="tpu_custom_call" | custom-call | tf_op jit(solution)/shard_map/join0/pallas_call | solution.py:235
  54.8 1.9 %collective-permute-done.16.refs_2_ = bf16[2,64,384]{2,1,0:T(8,128)(2,1)S(1)} collective-permute-done((bf16[2,64,384]{2,1,0:T(8,128)(2,1)S(1)}, bf16[2,64,384]{2,1,0:T(8,128)(2,1)S(1)}, u32[]{:S(2)}, u32[]{:S(2)}) %collective-permute-start.16) | collective-permute-done | bytes 98336 | tf_op jit(solution)/shard_map/ppermute | solution.py:32
  56.7 0.8 %join1.1 = bf16[2,64,3072]{2,1,0:T(8,128)(2,1)} custom-call(bf16[2,64,384]{2,1,0:T(8,128)(2,1)S(1)} %get-tuple-element.62.refs_0_, bf16[2,64,384]{2,1,0:T(8,128)(2,1)S(1)} %collective-permute-done.15.refs_1_, bf16[2,64,384]{2,1,0:T(8,128)(2,1)S(1)} %collective-permute-done.16.refs_2_, ...), custom_call_target="tpu_custom_call", output_to_operand_aliasing={{}: (4, {})} | custom-call | tf_op jit(solution)/shard_map/join1/pallas_call | solution.py:235
  (24 shorter events, 0.1 us)
Async XLA Ops:
  0.6 14.3 %copy-start.2 = (s32[1,4]{1,0:T(1,128)S(1)}, s32[1,4]{1,0:T(1,128)}, u32[]{:S(2)}) copy-start(s32[1,4]{1,0:T(1,128)} %plan_ref.1) | copy-start | bytes 52
  0.6 14.3 %copy-start.3 = (s32[1,4]{1,0:T(1,128)S(1)}, s32[1,4]{1,0:T(1,128)}, u32[]{:S(2)}) copy-start(s32[1,4]{1,0:T(1,128)} %key_len_ref.1) | copy-start | bytes 52
  0.7 14.2 %copy-start.4 = (s32[1,4]{1,0:T(1,128)S(1)}, s32[1,4]{1,0:T(1,128)}, u32[]{:S(2)}) copy-start(s32[1,4]{1,0:T(1,128)} %query_len_ref.1) | copy-start | bytes 52
  1.8 8.8 %collective-permute-start = (bf16[2,64,384]{2,1,0:T(8,128)(2,1)S(1)}, bf16[2,64,384]{2,1,0:T(8,128)(2,1)S(1)}, u32[]{:S(2)}, u32[]{:S(2)}) collective-permute-start(bf16[2,64,384]{2,1,0:T(8,128)(2,1)S(1)} %get-tuple-element.38), channel_id=1, source_target_pairs={{0,1},{1,2},{2,3},{3,0},{4,5},{5,6},{6,7},{7,4},{8,9},{9,10},{10,1... | collective-permute-start | bytes 294920 | tf_op jit(solution)/shard_map/ppermute | solution.py:32
  4.8 15.6 %collective-permute-start.6 = (bf16[2,64,384]{2,1,0:T(8,128)(2,1)S(1)}, bf16[2,64,384]{2,1,0:T(8,128)(2,1)S(1)}, u32[]{:S(2)}, u32[]{:S(2)}) collective-permute-start(bf16[2,64,384]{2,1,0:T(8,128)(2,1)S(1)} %get-tuple-element.47), channel_id=1, source_target_pairs={{0,2},{1,3},{2,0},{3,1},{4,6},{5,7},{6,4},{7,5},{8,10},{9,11},{10,... | collective-permute-start | bytes 294920 | tf_op jit(solution)/shard_map/ppermute | solution.py:32
  7.4 21.5 %copy-start = (bf16[1,1,512,768]{3,2,1,0:T(8,128)(2,1)S(1)}, bf16[1,1,512,768]{3,2,1,0:T(8,128)(2,1)}, u32[]{:S(2)}) copy-start(bf16[1,1,512,768]{3,2,1,0:T(8,128)(2,1)} %param.7) | copy-start | bytes 2359300
  7.4 21.5 %copy-start.1 = (bf16[1,1,512,768]{3,2,1,0:T(8,128)(2,1)S(1)}, bf16[1,1,512,768]{3,2,1,0:T(8,128)(2,1)}, u32[]{:S(2)}) copy-start(bf16[1,1,512,768]{3,2,1,0:T(8,128)(2,1)} %param.8) | copy-start | bytes 2359300
  7.4 13.0 %collective-permute-start.7 = (bf16[2,64,384]{2,1,0:T(8,128)(2,1)S(1)}, bf16[2,64,384]{2,1,0:T(8,128)(2,1)S(1)}, u32[]{:S(2)}, u32[]{:S(2)}) collective-permute-start(bf16[2,64,384]{2,1,0:T(8,128)(2,1)S(1)} %get-tuple-element.48), channel_id=1, source_target_pairs={{0,3},{1,0},{2,1},{3,2},{4,7},{5,4},{6,5},{7,6},{8,11},{9,8},{10,9... | collective-permute-start | bytes 294920 | tf_op jit(solution)/shard_map/ppermute | solution.py:32
  11.6 11.8 %collective-permute-start.1 = (bf16[2,64,384]{2,1,0:T(8,128)(2,1)S(1)}, bf16[2,64,384]{2,1,0:T(8,128)(2,1)S(1)}, u32[]{:S(2)}, u32[]{:S(2)}) collective-permute-start(bf16[2,64,384]{2,1,0:T(8,128)(2,1)S(1)} %get-tuple-element.40), channel_id=1, source_target_pairs={{0,1},{1,2},{2,3},{3,0},{4,5},{5,6},{6,7},{7,4},{8,9},{9,10},{10,1... | collective-permute-start | bytes 294920 | tf_op jit(solution)/shard_map/ppermute | solution.py:32
  15.5 8.6 %collective-permute-start.2 = (bf16[2,64,384]{2,1,0:T(8,128)(2,1)S(1)}, bf16[2,64,384]{2,1,0:T(8,128)(2,1)S(1)}, u32[]{:S(2)}, u32[]{:S(2)}) collective-permute-start(bf16[2,64,384]{2,1,0:T(8,128)(2,1)S(1)} %get-tuple-element.41), channel_id=1, source_target_pairs={{0,2},{1,3},{2,0},{3,1},{4,6},{5,7},{6,4},{7,5},{8,10},{9,11},{10,... | collective-permute-start | bytes 294920 | tf_op jit(solution)/shard_map/ppermute | solution.py:32
  17.5 6.6 %collective-permute-start.3 = (bf16[2,64,384]{2,1,0:T(8,128)(2,1)S(1)}, bf16[2,64,384]{2,1,0:T(8,128)(2,1)S(1)}, u32[]{:S(2)}, u32[]{:S(2)}) collective-permute-start(bf16[2,64,384]{2,1,0:T(8,128)(2,1)S(1)} %get-tuple-element.42), channel_id=1, source_target_pairs={{0,3},{1,0},{2,1},{3,2},{4,7},{5,4},{6,5},{7,6},{8,11},{9,8},{10,9... | collective-permute-start | bytes 294920 | tf_op jit(solution)/shard_map/ppermute | solution.py:32
  20.6 6.5 %collective-permute-start.8 = (bf16[2,64,384]{2,1,0:T(8,128)(2,1)S(1)}, bf16[2,64,384]{2,1,0:T(8,128)(2,1)S(1)}, u32[]{:S(2)}, u32[]{:S(2)}) collective-permute-start(bf16[2,64,384]{2,1,0:T(8,128)(2,1)S(1)} %get-tuple-element.50), channel_id=1, source_target_pairs={{0,8},{8,0},{16,24},{24,16},{1,9},{9,1},{17,25},{25,17},{2,10},{10... | collective-permute-start | bytes 294920 | tf_op jit(solution)/shard_map/ppermute | solution.py:28
  21.8 5.2 %collective-permute-start.9 = (bf16[2,64,384]{2,1,0:T(8,128)(2,1)S(1)}, bf16[2,64,384]{2,1,0:T(8,128)(2,1)S(1)}, u32[]{:S(2)}, u32[]{:S(2)}) collective-permute-start(bf16[2,64,384]{2,1,0:T(8,128)(2,1)S(1)} %get-tuple-element.51), channel_id=1, source_target_pairs={{0,16},{8,24},{16,0},{24,8},{1,17},{9,25},{17,1},{25,9},{2,18},{10... | collective-permute-start | bytes 294920 | tf_op jit(solution)/shard_map/ppermute | solution.py:28
  23.4 5.5 %collective-permute-start.10 = (bf16[2,64,384]{2,1,0:T(8,128)(2,1)S(1)}, bf16[2,64,384]{2,1,0:T(8,128)(2,1)S(1)}, u32[]{:S(2)}, u32[]{:S(2)}) collective-permute-start(bf16[2,64,384]{2,1,0:T(8,128)(2,1)S(1)} %get-tuple-element.52), channel_id=1, source_target_pairs={{0,24},{8,16},{16,8},{24,0},{1,25},{9,17},{17,9},{25,1},{2,26},{10... | collective-permute-start | bytes 294920 | tf_op jit(solution)/shard_map/ppermute | solution.py:28
  24.2 10.1 %collective-permute-start.4 = (bf16[2,64,384]{2,1,0:T(8,128)(2,1)S(1)}, bf16[2,64,384]{2,1,0:T(8,128)(2,1)S(1)}, u32[]{:S(2)}, u32[]{:S(2)}) collective-permute-start(bf16[2,64,384]{2,1,0:T(8,128)(2,1)S(1)} %get-tuple-element.44), channel_id=1, source_target_pairs={{0,8},{8,0},{16,24},{24,16},{1,9},{9,1},{17,25},{25,17},{2,10},{10... | collective-permute-start | bytes 294920 | tf_op jit(solution)/shard_map/ppermute | solution.py:28
  25.5 9.9 %collective-permute-start.5 = (bf16[2,64,384]{2,1,0:T(8,128)(2,1)S(1)}, bf16[2,64,384]{2,1,0:T(8,128)(2,1)S(1)}, u32[]{:S(2)}, u32[]{:S(2)}) collective-permute-start(bf16[2,64,384]{2,1,0:T(8,128)(2,1)S(1)} %get-tuple-element.45), channel_id=1, source_target_pairs={{0,16},{8,24},{16,0},{24,8},{1,17},{9,25},{17,1},{25,9},{2,18},{10... | collective-permute-start | bytes 294920 | tf_op jit(solution)/shard_map/ppermute | solution.py:28
  30.7 6.6 %collective-permute-start.11 = (bf16[2,64,384]{2,1,0:T(8,128)(2,1)S(1)}, bf16[2,64,384]{2,1,0:T(8,128)(2,1)S(1)}, u32[]{:S(2)}, u32[]{:S(2)}) collective-permute-start(bf16[2,64,384]{2,1,0:T(8,128)(2,1)S(1)} %pick1.3), channel_id=1, source_target_pairs={{0,24},{8,16},{16,8},{24,0},{1,25},{9,17},{17,9},{25,1},{2,26},{10... | collective-permute-start | bytes 294920 | tf_op jit(solution)/shard_map/ppermute | solution.py:28
  31.9 8.8 %collective-permute-start.18 = (bf16[2,64,384]{2,1,0:T(8,128)(2,1)S(1)}, bf16[2,64,384]{2,1,0:T(8,128)(2,1)S(1)}, u32[]{:S(2)}, u32[]{:S(2)}) collective-permute-start(bf16[2,64,384]{2,1,0:T(8,128)(2,1)S(1)} %get-tuple-element.66), channel_id=1, source_target_pairs={{0,8},{8,0},{16,24},{24,16},{1,9},{9,1},{17,25},{25,17},{2,10},{10... | collective-permute-start | bytes 294920 | tf_op jit(solution)/shard_map/ppermute | solution.py:28
  33.0 9.7 %collective-permute-start.19 = (bf16[2,64,384]{2,1,0:T(8,128)(2,1)S(1)}, bf16[2,64,384]{2,1,0:T(8,128)(2,1)S(1)}, u32[]{:S(2)}, u32[]{:S(2)}) collective-permute-start(bf16[2,64,384]{2,1,0:T(8,128)(2,1)S(1)} %get-tuple-element.67), channel_id=1, source_target_pairs={{0,16},{8,24},{16,0},{24,8},{1,17},{9,25},{17,1},{25,9},{2,18},{10... | collective-permute-start | bytes 294920 | tf_op jit(solution)/shard_map/ppermute | solution.py:28
  34.3 8.4 %collective-permute-start.20 = (bf16[2,64,384]{2,1,0:T(8,128)(2,1)S(1)}, bf16[2,64,384]{2,1,0:T(8,128)(2,1)S(1)}, u32[]{:S(2)}, u32[]{:S(2)}) collective-permute-start(bf16[2,64,384]{2,1,0:T(8,128)(2,1)S(1)} %get-tuple-element.68), channel_id=1, source_target_pairs={{0,24},{8,16},{16,8},{24,0},{1,25},{9,17},{17,9},{25,1},{2,26},{10... | collective-permute-start | bytes 294920 | tf_op jit(solution)/shard_map/ppermute | solution.py:28
  39.1 5.1 %collective-permute-start.12 = (bf16[2,64,384]{2,1,0:T(8,128)(2,1)S(1)}, bf16[2,64,384]{2,1,0:T(8,128)(2,1)S(1)}, u32[]{:S(2)}, u32[]{:S(2)}) collective-permute-start(bf16[2,64,384]{2,1,0:T(8,128)(2,1)S(1)} %get-tuple-element.59), channel_id=1, source_target_pairs={{0,8},{8,0},{16,24},{24,16},{1,9},{9,1},{17,25},{25,17},{2,10},{10... | collective-permute-start | bytes 294920 | tf_op jit(solution)/shard_map/ppermute | solution.py:28
  39.7 7.2 %collective-permute-start.13 = (bf16[2,64,384]{2,1,0:T(8,128)(2,1)S(1)}, bf16[2,64,384]{2,1,0:T(8,128)(2,1)S(1)}, u32[]{:S(2)}, u32[]{:S(2)}) collective-permute-start(bf16[2,64,384]{2,1,0:T(8,128)(2,1)S(1)} %get-tuple-element.60), channel_id=1, source_target_pairs={{0,16},{8,24},{16,0},{24,8},{1,17},{9,25},{17,1},{25,9},{2,18},{10... | collective-permute-start | bytes 294920 | tf_op jit(solution)/shard_map/ppermute | solution.py:28
  40.7 6.2 %collective-permute-start.14 = (bf16[2,64,384]{2,1,0:T(8,128)(2,1)S(1)}, bf16[2,64,384]{2,1,0:T(8,128)(2,1)S(1)}, u32[]{:S(2)}, u32[]{:S(2)}) collective-permute-start(bf16[2,64,384]{2,1,0:T(8,128)(2,1)S(1)} %get-tuple-element.61), channel_id=1, source_target_pairs={{0,24},{8,16},{16,8},{24,0},{1,25},{9,17},{17,9},{25,1},{2,26},{10... | collective-permute-start | bytes 294920 | tf_op jit(solution)/shard_map/ppermute | solution.py:28
  43.0 6.6 %collective-permute-start.21 = (bf16[2,64,384]{2,1,0:T(8,128)(2,1)S(1)}, bf16[2,64,384]{2,1,0:T(8,128)(2,1)S(1)}, u32[]{:S(2)}, u32[]{:S(2)}) collective-permute-start(bf16[2,64,384]{2,1,0:T(8,128)(2,1)S(1)} %get-tuple-element.70), channel_id=1, source_target_pairs={{0,1},{1,2},{2,3},{3,0},{4,5},{5,6},{6,7},{7,4},{8,9},{9,10},{10,1... | collective-permute-start | bytes 294920 | tf_op jit(solution)/shard_map/ppermute | solution.py:32
  43.1 10.9 %collective-permute-start.22 = (bf16[2,64,384]{2,1,0:T(8,128)(2,1)S(1)}, bf16[2,64,384]{2,1,0:T(8,128)(2,1)S(1)}, u32[]{:S(2)}, u32[]{:S(2)}) collective-permute-start(bf16[2,64,384]{2,1,0:T(8,128)(2,1)S(1)} %get-tuple-element.71), channel_id=1, source_target_pairs={{0,2},{1,3},{2,0},{3,1},{4,6},{5,7},{6,4},{7,5},{8,10},{9,11},{10,... | collective-permute-start | bytes 294920 | tf_op jit(solution)/shard_map/ppermute | solution.py:32
  44.3 9.7 %collective-permute-start.23 = (bf16[2,64,384]{2,1,0:T(8,128)(2,1)S(1)}, bf16[2,64,384]{2,1,0:T(8,128)(2,1)S(1)}, u32[]{:S(2)}, u32[]{:S(2)}) collective-permute-start(bf16[2,64,384]{2,1,0:T(8,128)(2,1)S(1)} %get-tuple-element.72), channel_id=1, source_target_pairs={{0,3},{1,0},{2,1},{3,2},{4,7},{5,4},{6,5},{7,6},{8,11},{9,8},{10,9... | collective-permute-start | bytes 294920 | tf_op jit(solution)/shard_map/ppermute | solution.py:32
  47.2 7.6 %collective-permute-start.15 = (bf16[2,64,384]{2,1,0:T(8,128)(2,1)S(1)}, bf16[2,64,384]{2,1,0:T(8,128)(2,1)S(1)}, u32[]{:S(2)}, u32[]{:S(2)}) collective-permute-start(bf16[2,64,384]{2,1,0:T(8,128)(2,1)S(1)} %get-tuple-element.63), channel_id=1, source_target_pairs={{0,1},{1,2},{2,3},{3,0},{4,5},{5,6},{6,7},{7,4},{8,9},{9,10},{10,1... | collective-permute-start | bytes 294920 | tf_op jit(solution)/shard_map/ppermute | solution.py:32
  47.9 8.9 %collective-permute-start.16 = (bf16[2,64,384]{2,1,0:T(8,128)(2,1)S(1)}, bf16[2,64,384]{2,1,0:T(8,128)(2,1)S(1)}, u32[]{:S(2)}, u32[]{:S(2)}) collective-permute-start(bf16[2,64,384]{2,1,0:T(8,128)(2,1)S(1)} %get-tuple-element.64), channel_id=1, source_target_pairs={{0,2},{1,3},{2,0},{3,1},{4,6},{5,7},{6,4},{7,5},{8,10},{9,11},{10,... | collective-permute-start | bytes 294920 | tf_op jit(solution)/shard_map/ppermute | solution.py:32
  49.7 7.1 %collective-permute-start.17 = (bf16[2,64,384]{2,1,0:T(8,128)(2,1)S(1)}, bf16[2,64,384]{2,1,0:T(8,128)(2,1)S(1)}, u32[]{:S(2)}, u32[]{:S(2)}) collective-permute-start(bf16[2,64,384]{2,1,0:T(8,128)(2,1)S(1)} %get-tuple-element.65), channel_id=1, source_target_pairs={{0,3},{1,0},{2,1},{3,2},{4,7},{5,4},{6,5},{7,6},{8,11},{9,8},{10,9... | collective-permute-start | bytes 294920 | tf_op jit(solution)/shard_map/ppermute | solution.py:32

commit v6 on v5

--- a/solution.py
+++ b/solution.py
@@ -55,7 +55,14 @@
     run_copies([(memory_ref.at[:, :, columns_of(chunk, width, head_cols, o)], out) for o, out in zip(owners, outs)], sem)
 
 
-def facts_kernel(section_count, plan_ref, key_len_ref, query_len_ref, facts_ref):
+def first_split_kernel(tp_count, chunk, width, head_cols, memory_ref, plan_in, key_len_in, query_len_in, facts_ref, *refs):
+    outs, (plan_ref, key_len_ref, query_len_ref, sem) = refs[:tp_count], refs[tp_count:]
+    me = lax.axis_index("tp")
+    section_count = plan_ref.shape[1]
+    owners = [ahead(me, step, tp_count) for step in range(tp_count)]
+    pairs = [(memory_ref.at[:, :, columns_of(chunk, width, head_cols, o)], out) for o, out in zip(owners, outs)]
+    scalars = [(plan_in, plan_ref), (key_len_in, key_len_ref), (query_len_in, query_len_ref)]
+    run_copies(pairs + scalars, sem)
     for section in range(section_count):
         facts_ref[section] = plan_ref[0, section]
     micro = plan_ref[0, lax.axis_index("section")]
@@ -163,9 +170,20 @@
 
     memory = pltpu.with_memory_space_constraint(memory, pltpu.HBM)
     copy_sem = pltpu.SemaphoreType.DMA((tp_count,))
-    parts = []
-    for chunk in range(chunks):
-        gate = [parts[-1][1]] if parts else []
+    scalars = [pltpu.with_memory_space_constraint(array, pltpu.HBM) for array in (plan, enc_lengths, tgt_lengths)]
+    facts, *split = pl.pallas_call(
+        functools.partial(first_split_kernel, tp_count, 0, width, head_cols),
+        out_shape=[pltpu.SMEM((section_count + 2,), jnp.int32)] + [piece] * tp_count,
+        in_specs=[ANY] * 4,
+        out_specs=[SMEM] + [VMEM] * tp_count,
+        scratch_shapes=[pltpu.SMEM(array.shape, jnp.int32) for array in (plan, enc_lengths, tgt_lengths)]
+        + [pltpu.SemaphoreType.DMA((tp_count + 3,))],
+        compiler_params=params,
+        name="split0",
+    )(memory, *scalars)
+    parts = [[split[0]] + [shift(split[step], step, tp_count) for step in range(1, tp_count)]]
+    for chunk in range(1, chunks):
+        gate = [parts[-1][1]]
         split = pl.pallas_call(
             functools.partial(split_kernel, tp_count, chunk, width, head_cols),
             out_shape=[piece] * tp_count,
@@ -176,14 +194,6 @@
             name=f"split{chunk}",
         )(memory, *gate)
         parts.append([split[0]] + [shift(split[step], step, tp_count) for step in range(1, tp_count)])
-    facts = pl.pallas_call(
-        functools.partial(facts_kernel, section_count),
-        out_shape=pltpu.SMEM((section_count + 2,), jnp.int32),
-        in_specs=[SMEM] * 3,
-        out_specs=SMEM,
-        compiler_params=params,
-        name="facts",
-    )(plan, enc_lengths, tgt_lengths)
     facts = pltpu.with_memory_space_constraint(facts, pltpu.SMEM)
 
     def pick(chunk, steps, gate):

time: 57.7 us -> 57.8 us (level)
  waiting for transfers between devices: 7.81 us -> 9.24 us
  starting transfers between devices: 38.5 us -> 37.7 us
    ppermute x12, waiting for transfers between devices: 3.97 us -> 6.49 us  [shift(): lax.ppermute(piece, 'tp', [(i, (i + step) % count) for i in range(count)])]
    pallas_call x2 -> x1, Pallas kernels: 2.16 us -> 1.07 us  [body(): pl.pallas_call(functools.partial(split_kernel, tp_count, chunk, width, he...]
    ppermute x12, waiting for transfers between devices: 3.84 us -> 2.75 us  [swap(): return lax.ppermute(piece, 'section', [(i, i ^ step) for i in range(count)])]
    ppermute x12, starting transfers between devices: 23.9 us -> 22.8 us  [shift(): lax.ppermute(piece, 'tp', [(i, (i + step) % count) for i in range(count)])]
    pallas_call x1, Pallas kernels: 0.57 us -> 1.15 us  [body(): pl.pallas_call(functools.partial(first_split_kernel, tp_count, 0, width,...]
    unnamed x12 -> x6, local copies, waits for them, and re-layouts: 1.78 us -> 1.77 us
  transfers between devices with their start and end apart: 24 -> 24, of which waited for: 5 -> 6; matrix products, arithmetic and copies ran while one was open for 3% -> 3% of each run, Pallas kernels for 12% -> 11%
where the time goes in v6:
time: 57.8 us; the launch traced here: 57.6 us
  starting transfers between devices  37.7 us (65%)
  waiting for transfers between devices  9.24 us (16%)
  Pallas kernels  8.15 us (14%)
  local copies, waits for them, and re-layouts  1.77 us (3%)
  between operations  0.74 us (1%)
    ppermute x12, starting transfers between devices, shift(): lax.ppermute(piece, 'tp', [(i, (i + step) % count) for i in range(count)])  22.8 us
    ppermute x12, starting transfers between devices, swap(): return lax.ppermute(piece, 'section', [(i, i ^ step) for i in range(count)])  14.9 us
    ppermute x12, waiting for transfers between devices, shift(): lax.ppermute(piece, 'tp', [(i, (i + step) % count) for i in range(count)])  6.49 us
    pallas_call x2, Pallas kernels, body(): pl.pallas_call(functools.partial(heads_kernel, section_count, chunk, widt...  3.54 us
    ppermute x12, waiting for transfers between devices, swap(): return lax.ppermute(piece, 'section', [(i, i ^ step) for i in range(count)])  2.75 us
    unnamed x6, local copies, waits for them, and re-layouts  1.77 us
    pallas_call x2, Pallas kernels, body(): pl.pallas_call(functools.partial(join_kernel, tp_count, chunk, width, hea...  1.54 us
  transfers between devices with their start and end apart: 24, of which 6 were waited for; matrix products, arithmetic and copies ran while one was open for 3% of the time, Pallas kernels for 11%

profile of v6, /device:TPU:0, one launch (start us, length us, event | category | flops | bytes accessed | tf_op | source)
XLA Modules:
  0.0 57.6 jit_solution(6883197554564040467)
XLA Ops:
  0.6 1.2 %split0.1 = (s32[6]{0:T(128)S(4)}, bf16[2,64,384]{2,1,0:T(8,128)(2,1)S(1)}, bf16[2,64,384]{2,1,0:T(8,128)(2,1)S(1)}, bf16[2,64,384]{2,1,0:T(8,128)(2,1)S(1)}, bf16[2,64,384]{2,1,0:T(8,128)(2,1)S(1)}) custom-call(bf16[2,64,3072]{2,1,0:T(8,128)(2,1)} %bitcast.14, s32[1,4]{1,0:T(1,128)} %plan_in.1, s32[1,4]{1,0:T(1,128)} %key_len_in.1, s32[1,4]{1,0:T(1,128)} %query_len_in.1), custom_call_target="tpu_custom_call" | custom-call | tf_op jit(solution)/shard_map/split0/pallas_call | solution.py:174
  1.8 3.1 %collective-permute-start = (bf16[2,64,384]{2,1,0:T(8,128)(2,1)S(1)}, bf16[2,64,384]{2,1,0:T(8,128)(2,1)S(1)}, u32[]{:S(2)}, u32[]{:S(2)}) collective-permute-start(bf16[2,64,384]{2,1,0:T(8,128)(2,1)S(1)} %get-tuple-element.40), channel_id=1, source_target_pairs={{0,1},{1,2},{2,3},{3,0},{4,5},{5,6},{6,7},{7,4},{8,9},{9,10},{10,1... | collective-permute-start | bytes 294920 | tf_op jit(solution)/shard_map/ppermute | solution.py:32
  4.9 2.6 %collective-permute-start.6 = (bf16[2,64,384]{2,1,0:T(8,128)(2,1)S(1)}, bf16[2,64,384]{2,1,0:T(8,128)(2,1)S(1)}, u32[]{:S(2)}, u32[]{:S(2)}) collective-permute-start(bf16[2,64,384]{2,1,0:T(8,128)(2,1)S(1)} %get-tuple-element.49), channel_id=1, source_target_pairs={{0,2},{1,3},{2,0},{3,1},{4,6},{5,7},{6,4},{7,5},{8,10},{9,11},{10,... | collective-permute-start | bytes 294920 | tf_op jit(solution)/shard_map/ppermute | solution.py:32
  7.5 1.3 %collective-permute-start.7 = (bf16[2,64,384]{2,1,0:T(8,128)(2,1)S(1)}, bf16[2,64,384]{2,1,0:T(8,128)(2,1)S(1)}, u32[]{:S(2)}, u32[]{:S(2)}) collective-permute-start(bf16[2,64,384]{2,1,0:T(8,128)(2,1)S(1)} %get-tuple-element.50), channel_id=1, source_target_pairs={{0,3},{1,0},{2,1},{3,2},{4,7},{5,4},{6,5},{7,6},{8,11},{9,8},{10,9... | collective-permute-start | bytes 294920 | tf_op jit(solution)/shard_map/ppermute | solution.py:32
  8.8 1.7 %collective-permute-done.refs_0_.refs_1_ = bf16[2,64,384]{2,1,0:T(8,128)(2,1)S(1)} collective-permute-done((bf16[2,64,384]{2,1,0:T(8,128)(2,1)S(1)}, bf16[2,64,384]{2,1,0:T(8,128)(2,1)S(1)}, u32[]{:S(2)}, u32[]{:S(2)}) %collective-permute-start) | collective-permute-done | bytes 98336 | tf_op jit(solution)/shard_map/ppermute | solution.py:32
  10.5 1.1 %split1.1 = (bf16[2,64,384]{2,1,0:T(8,128)(2,1)S(1)}, bf16[2,64,384]{2,1,0:T(8,128)(2,1)S(1)}, bf16[2,64,384]{2,1,0:T(8,128)(2,1)S(1)}, bf16[2,64,384]{2,1,0:T(8,128)(2,1)S(1)}) custom-call(bf16[2,64,3072]{2,1,0:T(8,128)(2,1)} %bitcast.15, bf16[2,64,384]{2,1,0:T(8,128)(2,1)S(1)} %collective-permute-done.refs_0_.refs_1_), custom_call_target="tpu_custom_call" | custom-call | tf_op jit(solution)/shard_map/split1/pallas_call | solution.py:187
  11.6 3.3 %collective-permute-start.1 = (bf16[2,64,384]{2,1,0:T(8,128)(2,1)S(1)}, bf16[2,64,384]{2,1,0:T(8,128)(2,1)S(1)}, u32[]{:S(2)}, u32[]{:S(2)}) collective-permute-start(bf16[2,64,384]{2,1,0:T(8,128)(2,1)S(1)} %get-tuple-element.42), channel_id=1, source_target_pairs={{0,1},{1,2},{2,3},{3,0},{4,5},{5,6},{6,7},{7,4},{8,9},{9,10},{10,1... | collective-permute-start | bytes 294920 | tf_op jit(solution)/shard_map/ppermute | solution.py:32
  14.9 2.0 %collective-permute-start.2 = (bf16[2,64,384]{2,1,0:T(8,128)(2,1)S(1)}, bf16[2,64,384]{2,1,0:T(8,128)(2,1)S(1)}, u32[]{:S(2)}, u32[]{:S(2)}) collective-permute-start(bf16[2,64,384]{2,1,0:T(8,128)(2,1)S(1)} %get-tuple-element.43), channel_id=1, source_target_pairs={{0,2},{1,3},{2,0},{3,1},{4,6},{5,7},{6,4},{7,5},{8,10},{9,11},{10,... | collective-permute-start | bytes 294920 | tf_op jit(solution)/shard_map/ppermute | solution.py:32
  17.0 2.8 %collective-permute-start.3 = (bf16[2,64,384]{2,1,0:T(8,128)(2,1)S(1)}, bf16[2,64,384]{2,1,0:T(8,128)(2,1)S(1)}, u32[]{:S(2)}, u32[]{:S(2)}) collective-permute-start(bf16[2,64,384]{2,1,0:T(8,128)(2,1)S(1)} %get-tuple-element.44), channel_id=1, source_target_pairs={{0,3},{1,0},{2,1},{3,2},{4,7},{5,4},{6,5},{7,6},{8,11},{9,8},{10,9... | collective-permute-start | bytes 294920 | tf_op jit(solution)/shard_map/ppermute | solution.py:32
  19.8 0.0 collective-permute-done.6.refs_2_
  19.8 0.0 collective-permute-done.7.refs_3_
  19.8 0.1 pick0.1
  19.9 1.3 %collective-permute-start.8 = (bf16[2,64,384]{2,1,0:T(8,128)(2,1)S(1)}, bf16[2,64,384]{2,1,0:T(8,128)(2,1)S(1)}, u32[]{:S(2)}, u32[]{:S(2)}) collective-permute-start(bf16[2,64,384]{2,1,0:T(8,128)(2,1)S(1)} %get-tuple-element.52), channel_id=1, source_target_pairs={{0,8},{8,0},{16,24},{24,16},{1,9},{9,1},{17,25},{25,17},{2,10},{10... | collective-permute-start | bytes 294920 | tf_op jit(solution)/shard_map/ppermute | solution.py:28
  21.2 1.5 %collective-permute-start.9 = (bf16[2,64,384]{2,1,0:T(8,128)(2,1)S(1)}, bf16[2,64,384]{2,1,0:T(8,128)(2,1)S(1)}, u32[]{:S(2)}, u32[]{:S(2)}) collective-permute-start(bf16[2,64,384]{2,1,0:T(8,128)(2,1)S(1)} %get-tuple-element.53), channel_id=1, source_target_pairs={{0,16},{8,24},{16,0},{24,8},{1,17},{9,25},{17,1},{25,9},{2,18},{10... | collective-permute-start | bytes 294920 | tf_op jit(solution)/shard_map/ppermute | solution.py:28
  22.7 0.0 collective-permute-done.1.refs_1_
  22.7 0.7 %collective-permute-start.10 = (bf16[2,64,384]{2,1,0:T(8,128)(2,1)S(1)}, bf16[2,64,384]{2,1,0:T(8,128)(2,1)S(1)}, u32[]{:S(2)}, u32[]{:S(2)}) collective-permute-start(bf16[2,64,384]{2,1,0:T(8,128)(2,1)S(1)} %get-tuple-element.54), channel_id=1, source_target_pairs={{0,24},{8,16},{16,8},{24,0},{1,25},{9,17},{17,9},{25,1},{2,26},{10... | collective-permute-start | bytes 294920 | tf_op jit(solution)/shard_map/ppermute | solution.py:28
  23.5 0.1 pick1.2
  23.6 1.3 %collective-permute-start.4 = (bf16[2,64,384]{2,1,0:T(8,128)(2,1)S(1)}, bf16[2,64,384]{2,1,0:T(8,128)(2,1)S(1)}, u32[]{:S(2)}, u32[]{:S(2)}) collective-permute-start(bf16[2,64,384]{2,1,0:T(8,128)(2,1)S(1)} %get-tuple-element.46), channel_id=1, source_target_pairs={{0,8},{8,0},{16,24},{24,16},{1,9},{9,1},{17,25},{25,17},{2,10},{10... | collective-permute-start | bytes 294920 | tf_op jit(solution)/shard_map/ppermute | solution.py:28
  24.9 1.5 %collective-permute-start.5 = (bf16[2,64,384]{2,1,0:T(8,128)(2,1)S(1)}, bf16[2,64,384]{2,1,0:T(8,128)(2,1)S(1)}, u32[]{:S(2)}, u32[]{:S(2)}) collective-permute-start(bf16[2,64,384]{2,1,0:T(8,128)(2,1)S(1)} %get-tuple-element.47), channel_id=1, source_target_pairs={{0,16},{8,24},{16,0},{24,8},{1,17},{9,25},{17,1},{25,9},{2,18},{10... | collective-permute-start | bytes 294920 | tf_op jit(solution)/shard_map/ppermute | solution.py:28
  26.4 2.0 %collective-permute-done.10.refs_3_ = bf16[2,64,384]{2,1,0:T(8,128)(2,1)S(1)} collective-permute-done((bf16[2,64,384]{2,1,0:T(8,128)(2,1)S(1)}, bf16[2,64,384]{2,1,0:T(8,128)(2,1)S(1)}, u32[]{:S(2)}, u32[]{:S(2)}) %collective-permute-start.10) | collective-permute-done | bytes 98336 | tf_op jit(solution)/shard_map/ppermute | solution.py:28
  28.4 1.8 %heads0.1 = (bf16[512,768]{1,0:T(8,128)(2,1)S(1)}, bf16[512,768]{1,0:T(8,128)(2,1)S(1)}, bf16[2,64,384]{2,1,0:T(8,128)(2,1)S(1)}, bf16[2,64,384]{2,1,0:T(8,128)(...) custom-call(s32[6]{0:T(128)S(4)} %get-tuple-element.39.facts_ref, ...), custom_call_target="tpu_custom_call" | custom-call | flops 603979776 | bytes 8388608 | tf_op jit(solution)/shard_map/heads0/pallas_call | solution.py:218
  30.2 1.4 %collective-permute-start.11 = (bf16[2,64,384]{2,1,0:T(8,128)(2,1)S(1)}, bf16[2,64,384]{2,1,0:T(8,128)(2,1)S(1)}, u32[]{:S(2)}, u32[]{:S(2)}) collective-permute-start(bf16[2,64,384]{2,1,0:T(8,128)(2,1)S(1)} %pick1.3), channel_id=1, source_target_pairs={{0,24},{8,16},{16,8},{24,0},{1,25},{9,17},{17,9},{25,1},{2,26},{10... | collective-permute-start | bytes 294920 | tf_op jit(solution)/shard_map/ppermute | solution.py:28
  31.6 0.7 %collective-permute-start.18 = (bf16[2,64,384]{2,1,0:T(8,128)(2,1)S(1)}, bf16[2,64,384]{2,1,0:T(8,128)(2,1)S(1)}, u32[]{:S(2)}, u32[]{:S(2)}) collective-permute-start(bf16[2,64,384]{2,1,0:T(8,128)(2,1)S(1)} %get-tuple-element.68), channel_id=1, source_target_pairs={{0,8},{8,0},{16,24},{24,16},{1,9},{9,1},{17,25},{25,17},{2,10},{10... | collective-permute-start | bytes 294920 | tf_op jit(solution)/shard_map/ppermute | solution.py:28
  32.2 1.5 %collective-permute-start.19 = (bf16[2,64,384]{2,1,0:T(8,128)(2,1)S(1)}, bf16[2,64,384]{2,1,0:T(8,128)(2,1)S(1)}, u32[]{:S(2)}, u32[]{:S(2)}) collective-permute-start(bf16[2,64,384]{2,1,0:T(8,128)(2,1)S(1)} %get-tuple-element.69), channel_id=1, source_target_pairs={{0,16},{8,24},{16,0},{24,8},{1,17},{9,25},{17,1},{25,9},{2,18},{10... | collective-permute-start | bytes 294920 | tf_op jit(solution)/shard_map/ppermute | solution.py:28
  33.8 1.3 %collective-permute-start.20 = (bf16[2,64,384]{2,1,0:T(8,128)(2,1)S(1)}, bf16[2,64,384]{2,1,0:T(8,128)(2,1)S(1)}, u32[]{:S(2)}, u32[]{:S(2)}) collective-permute-start(bf16[2,64,384]{2,1,0:T(8,128)(2,1)S(1)} %get-tuple-element.70), channel_id=1, source_target_pairs={{0,24},{8,16},{16,8},{24,0},{1,25},{9,17},{17,9},{25,1},{2,26},{10... | collective-permute-start | bytes 294920 | tf_op jit(solution)/shard_map/ppermute | solution.py:28
  35.1 0.0 collective-permute-done.5.refs_2_
  35.1 0.7 %collective-permute-done.11.refs_3_ = bf16[2,64,384]{2,1,0:T(8,128)(2,1)S(1)} collective-permute-done((bf16[2,64,384]{2,1,0:T(8,128)(2,1)S(1)}, bf16[2,64,384]{2,1,0:T(8,128)(2,1)S(1)}, u32[]{:S(2)}, u32[]{:S(2)}) %collective-permute-start.11) | collective-permute-done | bytes 98336 | tf_op jit(solution)/shard_map/ppermute | solution.py:28
  35.8 1.8 %heads1.1 = (bf16[512,768]{1,0:T(8,128)(2,1)S(1)}, bf16[512,768]{1,0:T(8,128)(2,1)S(1)}, bf16[2,64,384]{2,1,0:T(8,128)(2,1)S(1)}, bf16[2,64,384]{2,1,0:T(8,128)(...) custom-call(s32[6]{0:T(128)S(4)} %get-tuple-element.39.facts_ref, ...), custom_call_target="tpu_custom_call", output_to_operand_aliasing={{0}: (7, {}), {1}: (8, {})} | custom-call | flops 603979776 | bytes 8388608 | tf_op jit(solution)/shard_map/heads1/pallas_call | solution.py:218
  37.6 2.1 %collective-permute-start.12 = (bf16[2,64,384]{2,1,0:T(8,128)(2,1)S(1)}, bf16[2,64,384]{2,1,0:T(8,128)(2,1)S(1)}, u32[]{:S(2)}, u32[]{:S(2)}) collective-permute-start(bf16[2,64,384]{2,1,0:T(8,128)(2,1)S(1)} %get-tuple-element.61), channel_id=1, source_target_pairs={{0,8},{8,0},{16,24},{24,16},{1,9},{9,1},{17,25},{25,17},{2,10},{10... | collective-permute-start | bytes 294920 | tf_op jit(solution)/shard_map/ppermute | solution.py:28
  39.7 0.0 collective-permute-done.18.refs_1_
  39.7 1.5 %collective-permute-start.14 = (bf16[2,64,384]{2,1,0:T(8,128)(2,1)S(1)}, bf16[2,64,384]{2,1,0:T(8,128)(2,1)S(1)}, u32[]{:S(2)}, u32[]{:S(2)}) collective-permute-start(bf16[2,64,384]{2,1,0:T(8,128)(2,1)S(1)} %get-tuple-element.63), channel_id=1, source_target_pairs={{0,24},{8,16},{16,8},{24,0},{1,25},{9,17},{17,9},{25,1},{2,26},{10... | collective-permute-start | bytes 294920 | tf_op jit(solution)/shard_map/ppermute | solution.py:28
  41.3 0.3 sum0.1
  41.6 1.0 %collective-permute-start.21 = (bf16[2,64,384]{2,1,0:T(8,128)(2,1)S(1)}, bf16[2,64,384]{2,1,0:T(8,128)(2,1)S(1)}, u32[]{:S(2)}, u32[]{:S(2)}) collective-permute-start(bf16[2,64,384]{2,1,0:T(8,128)(2,1)S(1)} %get-tuple-element.72), channel_id=1, source_target_pairs={{0,1},{1,2},{2,3},{3,0},{4,5},{5,6},{6,7},{7,4},{8,9},{9,10},{10,1... | collective-permute-start | bytes 294920 | tf_op jit(solution)/shard_map/ppermute | solution.py:32
  42.5 0.9 %collective-permute-start.22 = (bf16[2,64,384]{2,1,0:T(8,128)(2,1)S(1)}, bf16[2,64,384]{2,1,0:T(8,128)(2,1)S(1)}, u32[]{:S(2)}, u32[]{:S(2)}) collective-permute-start(bf16[2,64,384]{2,1,0:T(8,128)(2,1)S(1)} %get-tuple-element.73), channel_id=1, source_target_pairs={{0,2},{1,3},{2,0},{3,1},{4,6},{5,7},{6,4},{7,5},{8,10},{9,11},{10,... | collective-permute-start | bytes 294920 | tf_op jit(solution)/shard_map/ppermute | solution.py:32
  43.4 2.2 %collective-permute-start.23 = (bf16[2,64,384]{2,1,0:T(8,128)(2,1)S(1)}, bf16[2,64,384]{2,1,0:T(8,128)(2,1)S(1)}, u32[]{:S(2)}, u32[]{:S(2)}) collective-permute-start(bf16[2,64,384]{2,1,0:T(8,128)(2,1)S(1)} %get-tuple-element.74), channel_id=1, source_target_pairs={{0,3},{1,0},{2,1},{3,2},{4,7},{5,4},{6,5},{7,6},{8,11},{9,8},{10,9... | collective-permute-start | bytes 294920 | tf_op jit(solution)/shard_map/ppermute | solution.py:32
  45.6 0.3 sum1.1
  45.9 0.5 collective-permute-start.15
  46.4 1.5 %collective-permute-start.16 = (bf16[2,64,384]{2,1,0:T(8,128)(2,1)S(1)}, bf16[2,64,384]{2,1,0:T(8,128)(2,1)S(1)}, u32[]{:S(2)}, u32[]{:S(2)}) collective-permute-start(bf16[2,64,384]{2,1,0:T(8,128)(2,1)S(1)} %get-tuple-element.66), channel_id=1, source_target_pairs={{0,2},{1,3},{2,0},{3,1},{4,6},{5,7},{6,4},{7,5},{8,10},{9,11},{10,... | collective-permute-start | bytes 294920 | tf_op jit(solution)/shard_map/ppermute | solution.py:32
  47.9 1.3 %collective-permute-done.21.refs_1_ = bf16[2,64,384]{2,1,0:T(8,128)(2,1)S(1)} collective-permute-done((bf16[2,64,384]{2,1,0:T(8,128)(2,1)S(1)}, bf16[2,64,384]{2,1,0:T(8,128)(2,1)S(1)}, u32[]{:S(2)}, u32[]{:S(2)}) %collective-permute-start.21) | collective-permute-done | bytes 98336 | tf_op jit(solution)/shard_map/ppermute | solution.py:32
  49.2 1.6 %collective-permute-start.17 = (bf16[2,64,384]{2,1,0:T(8,128)(2,1)S(1)}, bf16[2,64,384]{2,1,0:T(8,128)(2,1)S(1)}, u32[]{:S(2)}, u32[]{:S(2)}) collective-permute-start(bf16[2,64,384]{2,1,0:T(8,128)(2,1)S(1)} %get-tuple-element.67), channel_id=1, source_target_pairs={{0,3},{1,0},{2,1},{3,2},{4,7},{5,4},{6,5},{7,6},{8,11},{9,8},{10,9... | collective-permute-start | bytes 294920 | tf_op jit(solution)/shard_map/ppermute | solution.py:32
  50.8 0.9 %copy.16 = bf16[1,1,512,768]{3,2,1,0:T(8,128)(2,1)} copy(bf16[1,1,512,768]{3,2,1,0:T(8,128)(2,1)S(1)} %bitcast.8) | data formatting | bytes 1572864
  51.7 0.9 %copy.17 = bf16[1,1,512,768]{3,2,1,0:T(8,128)(2,1)} copy(bf16[1,1,512,768]{3,2,1,0:T(8,128)(2,1)S(1)} %bitcast.9) | data formatting | bytes 1572864
  52.5 1.6 %collective-permute-done.22.refs_2_ = bf16[2,64,384]{2,1,0:T(8,128)(2,1)S(1)} collective-permute-done((bf16[2,64,384]{2,1,0:T(8,128)(2,1)S(1)}, bf16[2,64,384]{2,1,0:T(8,128)(2,1)S(1)}, u32[]{:S(2)}, u32[]{:S(2)}) %collective-permute-start.22) | collective-permute-done | bytes 98336 | tf_op jit(solution)/shard_map/ppermute | solution.py:32
  54.1 0.0 collective-permute-done.23.refs_3_
  54.1 0.8 %join0.1.refs_4_ = bf16[2,64,3072]{2,1,0:T(8,128)(2,1)} custom-call(bf16[2,64,384]{2,1,0:T(8,128)(2,1)S(1)} %get-tuple-element.71.refs_0_, bf16[2,64,384]{2,1,0:T(8,128)(2,1)S(1)} %collective-permute-done.21.refs_1_, bf16[2,64,384]{2,1,0:T(8,128)(2,1)S(1)} %collective-permute-done.22.refs_2_, bf16[2,64,384]{2,1,0:T(8,128)(2,1)S(1)} %collective-permute-done.23.refs_3_), custom_call_target="tpu_custom_call" | custom-call | tf_op jit(solution)/shard_map/join0/pallas_call | solution.py:245
  54.9 1.9 %collective-permute-done.16.refs_2_ = bf16[2,64,384]{2,1,0:T(8,128)(2,1)S(1)} collective-permute-done((bf16[2,64,384]{2,1,0:T(8,128)(2,1)S(1)}, bf16[2,64,384]{2,1,0:T(8,128)(2,1)S(1)}, u32[]{:S(2)}, u32[]{:S(2)}) %collective-permute-start.16) | collective-permute-done | bytes 98336 | tf_op jit(solution)/shard_map/ppermute | solution.py:32
  56.8 0.0 collective-permute-done.17.refs_3_
  56.8 0.8 %join1.1 = bf16[2,64,3072]{2,1,0:T(8,128)(2,1)} custom-call(bf16[2,64,384]{2,1,0:T(8,128)(2,1)S(1)} %get-tuple-element.64.refs_0_, bf16[2,64,384]{2,1,0:T(8,128)(2,1)S(1)} %collective-permute-done.15.refs_1_, bf16[2,64,384]{2,1,0:T(8,128)(2,1)S(1)} %collective-permute-done.16.refs_2_, ...), custom_call_target="tpu_custom_call", output_to_operand_aliasing={{}: (4, {})} | custom-call | tf_op jit(solution)/shard_map/join1/pallas_call | solution.py:245
  (17 shorter events, 0.1 us)
Async XLA Ops:
  1.8 8.8 %collective-permute-start = (bf16[2,64,384]{2,1,0:T(8,128)(2,1)S(1)}, bf16[2,64,384]{2,1,0:T(8,128)(2,1)S(1)}, u32[]{:S(2)}, u32[]{:S(2)}) collective-permute-start(bf16[2,64,384]{2,1,0:T(8,128)(2,1)S(1)} %get-tuple-element.40), channel_id=1, source_target_pairs={{0,1},{1,2},{2,3},{3,0},{4,5},{5,6},{6,7},{7,4},{8,9},{9,10},{10,1... | collective-permute-start | bytes 294920 | tf_op jit(solution)/shard_map/ppermute | solution.py:32
  4.9 15.0 %collective-permute-start.6 = (bf16[2,64,384]{2,1,0:T(8,128)(2,1)S(1)}, bf16[2,64,384]{2,1,0:T(8,128)(2,1)S(1)}, u32[]{:S(2)}, u32[]{:S(2)}) collective-permute-start(bf16[2,64,384]{2,1,0:T(8,128)(2,1)S(1)} %get-tuple-element.49), channel_id=1, source_target_pairs={{0,2},{1,3},{2,0},{3,1},{4,6},{5,7},{6,4},{7,5},{8,10},{9,11},{10,... | collective-permute-start | bytes 294920 | tf_op jit(solution)/shard_map/ppermute | solution.py:32
  7.5 20.9 %copy-start = (bf16[1,1,512,768]{3,2,1,0:T(8,128)(2,1)S(1)}, bf16[1,1,512,768]{3,2,1,0:T(8,128)(2,1)}, u32[]{:S(2)}) copy-start(bf16[1,1,512,768]{3,2,1,0:T(8,128)(2,1)} %param.7) | copy-start | bytes 2359300
  7.5 20.9 %copy-start.1 = (bf16[1,1,512,768]{3,2,1,0:T(8,128)(2,1)S(1)}, bf16[1,1,512,768]{3,2,1,0:T(8,128)(2,1)}, u32[]{:S(2)}) copy-start(bf16[1,1,512,768]{3,2,1,0:T(8,128)(2,1)} %param.8) | copy-start | bytes 2359300
  7.5 12.4 %collective-permute-start.7 = (bf16[2,64,384]{2,1,0:T(8,128)(2,1)S(1)}, bf16[2,64,384]{2,1,0:T(8,128)(2,1)S(1)}, u32[]{:S(2)}, u32[]{:S(2)}) collective-permute-start(bf16[2,64,384]{2,1,0:T(8,128)(2,1)S(1)} %get-tuple-element.50), channel_id=1, source_target_pairs={{0,3},{1,0},{2,1},{3,2},{4,7},{5,4},{6,5},{7,6},{8,11},{9,8},{10,9... | collective-permute-start | bytes 294920 | tf_op jit(solution)/shard_map/ppermute | solution.py:32
  11.6 11.1 %collective-permute-start.1 = (bf16[2,64,384]{2,1,0:T(8,128)(2,1)S(1)}, bf16[2,64,384]{2,1,0:T(8,128)(2,1)S(1)}, u32[]{:S(2)}, u32[]{:S(2)}) collective-permute-start(bf16[2,64,384]{2,1,0:T(8,128)(2,1)S(1)} %get-tuple-element.42), channel_id=1, source_target_pairs={{0,1},{1,2},{2,3},{3,0},{4,5},{5,6},{6,7},{7,4},{8,9},{9,10},{10,1... | collective-permute-start | bytes 294920 | tf_op jit(solution)/shard_map/ppermute | solution.py:32
  14.9 8.6 %collective-permute-start.2 = (bf16[2,64,384]{2,1,0:T(8,128)(2,1)S(1)}, bf16[2,64,384]{2,1,0:T(8,128)(2,1)S(1)}, u32[]{:S(2)}, u32[]{:S(2)}) collective-permute-start(bf16[2,64,384]{2,1,0:T(8,128)(2,1)S(1)} %get-tuple-element.43), channel_id=1, source_target_pairs={{0,2},{1,3},{2,0},{3,1},{4,6},{5,7},{6,4},{7,5},{8,10},{9,11},{10,... | collective-permute-start | bytes 294920 | tf_op jit(solution)/shard_map/ppermute | solution.py:32
  17.0 6.5 %collective-permute-start.3 = (bf16[2,64,384]{2,1,0:T(8,128)(2,1)S(1)}, bf16[2,64,384]{2,1,0:T(8,128)(2,1)S(1)}, u32[]{:S(2)}, u32[]{:S(2)}) collective-permute-start(bf16[2,64,384]{2,1,0:T(8,128)(2,1)S(1)} %get-tuple-element.44), channel_id=1, source_target_pairs={{0,3},{1,0},{2,1},{3,2},{4,7},{5,4},{6,5},{7,6},{8,11},{9,8},{10,9... | collective-permute-start | bytes 294920 | tf_op jit(solution)/shard_map/ppermute | solution.py:32
  19.9 6.5 %collective-permute-start.8 = (bf16[2,64,384]{2,1,0:T(8,128)(2,1)S(1)}, bf16[2,64,384]{2,1,0:T(8,128)(2,1)S(1)}, u32[]{:S(2)}, u32[]{:S(2)}) collective-permute-start(bf16[2,64,384]{2,1,0:T(8,128)(2,1)S(1)} %get-tuple-element.52), channel_id=1, source_target_pairs={{0,8},{8,0},{16,24},{24,16},{1,9},{9,1},{17,25},{25,17},{2,10},{10... | collective-permute-start | bytes 294920 | tf_op jit(solution)/shard_map/ppermute | solution.py:28
  21.2 5.2 %collective-permute-start.9 = (bf16[2,64,384]{2,1,0:T(8,128)(2,1)S(1)}, bf16[2,64,384]{2,1,0:T(8,128)(2,1)S(1)}, u32[]{:S(2)}, u32[]{:S(2)}) collective-permute-start(bf16[2,64,384]{2,1,0:T(8,128)(2,1)S(1)} %get-tuple-element.53), channel_id=1, source_target_pairs={{0,16},{8,24},{16,0},{24,8},{1,17},{9,25},{17,1},{25,9},{2,18},{10... | collective-permute-start | bytes 294920 | tf_op jit(solution)/shard_map/ppermute | solution.py:28
  22.7 5.6 %collective-permute-start.10 = (bf16[2,64,384]{2,1,0:T(8,128)(2,1)S(1)}, bf16[2,64,384]{2,1,0:T(8,128)(2,1)S(1)}, u32[]{:S(2)}, u32[]{:S(2)}) collective-permute-start(bf16[2,64,384]{2,1,0:T(8,128)(2,1)S(1)} %get-tuple-element.54), channel_id=1, source_target_pairs={{0,24},{8,16},{16,8},{24,0},{1,25},{9,17},{17,9},{25,1},{2,26},{10... | collective-permute-start | bytes 294920 | tf_op jit(solution)/shard_map/ppermute | solution.py:28
  23.6 10.2 %collective-permute-start.4 = (bf16[2,64,384]{2,1,0:T(8,128)(2,1)S(1)}, bf16[2,64,384]{2,1,0:T(8,128)(2,1)S(1)}, u32[]{:S(2)}, u32[]{:S(2)}) collective-permute-start(bf16[2,64,384]{2,1,0:T(8,128)(2,1)S(1)} %get-tuple-element.46), channel_id=1, source_target_pairs={{0,8},{8,0},{16,24},{24,16},{1,9},{9,1},{17,25},{25,17},{2,10},{10... | collective-permute-start | bytes 294920 | tf_op jit(solution)/shard_map/ppermute | solution.py:28
  24.9 10.2 %collective-permute-start.5 = (bf16[2,64,384]{2,1,0:T(8,128)(2,1)S(1)}, bf16[2,64,384]{2,1,0:T(8,128)(2,1)S(1)}, u32[]{:S(2)}, u32[]{:S(2)}) collective-permute-start(bf16[2,64,384]{2,1,0:T(8,128)(2,1)S(1)} %get-tuple-element.47), channel_id=1, source_target_pairs={{0,16},{8,24},{16,0},{24,8},{1,17},{9,25},{17,1},{25,9},{2,18},{10... | collective-permute-start | bytes 294920 | tf_op jit(solution)/shard_map/ppermute | solution.py:28
  30.2 5.6 %collective-permute-start.11 = (bf16[2,64,384]{2,1,0:T(8,128)(2,1)S(1)}, bf16[2,64,384]{2,1,0:T(8,128)(2,1)S(1)}, u32[]{:S(2)}, u32[]{:S(2)}) collective-permute-start(bf16[2,64,384]{2,1,0:T(8,128)(2,1)S(1)} %pick1.3), channel_id=1, source_target_pairs={{0,24},{8,16},{16,8},{24,0},{1,25},{9,17},{17,9},{25,1},{2,26},{10... | collective-permute-start | bytes 294920 | tf_op jit(solution)/shard_map/ppermute | solution.py:28
  31.6 8.1 %collective-permute-start.18 = (bf16[2,64,384]{2,1,0:T(8,128)(2,1)S(1)}, bf16[2,64,384]{2,1,0:T(8,128)(2,1)S(1)}, u32[]{:S(2)}, u32[]{:S(2)}) collective-permute-start(bf16[2,64,384]{2,1,0:T(8,128)(2,1)S(1)} %get-tuple-element.68), channel_id=1, source_target_pairs={{0,8},{8,0},{16,24},{24,16},{1,9},{9,1},{17,25},{25,17},{2,10},{10... | collective-permute-start | bytes 294920 | tf_op jit(solution)/shard_map/ppermute | solution.py:28
  32.2 9.0 %collective-permute-start.19 = (bf16[2,64,384]{2,1,0:T(8,128)(2,1)S(1)}, bf16[2,64,384]{2,1,0:T(8,128)(2,1)S(1)}, u32[]{:S(2)}, u32[]{:S(2)}) collective-permute-start(bf16[2,64,384]{2,1,0:T(8,128)(2,1)S(1)} %get-tuple-element.69), channel_id=1, source_target_pairs={{0,16},{8,24},{16,0},{24,8},{1,17},{9,25},{17,1},{25,9},{2,18},{10... | collective-permute-start | bytes 294920 | tf_op jit(solution)/shard_map/ppermute | solution.py:28
  33.8 7.5 %collective-permute-start.20 = (bf16[2,64,384]{2,1,0:T(8,128)(2,1)S(1)}, bf16[2,64,384]{2,1,0:T(8,128)(2,1)S(1)}, u32[]{:S(2)}, u32[]{:S(2)}) collective-permute-start(bf16[2,64,384]{2,1,0:T(8,128)(2,1)S(1)} %get-tuple-element.70), channel_id=1, source_target_pairs={{0,24},{8,16},{16,8},{24,0},{1,25},{9,17},{17,9},{25,1},{2,26},{10... | collective-permute-start | bytes 294920 | tf_op jit(solution)/shard_map/ppermute | solution.py:28
  37.6 5.8 %collective-permute-start.12 = (bf16[2,64,384]{2,1,0:T(8,128)(2,1)S(1)}, bf16[2,64,384]{2,1,0:T(8,128)(2,1)S(1)}, u32[]{:S(2)}, u32[]{:S(2)}) collective-permute-start(bf16[2,64,384]{2,1,0:T(8,128)(2,1)S(1)} %get-tuple-element.61), channel_id=1, source_target_pairs={{0,8},{8,0},{16,24},{24,16},{1,9},{9,1},{17,25},{25,17},{2,10},{10... | collective-permute-start | bytes 294920 | tf_op jit(solution)/shard_map/ppermute | solution.py:28
  39.7 5.9 %collective-permute-start.13 = (bf16[2,64,384]{2,1,0:T(8,128)(2,1)S(1)}, bf16[2,64,384]{2,1,0:T(8,128)(2,1)S(1)}, u32[]{:S(2)}, u32[]{:S(2)}) collective-permute-start(bf16[2,64,384]{2,1,0:T(8,128)(2,1)S(1)} %get-tuple-element.62), channel_id=1, source_target_pairs={{0,16},{8,24},{16,0},{24,8},{1,17},{9,25},{17,1},{25,9},{2,18},{10... | collective-permute-start | bytes 294920 | tf_op jit(solution)/shard_map/ppermute | solution.py:28
  39.7 5.9 %collective-permute-start.14 = (bf16[2,64,384]{2,1,0:T(8,128)(2,1)S(1)}, bf16[2,64,384]{2,1,0:T(8,128)(2,1)S(1)}, u32[]{:S(2)}, u32[]{:S(2)}) collective-permute-start(bf16[2,64,384]{2,1,0:T(8,128)(2,1)S(1)} %get-tuple-element.63), channel_id=1, source_target_pairs={{0,24},{8,16},{16,8},{24,0},{1,25},{9,17},{17,9},{25,1},{2,26},{10... | collective-permute-start | bytes 294920 | tf_op jit(solution)/shard_map/ppermute | solution.py:28
  41.6 7.6 %collective-permute-start.21 = (bf16[2,64,384]{2,1,0:T(8,128)(2,1)S(1)}, bf16[2,64,384]{2,1,0:T(8,128)(2,1)S(1)}, u32[]{:S(2)}, u32[]{:S(2)}) collective-permute-start(bf16[2,64,384]{2,1,0:T(8,128)(2,1)S(1)} %get-tuple-element.72), channel_id=1, source_target_pairs={{0,1},{1,2},{2,3},{3,0},{4,5},{5,6},{6,7},{7,4},{8,9},{9,10},{10,1... | collective-permute-start | bytes 294920 | tf_op jit(solution)/shard_map/ppermute | solution.py:32
  42.5 11.6 %collective-permute-start.22 = (bf16[2,64,384]{2,1,0:T(8,128)(2,1)S(1)}, bf16[2,64,384]{2,1,0:T(8,128)(2,1)S(1)}, u32[]{:S(2)}, u32[]{:S(2)}) collective-permute-start(bf16[2,64,384]{2,1,0:T(8,128)(2,1)S(1)} %get-tuple-element.73), channel_id=1, source_target_pairs={{0,2},{1,3},{2,0},{3,1},{4,6},{5,7},{6,4},{7,5},{8,10},{9,11},{10,... | collective-permute-start | bytes 294920 | tf_op jit(solution)/shard_map/ppermute | solution.py:32
  43.4 10.8 %collective-permute-start.23 = (bf16[2,64,384]{2,1,0:T(8,128)(2,1)S(1)}, bf16[2,64,384]{2,1,0:T(8,128)(2,1)S(1)}, u32[]{:S(2)}, u32[]{:S(2)}) collective-permute-start(bf16[2,64,384]{2,1,0:T(8,128)(2,1)S(1)} %get-tuple-element.74), channel_id=1, source_target_pairs={{0,3},{1,0},{2,1},{3,2},{4,7},{5,4},{6,5},{7,6},{8,11},{9,8},{10,9... | collective-permute-start | bytes 294920 | tf_op jit(solution)/shard_map/ppermute | solution.py:32
  45.9 9.0 %collective-permute-start.15 = (bf16[2,64,384]{2,1,0:T(8,128)(2,1)S(1)}, bf16[2,64,384]{2,1,0:T(8,128)(2,1)S(1)}, u32[]{:S(2)}, u32[]{:S(2)}) collective-permute-start(bf16[2,64,384]{2,1,0:T(8,128)(2,1)S(1)} %get-tuple-element.65), channel_id=1, source_target_pairs={{0,1},{1,2},{2,3},{3,0},{4,5},{5,6},{6,7},{7,4},{8,9},{9,10},{10,1... | collective-permute-start | bytes 294920 | tf_op jit(solution)/shard_map/ppermute | solution.py:32
  46.4 10.4 %collective-permute-start.16 = (bf16[2,64,384]{2,1,0:T(8,128)(2,1)S(1)}, bf16[2,64,384]{2,1,0:T(8,128)(2,1)S(1)}, u32[]{:S(2)}, u32[]{:S(2)}) collective-permute-start(bf16[2,64,384]{2,1,0:T(8,128)(2,1)S(1)} %get-tuple-element.66), channel_id=1, source_target_pairs={{0,2},{1,3},{2,0},{3,1},{4,6},{5,7},{6,4},{7,5},{8,10},{9,11},{10,... | collective-permute-start | bytes 294920 | tf_op jit(solution)/shard_map/ppermute | solution.py:32
  49.2 7.6 %collective-permute-start.17 = (bf16[2,64,384]{2,1,0:T(8,128)(2,1)S(1)}, bf16[2,64,384]{2,1,0:T(8,128)(2,1)S(1)}, u32[]{:S(2)}, u32[]{:S(2)}) collective-permute-start(bf16[2,64,384]{2,1,0:T(8,128)(2,1)S(1)} %get-tuple-element.67), channel_id=1, source_target_pairs={{0,3},{1,0},{2,1},{3,2},{4,7},{5,4},{6,5},{7,6},{8,11},{9,8},{10,9... | collective-permute-start | bytes 294920 | tf_op jit(solution)/shard_map/ppermute | solution.py:32
